TPU v7x, 32 devices: a whole 2x2x4 slice. The times are simulated.
32 devices in a mesh: groups: 1, ctx: 32 (over z, y, x, core).
Axes of the slice: x: 2, y: 2, z: 4, core: 2. Of those that a mesh axis runs over, the one named last changes fastest.
Arguments:
- queries: bfloat16 [8192, 2048], P(('groups', 'ctx')), may hold values from -6 to 6
- keys: bfloat16 [8192, 1024], P(('groups', 'ctx')), may hold values from -6 to 6
- values: bfloat16 [8192, 1024], P(('groups', 'ctx')), may hold values from -6 to 6
- out_grad: bfloat16 [8192, 2048], P(('groups', 'ctx')), may hold values from -96 to 96
- q_gain: float32 [128], replicated, may hold values from 0.25 to 1.75
- k_gain: float32 [128], replicated, may hold values from 0.25 to 1.75
- doc_ids: int32 [128], P(('groups', 'ctx')), may hold values from 0 to 7, never falling along the last dimension, each value on 1 to 48 neighbouring positions
Outputs:
- query_grad: bfloat16 [8192, 2048], P(('groups', 'ctx'))
- key_grad: bfloat16 [8192, 1024], P(('groups', 'ctx'))
- value_grad: bfloat16 [8192, 1024], P(('groups', 'ctx'))
Inputs may be any that keep to these rules, and one draw needn't show every extreme that they name: `doc_ids`: document ids never fall along the sequence; each document covers 1 to 48 whole blocks, and one covers exactly 48.
All inputs are finite; a program needn't handle non-finite values.
Results may differ from a plain program's by a relative error of at most 0.0075.
Values may be sent and summed in bfloat16 or wider, within the bound.
No kernel may reach another device: no remote copies, remote signals or barrier semaphores. Data moves between devices by JAX's collectives and lax.ppermute only.
A program may use at most 128 MiB of HBM per device.

v0:
```python
import functools

import jax
import jax.numpy as jnp
from jax import lax
from jax.experimental import pallas as pl
from jax.experimental.pallas import tpu as pltpu
from jax.sharding import PartitionSpec as P

HD = 128
WINDOW = 1024
BLK = 64
ID_ROWS = 16
VMEM_LIMIT = 12 * 1024 * 1024
HIDDEN = -1e30
SMALL = pl.CostEstimate(flops=2**20, bytes_accessed=2**16, transcendentals=0)

qk_scale = 168.0 ** (-0.5)
norm_epsilon = 1e-06


def inverse_rms(values_in, axis):
    return lax.rsqrt(jnp.mean(values_in * values_in, axis=axis, keepdims=True) + norm_epsilon)


def weights(scores, first, diagonal, token, e_ref, base):
    total = jnp.zeros((8, scores.shape[1]), jnp.float32)
    key = lax.broadcasted_iota(jnp.int32, (BLK, scores.shape[1]), 0)
    for at in range(0, scores.shape[0], BLK):
        block = scores[at : at + BLK] + jnp.where(first <= at, 0.0, HIDDEN)
        if diagonal == "window" and at < HD:
            block = jnp.where(key + at > token, block, HIDDEN)
        if diagonal == "causal" and at >= scores.shape[0] - HD:
            block = jnp.where(key + (at - scores.shape[0] + HD) <= token, block, HIDDEN)
        e = jnp.exp(block)
        total = total + jnp.sum(e.reshape(BLK // 8, 8, scores.shape[1]), axis=0)
        e_ref[base + at : base + at + BLK, :] = e.astype(e_ref.dtype)
    return jnp.sum(total, axis=0, keepdims=True)


def local_kernel(
    rows, meta, qg_m, qg_t, kv_m, kv_t, q_gain, k_gain,
    qt, qn, gt, k_own, kt_own, v_own, e_own, total_own, out_own, doc_own,
):
    f32, b16 = jnp.float32, jnp.bfloat16
    core = meta[0]
    wide = qt.shape[-1]
    blocks = rows // BLK
    runs = rows // HD
    gain = jnp.broadcast_to(q_gain[...], (HD, HD)).T * qk_scale
    gain = jnp.concatenate([gain] * (wide // HD), axis=1)
    for part, (qg, kv) in enumerate(((qg_m, kv_m), (qg_t, kv_t))):
        slot = core if part == 0 else 1 - core
        for head in range(wide // HD):
            columns = slice(head * HD, (head + 1) * HD)
            q, g = qg[0, :, columns].T, qg[1, :, columns].T
            for run in range(runs):
                tokens = slice(run * HD, (run + 1) * HD)
                qt[slot * runs + run, :, columns] = q[:, tokens]
                gt[slot * runs + run, :, columns] = g[:, tokens]
        off = pl.multiple_of(slot * rows, rows)
        k = kv[:rows].astype(f32)
        kn = (k * inverse_rms(k, -1) * k_gain[...]).astype(b16)
        k_own[pl.ds(off, rows), :] = kn
        kt_own[:, pl.ds(off, rows)] = kn.T
        v_own[pl.ds(off, rows), :] = kv[rows : 2 * rows]
    token = lax.rem(lax.broadcasted_iota(jnp.int32, (1, wide), 1), HD)
    ids = [[kv[2 * rows :, :1].astype(f32)[b : b + 1] for b in range(blocks)] for kv in (kv_m, kv_t)]
    base = 0
    for run in range(2 * runs):
        slot, inside = divmod(run * HD, rows)
        doc = jnp.zeros((1, wide), f32)
        for b in range(HD // BLK):
            at = inside // BLK + b
            here = jnp.where(core == slot, ids[0][at], ids[1][at])
            doc = jnp.where(token >= b * BLK, here, doc)
        doc_own[run] = doc
        earlier = jnp.zeros((1, wide), f32)
        for one in ids[0] + ids[1]:
            earlier = earlier + (one < doc).astype(f32)
        first = earlier.astype(jnp.int32) * BLK
        q = qt[run].astype(f32)
        qn_run = (q * inverse_rms(q, 0) * gain).astype(b16)
        qn[run] = qn_run
        count = (run + 1) * HD
        s = jnp.dot(k_own[:count, :], qn_run, preferred_element_type=f32)
        total_own[run] = weights(s, first, "causal", token, e_own, base)
        vt = v_own[:count, :].T
        out_own[run] = jnp.dot(vt, e_own[base : base + count, :], preferred_element_type=f32)
        base += count


def local(begin, heads, meta, qg_m, qg_t, kv_m, kv_t, q_gain, k_gain):
    f32, b16 = jnp.float32, jnp.bfloat16
    rows = qg_m.shape[1]
    group_cols = qg_m.shape[2] // (kv_m.shape[1] // HD)
    runs = 2 * rows // HD
    pairs = HD * runs * (runs + 1) // 2
    qg = pl.BlockSpec((2, rows, group_cols), lambda h, meta: (0, 0, begin + h))
    kv = pl.BlockSpec((kv_m.shape[0], HD), lambda h, meta: (0, begin + h))
    row = pl.BlockSpec((1, HD), lambda h, meta: (0, 0))
    out = lambda dtype, *shape: (
        pl.BlockSpec((None,) + shape, lambda h, meta: (h,) + (0,) * len(shape)),
        jax.ShapeDtypeStruct((heads,) + shape, dtype),
    )
    outs = [
        out(b16, runs, HD, group_cols), out(b16, runs, HD, group_cols),
        out(b16, runs, HD, group_cols), out(b16, 2 * rows, HD), out(b16, HD, 2 * rows),
        out(b16, 2 * rows, HD), out(b16, pairs, group_cols), out(f32, runs, 1, group_cols),
        out(f32, runs, HD, group_cols), out(f32, runs, 1, group_cols),
    ]
    return pl.pallas_call(
        functools.partial(local_kernel, rows),
        grid_spec=pltpu.PrefetchScalarGridSpec(
            num_scalar_prefetch=1,
            grid=(heads,),
            in_specs=[qg, qg, kv, kv, row, row],
            out_specs=[one[0] for one in outs],
        ),
        out_shape=[one[1] for one in outs],
        compiler_params=pltpu.CompilerParams(vmem_limit_bytes=VMEM_LIMIT),
        cost_estimate=SMALL,
        name=f"local_{begin}",
    )(meta, qg_m, qg_t, kv_m, kv_t, q_gain, k_gain)


def halo_kernel(
    piece, at, rows, meta, qn, gt, total_own, out_own, doc_own, kv1, kv2, k_gain,
    h1, h2, g_out, delta_out, dq_out,
    k_s, kt_s, v_s, vt_s, dk_s, dv_s, e_s,
):
    f32, b16 = jnp.float32, jnp.bfloat16
    core = meta[0]
    wide = qn.shape[-1]
    blocks = rows // BLK
    sources = ((kv2.at[at], 0), (kv1, 2 * rows))

    for source, base in sources:
        for part in range(2):
            off = pl.multiple_of(base + (core if part == 0 else 1 - core) * rows, rows)
            k = source[part, :rows].astype(f32)
            kn = (k * inverse_rms(k, -1) * k_gain[...]).astype(b16)
            k_s[pl.ds(off, rows), :] = kn
            kt_s[:, pl.ds(off, rows)] = kn.T
            v = source[part, rows : 2 * rows]
            v_s[pl.ds(off, rows), :] = v
            vt_s[:, pl.ds(off, rows)] = v.T

    token = lax.rem(lax.broadcasted_iota(jnp.int32, (1, wide), 1), HD)
    nt = (((1,), (1,)), ((), ()))
    ids = [
        source[part, 2 * rows :, :1].astype(f32)[b : b + 1]
        for source, base in sources
        for part in range(2)
        for b in range(blocks)
    ]
    for run in range(2 * rows // HD):
        low = run * HD
        doc = doc_own[piece, run]
        earlier = jnp.zeros((1, wide), f32)
        for one in ids:
            earlier = earlier + (one < doc).astype(f32)
        first = earlier.astype(jnp.int32) * BLK - low
        qn_run = qn[piece, run]
        s = jnp.dot(k_s[low:, :], qn_run, preferred_element_type=f32)
        total = total_own[piece, run] + weights(s, first, "window", token, e_s, low)
        e = e_s[low:, :]
        out = out_own[piece, run] + jnp.dot(vt_s[:, low:], e, preferred_element_type=f32)
        inverse = 1.0 / total
        g_l = (gt[piece, run].astype(f32) * inverse).astype(b16)
        delta = jnp.sum(g_l.astype(f32) * (out * inverse), axis=0, keepdims=True)
        g_out[run] = g_l
        delta_out[run] = delta
        dp = jnp.dot(v_s[low:, :], g_l, preferred_element_type=f32)
        ds = (e.astype(f32) * (dp - delta)).astype(b16)
        dv = lax.dot_general(e, g_l, nt, preferred_element_type=f32)
        dk = lax.dot_general(ds, qn_run, nt, preferred_element_type=f32)
        dv_s[low:, :] = dv if run == 0 else dv_s[low:, :] + dv
        dk_s[low:, :] = dk if run == 0 else dk_s[low:, :] + dk
        dq_out[run] = jnp.dot(kt_s[:, low:], ds, preferred_element_type=f32)

    for target, base in ((h2, 0), (h1, 2 * rows)):
        for part in range(2):
            off = pl.multiple_of(base + (core if part == 0 else 1 - core) * rows, rows)
            target[part, :rows] = dk_s[pl.ds(off, rows), :].astype(b16)
            target[part, rows:] = dv_s[pl.ds(off, rows), :].astype(b16)


def halo(piece, meta, qn, gt, total_own, out_own, doc_own, kv1, kv2, k_gain):
    array, at = kv2
    rows = (array.shape[2] - ID_ROWS) // 2
    runs, wide = qn.shape[1], qn.shape[-1]
    f32, b16 = jnp.float32, jnp.bfloat16
    vmem = pl.BlockSpec(memory_space=pltpu.VMEM)
    return pl.pallas_call(
        functools.partial(halo_kernel, piece, at, rows),
        in_specs=[pl.BlockSpec(memory_space=pltpu.SMEM)] + [vmem] * 8,
        out_specs=[vmem] * 5,
        scratch_shapes=[
            pltpu.VMEM((WINDOW, HD), b16),
            pltpu.VMEM((HD, WINDOW), b16),
            pltpu.VMEM((WINDOW, HD), b16),
            pltpu.VMEM((HD, WINDOW), b16),
            pltpu.VMEM((WINDOW, HD), f32),
            pltpu.VMEM((WINDOW, HD), f32),
            pltpu.VMEM((WINDOW, wide), b16),
        ],
        out_shape=[
            jax.ShapeDtypeStruct((2, 2 * rows, HD), b16),
            jax.ShapeDtypeStruct((2, 2 * rows, HD), b16),
            jax.ShapeDtypeStruct((runs, HD, wide), b16),
            jax.ShapeDtypeStruct((runs, 1, wide), f32),
            jax.ShapeDtypeStruct((runs, HD, wide), f32),
        ],
        compiler_params=pltpu.CompilerParams(vmem_limit_bytes=VMEM_LIMIT),
        cost_estimate=SMALL,
        name=f"halo_{piece}",
    )(meta, qn, gt, total_own, out_own, doc_own, kv1, array, k_gain)


def key_sum(even, own, swapped, returned):
    f32 = jnp.float32
    return own + returned.astype(f32) + jnp.where(even, swapped.astype(f32), 0.0)


def own_kernel(
    pieces, places, rows, meta, q_gain, qt, qn, k_own, kt_own, v_own, e_own, *refs
):
    f32, b16 = jnp.float32, jnp.bfloat16
    core, even = meta[0], meta[1] == 0
    count = len(pieces)
    inputs, refs = refs[: 3 * count], refs[3 * count :]
    ends, refs = refs[: 2 * len(places)], refs[2 * len(places) :]
    (dq_m, dq_t), outs, (dq_s, dk_s, dv_s) = refs[:2], refs[2:-3], refs[-3:]
    runs, wide = qt.shape[1], qt.shape[-1]
    nt = (((1,), (1,)), ((), ()))
    gain = jnp.broadcast_to(q_gain[...], (HD, HD)).T * qk_scale
    gain = jnp.concatenate([gain] * (wide // HD), axis=1)
    for at, piece in enumerate(pieces):
        g_in, delta_in, dq_in = inputs[3 * at : 3 * at + 3]
        base = runs * (runs + 1) // 2 * HD
        for run in reversed(range(runs)):
            keys = (run + 1) * HD
            base -= keys
            g_l, qn_run = g_in[run], qn[piece, run]
            e = e_own[piece, base : base + keys, :]
            dp = jnp.dot(v_own[piece, :keys, :], g_l, preferred_element_type=f32)
            ds = (e.astype(f32) * (dp - delta_in[run])).astype(b16)
            dv = lax.dot_general(e, g_l, nt, preferred_element_type=f32)
            dk = lax.dot_general(ds, qn_run, nt, preferred_element_type=f32)
            dv_s[:keys, :] = dv if run == runs - 1 else dv_s[:keys, :] + dv
            dk_s[:keys, :] = dk if run == runs - 1 else dk_s[:keys, :] + dk
            dq = dq_in[run] + jnp.dot(kt_own[piece, :, :keys], ds, preferred_element_type=f32)
            q = qt[piece, run].astype(f32)
            r = inverse_rms(q, 0)
            scaled = dq * gain
            dq = r * scaled - q * (r * r * r * jnp.mean(q * scaled, axis=0, keepdims=True))
            slot, inside = divmod(run * HD, rows)
            for head in range(wide // HD):
                lanes = slice(head * HD, (head + 1) * HD)
                columns = slice(at * wide + head * HD, at * wide + (head + 1) * HD)
                dq_s[slot, inside : inside + HD, columns] = dq[:, lanes].T.astype(b16)
        for part in range(2):
            tokens = pl.ds(pl.multiple_of((core if part == 0 else 1 - core) * rows, rows), rows)
            if places:
                swapped, returned = ends[2 * at : 2 * at + 2]
                columns = slice(at * HD, (at + 1) * HD)
                for which, sums in enumerate((dk_s, dv_s)):
                    span = slice(which * rows, (which + 1) * rows)
                    total = key_sum(
                        even, sums[tokens, :], swapped[part, span], returned[places[at], part, span]
                    )
                    outs[part][span, columns] = total.astype(b16)
            else:
                outs[at][part, :rows] = dk_s[tokens, :]
                outs[at][part, rows:] = dv_s[tokens, :]
    dq_m[...] = dq_s[core]
    dq_t[...] = dq_s[1 - core]


def own_keys(pieces, meta, q_gain, prepared, results, ends):
    qt, qn, k_own, kt_own, v_own, e_own = prepared
    rows = k_own.shape[1] // 2
    columns = len(pieces) * qt.shape[-1]
    f32, b16 = jnp.float32, jnp.bfloat16
    vmem = pl.BlockSpec(memory_space=pltpu.VMEM)
    dq = jax.ShapeDtypeStruct((rows, columns), b16)
    own = jax.ShapeDtypeStruct((2, 2 * rows, HD), f32)
    final = jax.ShapeDtypeStruct((2 * rows, len(pieces) * HD), b16)
    flat = [one for result in results for one in result]
    flat += [one for swapped, back in ends for one in (swapped, back[0])]
    places = tuple(back[1] for swapped, back in ends)
    outs = [dq, dq] + ([final] * 2 if ends else [own] * len(pieces))
    return pl.pallas_call(
        functools.partial(own_kernel, tuple(range(len(pieces))), places, rows),
        in_specs=[pl.BlockSpec(memory_space=pltpu.SMEM)] + [vmem] * (7 + len(flat)),
        out_specs=[vmem] * len(outs),
        scratch_shapes=[
            pltpu.VMEM((2, rows, columns), b16),
            pltpu.VMEM((2 * rows, HD), f32),
            pltpu.VMEM((2 * rows, HD), f32),
        ],
        out_shape=outs,
        compiler_params=pltpu.CompilerParams(vmem_limit_bytes=VMEM_LIMIT),
        cost_estimate=pl.CostEstimate(flops=2**32, bytes_accessed=2**22, transcendentals=0),
        name=f"own_{pieces[0]}",
    )(meta, q_gain, *prepared, *flat)


def finish_kernel(places, meta, *refs):
    outs = refs[3 * len(places) :]
    for at, at_returned in enumerate(places):
        own, swapped, returned = refs[3 * at : 3 * at + 3]
        for part in range(2):
            total = key_sum(meta[1] == 0, own[part], swapped[part], returned[at_returned, part])
            outs[part][:, at * HD : (at + 1) * HD] = total.astype(outs[part].dtype)


def finish(meta, owns, ends):
    vmem = pl.BlockSpec(memory_space=pltpu.VMEM)
    shape = jax.ShapeDtypeStruct((owns[0].shape[1], len(owns) * HD), jnp.bfloat16)
    flat = []
    for own, (swapped, back) in zip(owns, ends):
        flat += [own, swapped, back[0]]
    places = tuple(back[1] for swapped, back in ends)
    return pl.pallas_call(
        functools.partial(finish_kernel, places),
        in_specs=[pl.BlockSpec(memory_space=pltpu.SMEM)] + [vmem] * len(flat),
        out_specs=[vmem, vmem],
        out_shape=[shape, shape],
        compiler_params=pltpu.CompilerParams(vmem_limit_bytes=VMEM_LIMIT),
        cost_estimate=SMALL,
        name="finish",
    )(meta, *flat)


def join_query_kernel(count, *refs):
    core = lax.rem(lax.axis_index("ctx"), 2)
    out, sem = refs[2 * count], refs[-1]
    copies = []
    for parts, who in ((refs[:count], core), (refs[count : 2 * count], 1 - core)):
        at = 0
        for part in parts:
            width = part.shape[1]
            columns = pl.ds(pl.multiple_of(who * (out.shape[1] // 2) + at, HD), width)
            copies.append(pltpu.make_async_copy(part, out.at[:, columns], sem.at[len(copies)]))
            at += width
    for copy in copies:
        copy.start()
    for copy in copies:
        copy.wait()


def join_query(mine, theirs):
    width = 2 * sum(part.shape[1] for part in mine)
    vmem = pl.BlockSpec(memory_space=pltpu.VMEM)
    return pl.pallas_call(
        functools.partial(join_query_kernel, len(mine)),
        in_specs=[vmem] * (2 * len(mine)),
        out_specs=pl.BlockSpec(memory_space=pltpu.HBM),
        out_shape=jax.ShapeDtypeStruct((mine[0].shape[0], width), mine[0].dtype),
        scratch_shapes=[pltpu.SemaphoreType.DMA((2 * len(mine),))],
        compiler_params=pltpu.CompilerParams(vmem_limit_bytes=VMEM_LIMIT),
        cost_estimate=SMALL,
        name="join_query",
    )(*mine, *theirs)


def join_key_kernel(count, rows, k_gain, keys, *refs):
    f32 = jnp.float32
    core = lax.rem(lax.axis_index("ctx"), 2)
    key_out, value_out = refs[2 * count :]
    half = key_out.shape[1] // 2
    for parts, who in ((refs[:count], core), (refs[count : 2 * count], 1 - core)):
        at = 0
        for part in parts:
            for head in range(part.shape[1] // HD):
                columns = pl.ds(pl.multiple_of(who * half + at, HD), HD)
                inside = slice(head * HD, (head + 1) * HD)
                k = keys[:, columns].astype(f32)
                r = inverse_rms(k, -1)
                scaled = part[:rows, inside].astype(f32) * k_gain[...]
                grad = r * scaled - k * (r * r * r * jnp.mean(k * scaled, axis=-1, keepdims=True))
                key_out[:, columns] = grad.astype(key_out.dtype)
                value_out[:, columns] = part[rows:, inside]
                at += HD


def join_key(k_gain, keys, mine, theirs):
    rows, width = keys.shape
    vmem = pl.BlockSpec(memory_space=pltpu.VMEM)
    out = jax.ShapeDtypeStruct((rows, width), keys.dtype)
    return pl.pallas_call(
        functools.partial(join_key_kernel, len(mine), rows),
        in_specs=[vmem] * (2 + 2 * len(mine)),
        out_specs=[vmem, vmem],
        out_shape=[out, out],
        compiler_params=pltpu.CompilerParams(vmem_limit_bytes=VMEM_LIMIT),
        cost_estimate=SMALL,
        name="join_key",
    )(k_gain, keys, *mine, *theirs)


def lay_kernel(kv_m, kv_t, *outs):
    place = [(out, at) for out in outs for at in range(out.shape[0])]
    for part, kv in enumerate((kv_m, kv_t)):
        for head, (out, at) in enumerate(place):
            out[at, part] = kv[:, head * HD : (head + 1) * HD]


def lay(kv_m, kv_t):
    shape = lambda count: jax.ShapeDtypeStruct((count, 2, kv_m.shape[0], HD), kv_m.dtype)
    vmem = pl.BlockSpec(memory_space=pltpu.VMEM)
    return pl.pallas_call(
        lay_kernel,
        in_specs=[vmem, vmem],
        out_specs=[vmem] * 3,
        out_shape=[shape(1), shape(1), shape(kv_m.shape[1] // HD - 2)],
        compiler_params=pltpu.CompilerParams(vmem_limit_bytes=VMEM_LIMIT),
        cost_estimate=SMALL,
        name="lay",
    )(kv_m, kv_t)


def after(value, *others):
    return lax.optimization_barrier((value,) + others)[0]


def on_device(queries, keys, values, out_grad, q_gain, k_gain, doc_ids):
    f32, b16 = jnp.float32, jnp.bfloat16
    rows = queries.shape[0]
    half = keys.shape[1] // 2
    pieces = half // HD
    count = lax.axis_size("ctx")
    if WINDOW != 4 * rows or count % 4 != 0:
        raise ValueError("unsupported split")
    rank = lax.axis_index("ctx")
    core = lax.rem(rank, 2)
    parity = lax.rem(lax.div(rank, 2), 2)
    odd = parity == 1
    meta = jnp.stack([core, parity]).astype(jnp.int32)

    core_swap = [(i, i ^ 1) for i in range(count)]
    x_swap = [(i, i ^ 2) for i in range(count)]
    ahead = [(i, i + 4) for i in range(count - 4)]
    back = [(i + 4, i) for i in range(count - 4)]

    def half_of(array, who):
        width = array.shape[1] // 2
        return lax.dynamic_slice(array, (0, who * width), (rows, width))

    def both(one, two, who):
        return jnp.stack([half_of(one, who), half_of(two, who)])

    id_rows = jnp.pad((doc_ids + 1).astype(b16), (0, ID_ROWS - doc_ids.shape[0]))
    id_rows = jnp.broadcast_to(id_rows[:, None], (ID_ROWS, half))

    def pack(who):
        return jnp.concatenate([half_of(keys, who), half_of(values, who), id_rows])

    kv_t = lax.ppermute(pack(1 - core), "ctx", core_swap)
    kv_m = pack(core)

    blocks = lay(kv_m, kv_t)
    kv0, kv1, kv2 = [], [], []
    for block in blocks:
        moved = lax.ppermute(block, "ctx", ahead)
        kv0.extend((block, at) for at in range(block.shape[0]))
        kv2.extend((moved, at) for at in range(block.shape[0]))
    qg_m = both(queries, out_grad, core)
    qg_t = lax.ppermute(both(queries, out_grad, 1 - core), "ctx", core_swap)

    q_gain_row = q_gain.reshape(1, HD)
    k_gain_row = k_gain.reshape(1, HD)
    swapped, joined, returned, results, sums_h2 = [], [], [], [], []

    def x_hop(piece, turn):
        operand = jnp.where(turn, kv2[piece][0][kv2[piece][1]], kv0[piece][0][kv0[piece][1]])
        kv1.append(lax.ppermute(operand, "ctx", x_swap))
        return operand

    def send_back(group, turn):
        block = []
        for piece in group:
            arrived = jnp.where(turn, swapped[piece].astype(f32), 0.0)
            block.append((sums_h2[piece].astype(f32) + arrived).astype(b16))
        joined.append(jnp.stack(block))
        moved = lax.ppermute(joined[-1], "ctx", back)
        returned.extend((moved, at) for at in range(len(group)))

    hop_0 = x_hop(0, odd)
    middle = pieces // 2
    local_part = lambda begin, order: local(
        begin, middle, order, qg_m, qg_t, kv_m, kv_t, q_gain_row, k_gain_row
    )
    prepared = [local_part(0, after(meta, hop_0))]
    order = after(meta, x_hop(1, after(odd, prepared[0][7])))
    for piece in range(pieces):
        if piece == middle:
            prepared.append(local_part(middle, order))
        _, qn, gt, *_, total_own, out_own, doc_own = prepared[piece // middle]
        h1, h2, *result = halo(
            piece % middle, order, qn, gt, total_own, out_own, doc_own, kv1[piece], kv2[piece], k_gain_row
        )
        results.append(result)
        order = after(order, result[1])
        if piece + 2 < pieces:
            order = after(order, x_hop(piece + 2, after(odd, result[1])))
        swapped.append(lax.ppermute(h1, "ctx", x_swap))
        sums_h2.append(h2)
        if piece == 2:
            send_back((0, 1), after(odd, result[1]))
            order = after(order, joined[-1])
        elif piece > 2:
            send_back((piece - 1,), after(odd, result[1]))

    ends = lambda group: [(swapped[i], returned[i]) for i in group]
    late, soon = list(range(middle, pieces)), list(range(middle))

    def own_part(group, order, ends):
        qt, qn, _, k_own, kt_own, v_own, e_own, *_ = prepared[group[0] // middle]
        return own_keys(
            group, order, q_gain_row, (qt, qn, k_own, kt_own, v_own, e_own),
            [results[i] for i in group], ends,
        )

    order = after(order, joined[-1])
    dq_m_late, dq_t_late, *own_late = own_part(late, order, [])
    send_back((pieces - 1,), after(odd, dq_m_late))
    order = after(order, joined[-1], returned[0][0], returned[2][0])
    dq_m_soon, dq_t_soon, kv_m_soon, kv_t_soon = own_part(soon, order, ends(soon))
    swap = lambda array: lax.ppermute(array, "ctx", core_swap)
    query_grad = join_query([dq_m_soon, dq_m_late], [swap(dq_t_soon), swap(dq_t_late)])
    kv_m_late, kv_t_late = finish(order, own_late, ends(late))
    key_grad, value_grad = join_key(
        k_gain_row, keys, [kv_m_soon, kv_m_late], [swap(kv_t_soon), swap(kv_t_late)]
    )
    return (query_grad, key_grad, value_grad)


def solution(mesh):
    split = P(("groups", "ctx"), None)
    in_specs = (split, split, split, split, P(), P(), P(("groups", "ctx")))
    return jax.shard_map(
        on_device, mesh=mesh, in_specs=in_specs, out_specs=(split, split, split), check_vma=False
    )
```

profile of v0, /device:TPU:5, one launch (start us, length us, event | category | flops | bytes accessed | tf_op | source)
XLA Modules:
  0.0 88.2 jit_solution(15680715412008357968)
XLA Ops:
  7.4 3.1 %collective-permute-start.1 = (bf16[1,2,528,128]{3,2,1,0:T(8,128)(2,1)S(1)}, bf16[1,2,528,128]{3,2,1,0:T(8,128)(2,1)S(1)}, u32[]{:S(2)}, u32[]{:S(2)}) collective-permute-start(bf16[1,2,528,128]{3,2,1,0:T(8,128)(2,1)S(1)} %get-tuple-element.75), channel_id=1, source_target_pairs={{0,4},{1,5},{2,6},{3,7},{4,8},{5,9},{6,10},{7,11},{8,12},{9,13},{1... | collective-permute-start | bytes 811016 | tf_op jit(solution)/shard_map/ppermute | solution.py:467
  10.6 1.3 %pad_maximum_fusion.qg_m = bf16[2,256,1024]{2,1,0:T(8,128)(2,1)S(1)} fusion(bf16[1,256,1024]{2,1,0:T(8,128)(2,1)} %get-tuple-element.150, bf16[1,256,1024]{2,1,0:T(8,128)(2,1)} %get-tuple-element.159), kind=kLoop, calls=%fused_computation | loop fusion | flops 524288 | bytes 2097152 | tf_op jit(solution)/shard_map/stack | solution.py:453
  11.9 3.1 %collective-permute-start.3 = (bf16[1,2,528,128]{3,2,1,0:T(8,128)(2,1)S(1)}, bf16[1,2,528,128]{3,2,1,0:T(8,128)(2,1)S(1)}, u32[]{:S(2)}, u32[]{:S(2)}) collective-permute-start(bf16[1,2,528,128]{3,2,1,0:T(8,128)(2,1)S(1)} %get-tuple-element.79), channel_id=1, source_target_pairs={{0,4},{1,5},{2,6},{3,7},{4,8},{5,9},{6,10},{7,11},{8,12},{9,13},{1... | collective-permute-start | bytes 811016 | tf_op jit(solution)/shard_map/ppermute | solution.py:467
  15.1 3.1 %collective-permute-start.5 = (bf16[2,2,528,128]{3,2,1,0:T(8,128)(2,1)S(1)}, bf16[2,2,528,128]{3,2,1,0:T(8,128)(2,1)S(1)}, u32[]{:S(2)}, u32[]{:S(2)}) collective-permute-start(bf16[2,2,528,128]{3,2,1,0:T(8,128)(2,1)S(1)} %get-tuple-element.88), channel_id=1, source_target_pairs={{0,4},{1,5},{2,6},{3,7},{4,8},{5,9},{6,10},{7,11},{8,12},{9,13},{1... | collective-permute-start | bytes 1622024 | tf_op jit(solution)/shard_map/ppermute | solution.py:467
  19.7 3.4 %local_0.1 = (bf16[2,4,128,256]{3,2,1,0:T(8,128)(2,1)S(1)}, bf16[2,4,128,256]{3,2,1,0:T(8,128)(2,1)S(1)}, bf16[2,4,128,256]{3,2,1,0:T(8,128)(2,1)S(1)}, bf16[2,5...) custom-call(s32[2]{0:T(128)S(1)} %pad_add_fusion.meta, ...), custom_call_target="tpu_custom_call" | custom-call | flops 1048576 | bytes 65536 | tf_op jit(solution)/shard_map/local_0/pallas_call | solution.py:112
  25.5 4.1 %halo_0.2 = (bf16[2,512,128]{2,1,0:T(8,128)(2,1)S(1)}, bf16[2,512,128]{2,1,0:T(8,128)(2,1)S(1)}, bf16[4,128,256]{2,1,0:T(8,128)(2,1)S(1)}, f32[4,1,256]{2,1,0:T(1,128)S(1)}, f32[4,128,256]{2,1,0:T(8,128)S(1)}) custom-call(s32[2]{0:T(128)S(1)} %pad_add_fusion.meta, bf16[2,4,128,256]{3,2,1,0:T(8,128)(2,1)S(1)} %get-tuple-element.81.qn, ...), custom_call_target="tpu_custom_call" | custom-call | flops 1048576 | bytes 65536 | tf_op jit(solution)/shard_map/halo_0/pallas_call | solution.py:195
  29.6 5.2 %collective-permute-done.5.kv2 = bf16[2,2,528,128]{3,2,1,0:T(8,128)(2,1)S(1)} collective-permute-done((bf16[2,2,528,128]{3,2,1,0:T(8,128)(2,1)S(1)}, bf16[2,2,528,128]{3,2,1,0:T(8,128)(2,1)S(1)}, u32[]{:S(2)}, u32[]{:S(2)}) %collective-permute-start.5) | collective-permute-done | bytes 540704 | tf_op jit(solution)/shard_map/ppermute | solution.py:467
  36.4 4.1 %halo_1.2 = (bf16[2,512,128]{2,1,0:T(8,128)(2,1)S(1)}, bf16[2,512,128]{2,1,0:T(8,128)(2,1)S(1)}, bf16[4,128,256]{2,1,0:T(8,128)(2,1)S(1)}, f32[4,1,256]{2,1,0:T(1,128)S(1)}, f32[4,128,256]{2,1,0:T(8,128)S(1)}) custom-call(s32[2]{0:T(128)S(1)} %pad_add_fusion.meta, bf16[2,4,128,256]{3,2,1,0:T(8,128)(2,1)S(1)} %get-tuple-element.81.qn, ...), custom_call_target="tpu_custom_call" | custom-call | flops 1048576 | bytes 65536 | tf_op jit(solution)/shard_map/halo_1/pallas_call | solution.py:195
  40.5 1.3 %collective-permute-start.9 = (bf16[2,512,128]{2,1,0:T(8,128)(2,1)S(1)}, bf16[2,512,128]{2,1,0:T(8,128)(2,1)S(1)}, u32[]{:S(2)}, u32[]{:S(2)}) collective-permute-start(bf16[2,512,128]{2,1,0:T(8,128)(2,1)S(1)} %get-tuple-element.105), channel_id=1, source_target_pairs={{0,2},{1,3},{2,0},{3,1},{4,6},{5,7},{6,4},{7,5},{8,10},{9,11},{10,... | collective-permute-start | bytes 786440 | tf_op jit(solution)/shard_map/ppermute | solution.py:509
  42.1 3.6 %local_2.1 = (bf16[2,4,128,256]{3,2,1,0:T(8,128)(2,1)S(1)}, bf16[2,4,128,256]{3,2,1,0:T(8,128)(2,1)S(1)}, bf16[2,4,128,256]{3,2,1,0:T(8,128)(2,1)S(1)}, bf16[2,5...) custom-call(s32[2]{0:T(128)S(1)} %pad_add_fusion.meta, ...), custom_call_target="tpu_custom_call" | custom-call | flops 1048576 | bytes 65536 | tf_op jit(solution)/shard_map/local_2/pallas_call | solution.py:112
  45.7 4.1 %halo_0.3 = (bf16[2,512,128]{2,1,0:T(8,128)(2,1)S(1)}, bf16[2,512,128]{2,1,0:T(8,128)(2,1)S(1)}, bf16[4,128,256]{2,1,0:T(8,128)(2,1)S(1)}, f32[4,1,256]{2,1,0:T(1,128)S(1)}, f32[4,128,256]{2,1,0:T(8,128)S(1)}) custom-call(s32[2]{0:T(128)S(1)} %pad_add_fusion.meta, bf16[2,4,128,256]{3,2,1,0:T(8,128)(2,1)S(1)} %get-tuple-element.94.qn, ...), custom_call_target="tpu_custom_call" | custom-call | flops 1048576 | bytes 65536 | tf_op jit(solution)/shard_map/halo_0/pallas_call | solution.py:195
  49.8 1.3 %collective-permute-start.11 = (bf16[2,512,128]{2,1,0:T(8,128)(2,1)S(1)}, bf16[2,512,128]{2,1,0:T(8,128)(2,1)S(1)}, u32[]{:S(2)}, u32[]{:S(2)}) collective-permute-start(bf16[2,512,128]{2,1,0:T(8,128)(2,1)S(1)} %get-tuple-element.111), channel_id=1, source_target_pairs={{0,2},{1,3},{2,0},{3,1},{4,6},{5,7},{6,4},{7,5},{8,10},{9,11},{10,... | collective-permute-start | bytes 786440 | tf_op jit(solution)/shard_map/ppermute | solution.py:509
  51.2 2.2 %collective-permute-done.9.refs_8_ = bf16[2,512,128]{2,1,0:T(8,128)(2,1)S(1)} collective-permute-done((bf16[2,512,128]{2,1,0:T(8,128)(2,1)S(1)}, bf16[2,512,128]{2,1,0:T(8,128)(2,1)S(1)}, u32[]{:S(2)}, u32[]{:S(2)}) %collective-permute-start.9) | collective-permute-done | bytes 262176 | tf_op jit(solution)/shard_map/ppermute | solution.py:509
  53.5 1.9 %collective-permute-start.13 = (bf16[2,2,512,128]{3,2,1,0:T(8,128)(2,1)S(1)}, bf16[2,2,512,128]{3,2,1,0:T(8,128)(2,1)S(1)}, u32[]{:S(2)}, u32[]{:S(2)}) collective-permute-start(bf16[2,2,512,128]{3,2,1,0:T(8,128)(2,1)S(1)} %pad_maximum_fusion.2), channel_id=1, source_target_pairs={{4,0},{5,1},{6,2},{7,3},{8,4},{9,5},{10,6},{11,7},{12,8},{13,9},{1... | collective-permute-start | bytes 1572872 | tf_op jit(solution)/shard_map/ppermute | solution.py:488
  55.5 3.7 %collective-permute-done.10.kv1 = bf16[2,528,128]{2,1,0:T(8,128)(2,1)S(1)} collective-permute-done((bf16[2,528,128]{2,1,0:T(8,128)(2,1)S(1)}, bf16[2,528,128]{2,1,0:T(8,128)(2,1)S(1)}, u32[]{:S(2)}, u32[]{:S(2)}) %collective-permute-start.10) | collective-permute-done | bytes 270368 | tf_op jit(solution)/shard_map/ppermute | solution.py:479
  59.2 4.1 %halo_1.3 = (bf16[2,512,128]{2,1,0:T(8,128)(2,1)S(1)}, bf16[2,512,128]{2,1,0:T(8,128)(2,1)S(1)}, bf16[4,128,256]{2,1,0:T(8,128)(2,1)S(1)}, f32[4,1,256]{2,1,0:T(1,128)S(1)}, f32[4,128,256]{2,1,0:T(8,128)S(1)}) custom-call(s32[2]{0:T(128)S(1)} %pad_add_fusion.meta, bf16[2,4,128,256]{3,2,1,0:T(8,128)(2,1)S(1)} %get-tuple-element.94.qn, ...), custom_call_target="tpu_custom_call" | custom-call | flops 1048576 | bytes 65536 | tf_op jit(solution)/shard_map/halo_1/pallas_call | solution.py:195
  64.9 1.9 %collective-permute-start.14 = (bf16[1,2,512,128]{3,2,1,0:T(8,128)(2,1)S(1)}, bf16[1,2,512,128]{3,2,1,0:T(8,128)(2,1)S(1)}, u32[]{:S(2)}, u32[]{:S(2)}) collective-permute-start(bf16[1,2,512,128]{3,2,1,0:T(8,128)(2,1)S(1)} %fusion.4), channel_id=1, source_target_pairs={{4,0},{5,1},{6,2},{7,3},{8,4},{9,5},{10,6},{11,7},{12,8},{13,9},{1... | collective-permute-start | bytes 786440 | tf_op jit(solution)/shard_map/ppermute | solution.py:488
  66.8 2.7 %own_2.1 = (bf16[256,512]{1,0:T(8,128)(2,1)S(1)}, bf16[256,512]{1,0:T(8,128)(2,1)S(1)}, f32[2,512,128]{2,1,0:T(8,128)S(1)}, f32[2,512,128]{2,1,0:T(8,128)S(1)}) custom-call(s32[2]{0:T(128)S(1)} %pad_add_fusion.meta, f32[1,128]{1,0:T(1,128)S(1)} %bitcast.37, bf16[2,4,128,256]{3,2,1,0:T(8,128)(2,1)S(1)} %get-tuple-element.114.qt, ...), custom_call_target="tpu_custom_call" | custom-call | flops 4294967296 | bytes 4194304 | tf_op jit(solution)/shard_map/own_2/pallas_call | solution.py:294
  69.5 3.0 %collective-permute-start.16 = (bf16[256,512]{1,0:T(8,128)(2,1)S(1)}, bf16[256,512]{1,0:T(8,128)(2,1)S(1)}, u32[]{:S(2)}, u32[]{:S(2)}) collective-permute-start(bf16[256,512]{1,0:T(8,128)(2,1)S(1)} %get-tuple-element.138), channel_id=1, source_target_pairs={{0,1},{1,0},{2,3},{3,2},{4,5},{5,4},{6,7},{7,6},{8,9},{9,8},{10,11... | collective-permute-start | bytes 786440 | tf_op jit(solution)/shard_map/ppermute | solution.py:532
  72.7 2.1 %collective-permute-start.17 = (bf16[1,2,512,128]{3,2,1,0:T(8,128)(2,1)S(1)}, bf16[1,2,512,128]{3,2,1,0:T(8,128)(2,1)S(1)}, u32[]{:S(2)}, u32[]{:S(2)}) collective-permute-start(bf16[1,2,512,128]{3,2,1,0:T(8,128)(2,1)S(1)} %fusion.5), channel_id=1, source_target_pairs={{4,0},{5,1},{6,2},{7,3},{8,4},{9,5},{10,6},{11,7},{12,8},{13,9},{1... | collective-permute-start | bytes 786440 | tf_op jit(solution)/shard_map/ppermute | solution.py:488
  74.9 2.8 %own_0.1 = (bf16[256,512]{1,0:T(8,128)(2,1)S(1)}, bf16[256,512]{1,0:T(8,128)(2,1)S(1)}, bf16[512,256]{1,0:T(8,128)(2,1)S(1)}, bf16[512,256]{1,0:T(8,128)(2,1)S(1)}) custom-call(s32[2]{0:T(128)S(1)} %pad_add_fusion.meta, f32[1,128]{1,0:T(1,128)S(1)} %bitcast.38, bf16[2,4,128,256]{3,2,1,0:T(8,128)(2,1)S(1)} %get-tuple-element.127.qt, ...), custom_call_target="tpu_custom_call" | custom-call | flops 4294967296 | bytes 4194304 | tf_op jit(solution)/shard_map/own_0/pallas_call | solution.py:294
  77.7 2.2 %collective-permute-start.15 = (bf16[256,512]{1,0:T(8,128)(2,1)S(1)}, bf16[256,512]{1,0:T(8,128)(2,1)S(1)}, u32[]{:S(2)}, u32[]{:S(2)}) collective-permute-start(bf16[256,512]{1,0:T(8,128)(2,1)S(1)} %get-tuple-element.137), channel_id=1, source_target_pairs={{0,1},{1,0},{2,3},{3,2},{4,5},{5,4},{6,7},{7,6},{8,9},{9,8},{10,11... | collective-permute-start | bytes 786440 | tf_op jit(solution)/shard_map/ppermute | solution.py:532
  80.0 3.8 %collective-permute-done.17.refs_5_ = bf16[1,2,512,128]{3,2,1,0:T(8,128)(2,1)S(1)} collective-permute-done((bf16[1,2,512,128]{3,2,1,0:T(8,128)(2,1)S(1)}, bf16[1,2,512,128]{3,2,1,0:T(8,128)(2,1)S(1)}, u32[]{:S(2)}, u32[]{:S(2)}) %collective-permute-start.17) | collective-permute-done | bytes 262176 | tf_op jit(solution)/shard_map/ppermute | solution.py:488
  86.5 1.7 %join_key.1 = (bf16[256,1024]{1,0:T(8,128)(2,1)}, bf16[256,1024]{1,0:T(8,128)(2,1)}) custom-call(f32[1,128]{1,0:T(1,128)S(1)} %bitcast.34, bf16[256,1024]{1,0:T(8,128)(2,1)S(1)} %copy-done, bf16[512,256]{1,0:T(8,128)(2,1)S(1)} %get-tuple-element.139.refs_0_, bf16[512,256]{1,0:T(8,128)(2,1)S(1)} %get-tuple-element.142.refs_1_, ...), custom_call_target="tpu_custom_call" | custom-call | flops 1048576 | bytes 65536 | tf_op jit(solution)/shard_map/join_key/pallas_call | solution.py:393
  (55 shorter events, 17.2 us)
Async XLA Ops:
  2.6 1.7 %copy-start.3 = (bf16[256,2048]{1,0:T(8,128)(2,1)S(1)}, bf16[256,2048]{1,0:T(8,128)(2,1)}, u32[]{:S(2)}) copy-start(bf16[256,2048]{1,0:T(8,128)(2,1)} %param.10) | copy-start | bytes 3145732
  3.6 3.6 %collective-permute-start = (bf16[528,512]{1,0:T(8,128)(2,1)}, bf16[528,512]{1,0:T(8,128)(2,1)S(1)}, u32[]{:S(2)}, u32[]{:S(2)}) collective-permute-start(bf16[528,512]{1,0:T(8,128)(2,1)} %get-tuple-element.155), channel_id=1, source_target_pairs={{0,1},{1,0},{2,3},{3,2},{4,5},{5,4},{6,7},{7,6},{8,9},{9,8},{10,11... | collective-permute-start | bytes 1622024 | tf_op jit(solution)/shard_map/ppermute | solution.py:461
  6.6 13.1 %collective-permute-start.2 = (bf16[2,256,1024]{2,1,0:T(8,128)(2,1)}, bf16[2,256,1024]{2,1,0:T(8,128)(2,1)S(1)}, u32[]{:S(2)}, u32[]{:S(2)}) collective-permute-start(bf16[2,256,1024]{2,1,0:T(8,128)(2,1)} %pad_maximum_fusion.1), channel_id=1, source_target_pairs={{0,1},{1,0},{2,3},{3,2},{4,5},{5,4},{6,7},{7,6},{8,9},{9,8},{10,11... | collective-permute-start | bytes 3145736 | tf_op jit(solution)/shard_map/ppermute | solution.py:471
  7.4 10.8 %collective-permute-start.1 = (bf16[1,2,528,128]{3,2,1,0:T(8,128)(2,1)S(1)}, bf16[1,2,528,128]{3,2,1,0:T(8,128)(2,1)S(1)}, u32[]{:S(2)}, u32[]{:S(2)}) collective-permute-start(bf16[1,2,528,128]{3,2,1,0:T(8,128)(2,1)S(1)} %get-tuple-element.75), channel_id=1, source_target_pairs={{0,4},{1,5},{2,6},{3,7},{4,8},{5,9},{6,10},{7,11},{8,12},{9,13},{1... | collective-permute-start | bytes 811016 | tf_op jit(solution)/shard_map/ppermute | solution.py:467
  10.6 9.1 %copy-start.1 = (f32[128]{0:T(128)S(1)}, f32[128]{0:T(128)}, u32[]{:S(2)}) copy-start(f32[128]{0:T(128)} %param.12) | copy-start | bytes 1540
  10.6 9.0 %copy-start.2 = (f32[128]{0:T(128)S(1)}, f32[128]{0:T(128)}, u32[]{:S(2)}) copy-start(f32[128]{0:T(128)} %param.11) | copy-start | bytes 1540
  11.9 11.3 %collective-permute-start.3 = (bf16[1,2,528,128]{3,2,1,0:T(8,128)(2,1)S(1)}, bf16[1,2,528,128]{3,2,1,0:T(8,128)(2,1)S(1)}, u32[]{:S(2)}, u32[]{:S(2)}) collective-permute-start(bf16[1,2,528,128]{3,2,1,0:T(8,128)(2,1)S(1)} %get-tuple-element.79), channel_id=1, source_target_pairs={{0,4},{1,5},{2,6},{3,7},{4,8},{5,9},{6,10},{7,11},{8,12},{9,13},{1... | collective-permute-start | bytes 811016 | tf_op jit(solution)/shard_map/ppermute | solution.py:467
  15.1 19.7 %collective-permute-start.5 = (bf16[2,2,528,128]{3,2,1,0:T(8,128)(2,1)S(1)}, bf16[2,2,528,128]{3,2,1,0:T(8,128)(2,1)S(1)}, u32[]{:S(2)}, u32[]{:S(2)}) collective-permute-start(bf16[2,2,528,128]{3,2,1,0:T(8,128)(2,1)S(1)} %get-tuple-element.88), channel_id=1, source_target_pairs={{0,4},{1,5},{2,6},{3,7},{4,8},{5,9},{6,10},{7,11},{8,12},{9,13},{1... | collective-permute-start | bytes 1622024 | tf_op jit(solution)/shard_map/ppermute | solution.py:467
  18.3 7.2 %collective-permute-start.4 = (bf16[2,528,128]{2,1,0:T(8,128)(2,1)S(1)}, bf16[2,528,128]{2,1,0:T(8,128)(2,1)S(1)}, u32[]{:S(2)}, u32[]{:S(2)}) collective-permute-start(bf16[2,528,128]{2,1,0:T(8,128)(2,1)S(1)} %select_bitcast_fusion.1), channel_id=1, source_target_pairs={{0,2},{1,3},{2,0},{3,1},{4,6},{5,7},{6,4},{7,5},{8,10},{9,11},{10,... | collective-permute-start | bytes 811016 | tf_op jit(solution)/shard_map/ppermute | solution.py:479
  23.3 13.1 %collective-permute-start.6 = (bf16[2,528,128]{2,1,0:T(8,128)(2,1)S(1)}, bf16[2,528,128]{2,1,0:T(8,128)(2,1)S(1)}, u32[]{:S(2)}, u32[]{:S(2)}) collective-permute-start(bf16[2,528,128]{2,1,0:T(8,128)(2,1)S(1)} %select_bitcast_fusion), channel_id=1, source_target_pairs={{0,2},{1,3},{2,0},{3,1},{4,6},{5,7},{6,4},{7,5},{8,10},{9,11},{10,... | collective-permute-start | bytes 811016 | tf_op jit(solution)/shard_map/ppermute | solution.py:479
  34.9 10.8 %collective-permute-start.7 = (bf16[2,528,128]{2,1,0:T(8,128)(2,1)S(1)}, bf16[2,528,128]{2,1,0:T(8,128)(2,1)S(1)}, u32[]{:S(2)}, u32[]{:S(2)}) collective-permute-start(bf16[2,528,128]{2,1,0:T(8,128)(2,1)S(1)} %fusion.1), channel_id=1, source_target_pairs={{0,2},{1,3},{2,0},{3,1},{4,6},{5,7},{6,4},{7,5},{8,10},{9,11},{10,... | collective-permute-start | bytes 811016 | tf_op jit(solution)/shard_map/ppermute | solution.py:479
  36.1 14.9 %collective-permute-start.8 = (bf16[2,512,128]{2,1,0:T(8,128)(2,1)S(1)}, bf16[2,512,128]{2,1,0:T(8,128)(2,1)S(1)}, u32[]{:S(2)}, u32[]{:S(2)}) collective-permute-start(bf16[2,512,128]{2,1,0:T(8,128)(2,1)S(1)} %get-tuple-element.103), channel_id=1, source_target_pairs={{0,2},{1,3},{2,0},{3,1},{4,6},{5,7},{6,4},{7,5},{8,10},{9,11},{10,... | collective-permute-start | bytes 786440 | tf_op jit(solution)/shard_map/ppermute | solution.py:509
  40.5 12.9 %collective-permute-start.9 = (bf16[2,512,128]{2,1,0:T(8,128)(2,1)S(1)}, bf16[2,512,128]{2,1,0:T(8,128)(2,1)S(1)}, u32[]{:S(2)}, u32[]{:S(2)}) collective-permute-start(bf16[2,512,128]{2,1,0:T(8,128)(2,1)S(1)} %get-tuple-element.105), channel_id=1, source_target_pairs={{0,2},{1,3},{2,0},{3,1},{4,6},{5,7},{6,4},{7,5},{8,10},{9,11},{10,... | collective-permute-start | bytes 786440 | tf_op jit(solution)/shard_map/ppermute | solution.py:509
  41.8 17.4 %collective-permute-start.10 = (bf16[2,528,128]{2,1,0:T(8,128)(2,1)S(1)}, bf16[2,528,128]{2,1,0:T(8,128)(2,1)S(1)}, u32[]{:S(2)}, u32[]{:S(2)}) collective-permute-start(bf16[2,528,128]{2,1,0:T(8,128)(2,1)S(1)} %fusion), channel_id=1, source_target_pairs={{0,2},{1,3},{2,0},{3,1},{4,6},{5,7},{6,4},{7,5},{8,10},{9,11},{10,... | collective-permute-start | bytes 811016 | tf_op jit(solution)/shard_map/ppermute | solution.py:479
  49.8 15.0 %collective-permute-start.11 = (bf16[2,512,128]{2,1,0:T(8,128)(2,1)S(1)}, bf16[2,512,128]{2,1,0:T(8,128)(2,1)S(1)}, u32[]{:S(2)}, u32[]{:S(2)}) collective-permute-start(bf16[2,512,128]{2,1,0:T(8,128)(2,1)S(1)} %get-tuple-element.111), channel_id=1, source_target_pairs={{0,2},{1,3},{2,0},{3,1},{4,6},{5,7},{6,4},{7,5},{8,10},{9,11},{10,... | collective-permute-start | bytes 786440 | tf_op jit(solution)/shard_map/ppermute | solution.py:509
  53.5 21.3 %collective-permute-start.13 = (bf16[2,2,512,128]{3,2,1,0:T(8,128)(2,1)S(1)}, bf16[2,2,512,128]{3,2,1,0:T(8,128)(2,1)S(1)}, u32[]{:S(2)}, u32[]{:S(2)}) collective-permute-start(bf16[2,2,512,128]{3,2,1,0:T(8,128)(2,1)S(1)} %pad_maximum_fusion.2), channel_id=1, source_target_pairs={{4,0},{5,1},{6,2},{7,3},{8,4},{9,5},{10,6},{11,7},{12,8},{13,9},{1... | collective-permute-start | bytes 1572872 | tf_op jit(solution)/shard_map/ppermute | solution.py:488
  63.3 9.3 %collective-permute-start.12 = (bf16[2,512,128]{2,1,0:T(8,128)(2,1)S(1)}, bf16[2,512,128]{2,1,0:T(8,128)(2,1)S(1)}, u32[]{:S(2)}, u32[]{:S(2)}) collective-permute-start(bf16[2,512,128]{2,1,0:T(8,128)(2,1)S(1)} %get-tuple-element.125), channel_id=1, source_target_pairs={{0,2},{1,3},{2,0},{3,1},{4,6},{5,7},{6,4},{7,5},{8,10},{9,11},{10,... | collective-permute-start | bytes 786440 | tf_op jit(solution)/shard_map/ppermute | solution.py:509
  64.9 9.9 %collective-permute-start.14 = (bf16[1,2,512,128]{3,2,1,0:T(8,128)(2,1)S(1)}, bf16[1,2,512,128]{3,2,1,0:T(8,128)(2,1)S(1)}, u32[]{:S(2)}, u32[]{:S(2)}) collective-permute-start(bf16[1,2,512,128]{3,2,1,0:T(8,128)(2,1)S(1)} %fusion.4), channel_id=1, source_target_pairs={{4,0},{5,1},{6,2},{7,3},{8,4},{9,5},{10,6},{11,7},{12,8},{13,9},{1... | collective-permute-start | bytes 786440 | tf_op jit(solution)/shard_map/ppermute | solution.py:488
  69.5 15.8 %collective-permute-start.16 = (bf16[256,512]{1,0:T(8,128)(2,1)S(1)}, bf16[256,512]{1,0:T(8,128)(2,1)S(1)}, u32[]{:S(2)}, u32[]{:S(2)}) collective-permute-start(bf16[256,512]{1,0:T(8,128)(2,1)S(1)} %get-tuple-element.138), channel_id=1, source_target_pairs={{0,1},{1,0},{2,3},{3,2},{4,5},{5,4},{6,7},{7,6},{8,9},{9,8},{10,11... | collective-permute-start | bytes 786440 | tf_op jit(solution)/shard_map/ppermute | solution.py:532
  72.7 11.2 %collective-permute-start.17 = (bf16[1,2,512,128]{3,2,1,0:T(8,128)(2,1)S(1)}, bf16[1,2,512,128]{3,2,1,0:T(8,128)(2,1)S(1)}, u32[]{:S(2)}, u32[]{:S(2)}) collective-permute-start(bf16[1,2,512,128]{3,2,1,0:T(8,128)(2,1)S(1)} %fusion.5), channel_id=1, source_target_pairs={{4,0},{5,1},{6,2},{7,3},{8,4},{9,5},{10,6},{11,7},{12,8},{13,9},{1... | collective-permute-start | bytes 786440 | tf_op jit(solution)/shard_map/ppermute | solution.py:488
  77.7 7.6 %collective-permute-start.15 = (bf16[256,512]{1,0:T(8,128)(2,1)S(1)}, bf16[256,512]{1,0:T(8,128)(2,1)S(1)}, u32[]{:S(2)}, u32[]{:S(2)}) collective-permute-start(bf16[256,512]{1,0:T(8,128)(2,1)S(1)} %get-tuple-element.137), channel_id=1, source_target_pairs={{0,1},{1,0},{2,3},{3,2},{4,5},{5,4},{6,7},{7,6},{8,9},{9,8},{10,11... | collective-permute-start | bytes 786440 | tf_op jit(solution)/shard_map/ppermute | solution.py:532
  79.9 6.4 %collective-permute-start.18 = (bf16[512,256]{1,0:T(8,128)(2,1)S(1)}, bf16[512,256]{1,0:T(8,128)(2,1)S(1)}, u32[]{:S(2)}, u32[]{:S(2)}) collective-permute-start(bf16[512,256]{1,0:T(8,128)(2,1)S(1)} %get-tuple-element.143), channel_id=1, source_target_pairs={{0,1},{1,0},{2,3},{3,2},{4,5},{5,4},{6,7},{7,6},{8,9},{9,8},{10,11... | collective-permute-start | bytes 786440 | tf_op jit(solution)/shard_map/ppermute | solution.py:532
  84.6 1.9 %copy-start = (bf16[256,1024]{1,0:T(8,128)(2,1)S(1)}, bf16[256,1024]{1,0:T(8,128)(2,1)}, u32[]{:S(2)}) copy-start(bf16[256,1024]{1,0:T(8,128)(2,1)} %keys.1) | copy-start | bytes 1572868
  84.6 1.9 %collective-permute-start.19 = (bf16[512,256]{1,0:T(8,128)(2,1)S(1)}, bf16[512,256]{1,0:T(8,128)(2,1)S(1)}, u32[]{:S(2)}, u32[]{:S(2)}) collective-permute-start(bf16[512,256]{1,0:T(8,128)(2,1)S(1)} %get-tuple-element.144), channel_id=1, source_target_pairs={{0,1},{1,0},{2,3},{3,2},{4,5},{5,4},{6,7},{7,6},{8,9},{9,8},{10,11... | collective-permute-start | bytes 786440 | tf_op jit(solution)/shard_map/ppermute | solution.py:532
  (1 other events, 1.7 us)
where the time goes:
time: 89.6 us; the launch traced here: 88.2 us
  Pallas kernels  32.4 us (36%)
  starting transfers between devices  31.1 us (35%)
  waiting for transfers between devices  16.5 us (18%)
  other arithmetic  4.69 us (5%)
  local copies, waits for them, and re-layouts  2.48 us (3%)
  between operations  0.93 us (1%)
    pallas_call x4, Pallas kernels, halo(): pl.pallas_call(functools.partial(halo_kernel, piece, at, rows), in_specs=...  16.3 us
    ppermute x3, starting transfers between devices, on_device(): moved = lax.ppermute(block, 'ctx', ahead)  9.44 us
    pallas_call x2, Pallas kernels, local(): pl.pallas_call(functools.partial(local_kernel, rows), grid_spec=pltpu.Pre...  6.94 us
    ppermute x4, starting transfers between devices, on_device(): swap = lambda array: lax.ppermute(array, 'ctx', core_swap)  6.07 us
    ppermute x3, starting transfers between devices, send_back(): moved = lax.ppermute(joined[-1], 'ctx', back)  5.98 us
    pallas_call x2, Pallas kernels, own_keys(): pl.pallas_call(functools.partial(own_kernel, tuple(range(len(pieces))), p...  5.53 us
    ppermute x3, waiting for transfers between devices, on_device(): moved = lax.ppermute(block, 'ctx', ahead)  5.39 us
    ppermute x4, waiting for transfers between devices, x_hop(): kv1.append(lax.ppermute(operand, 'ctx', x_swap))  4.7 us
  transfers between devices with their start and end apart: 20, of which 8 were waited for; matrix products, arithmetic and copies ran while one was open for 5% of the time, Pallas kernels for 35%

commit v1 on v0

--- a/solution.py
+++ b/solution.py
@@ -414,8 +414,8 @@
     return pl.pallas_call(
         lay_kernel,
         in_specs=[vmem, vmem],
-        out_specs=[vmem] * 3,
-        out_shape=[shape(1), shape(1), shape(kv_m.shape[1] // HD - 2)],
+        out_specs=[vmem] * (kv_m.shape[1] // HD),
+        out_shape=[shape(1)] * (kv_m.shape[1] // HD),
         compiler_params=pltpu.CompilerParams(vmem_limit_bytes=VMEM_LIMIT),
         cost_estimate=SMALL,
         name="lay",
@@ -461,12 +461,11 @@
     kv_t = lax.ppermute(pack(1 - core), "ctx", core_swap)
     kv_m = pack(core)
 
-    blocks = lay(kv_m, kv_t)
-    kv0, kv1, kv2 = [], [], []
-    for block in blocks:
-        moved = lax.ppermute(block, "ctx", ahead)
-        kv0.extend((block, at) for at in range(block.shape[0]))
-        kv2.extend((moved, at) for at in range(block.shape[0]))
+    kv0 = lay(kv_m, kv_t)
+    kv1, kv2 = [], []
+    for block in kv0[:-1]:
+        kv2.append((lax.ppermute(block, "ctx", ahead), 0))
+    neighbour = lax.ppermute(kv0[-1], "ctx", x_swap)
     qg_m = both(queries, out_grad, core)
     qg_t = lax.ppermute(both(queries, out_grad, 1 - core), "ctx", core_swap)
 
@@ -475,9 +474,17 @@
     swapped, joined, returned, results, sums_h2 = [], [], [], [], []
 
     def x_hop(piece, turn):
-        operand = jnp.where(turn, kv2[piece][0][kv2[piece][1]], kv0[piece][0][kv0[piece][1]])
+        operand = jnp.where(turn, kv2[piece][0][0], kv0[piece][0])
         kv1.append(lax.ppermute(operand, "ctx", x_swap))
         return operand
+
+    def far_hop(turn):
+        theirs = after(neighbour, turn)
+        block = jnp.concatenate([kv0[-1], theirs])
+        moved = lax.ppermute(block, "ctx", ahead)
+        kv2.append((moved, 0))
+        kv1.append(jnp.where(odd, theirs[0], moved[1]))
+        return block
 
     def send_back(group, turn):
         block = []
@@ -493,7 +500,7 @@
     local_part = lambda begin, order: local(
         begin, middle, order, qg_m, qg_t, kv_m, kv_t, q_gain_row, k_gain_row
     )
-    prepared = [local_part(0, after(meta, hop_0))]
+    prepared = [local_part(0, after(meta, hop_0, neighbour))]
     order = after(meta, x_hop(1, after(odd, prepared[0][7])))
     for piece in range(pieces):
         if piece == middle:
@@ -504,8 +511,8 @@
         )
         results.append(result)
         order = after(order, result[1])
-        if piece + 2 < pieces:
-            order = after(order, x_hop(piece + 2, after(odd, result[1])))
+        if piece + 3 < pieces:
+            order = after(order, x_hop(piece + 2, after(odd, result[1])), far_hop(result[1]))
         swapped.append(lax.ppermute(h1, "ctx", x_swap))
         sums_h2.append(h2)
         if piece == 2:

time: 89.6 us -> 82.8 us (0.924)
  waiting for transfers between devices: 16.5 us -> 2.62 us
  starting transfers between devices: 31.1 us -> 38.3 us
    ppermute x3 -> x5, waiting for transfers between devices: 5.39 us -> 0.01 us  [the longest x3 0.01 us: on_device(): kv2.append((lax.ppermute(block, 'ctx', ahead), 0))]
    ppermute x4, starting transfers between devices: 6.07 us -> 10.9 us  [on_device(): swap = lambda array: lax.ppermute(array, 'ctx', core_swap)]
    ppermute x3 -> x5, starting transfers between devices: 9.44 us -> 13.5 us  [the longest x3 9.43 us: on_device(): kv2.append((lax.ppermute(block, 'ctx', ahead), 0))]
    ppermute x3, waiting for transfers between devices: 3.85 us -> 0.61 us  [send_back(): moved = lax.ppermute(joined[-1], 'ctx', back)]
    ppermute x4 -> x3, waiting for transfers between devices: 4.7 us -> 1.83 us  [x_hop(): kv1.append(lax.ppermute(operand, 'ctx', x_swap))]
    ppermute x4, waiting for transfers between devices: 2.46 us -> 0.01 us  [on_device(): swapped.append(lax.ppermute(h1, 'ctx', x_swap))]
    ppermute x4 -> x3, starting transfers between devices: 4.15 us -> 1.92 us  [x_hop(): kv1.append(lax.ppermute(operand, 'ctx', x_swap))]
  transfers between devices with their start and end apart: 20 -> 21, of which waited for: 8 -> 4; matrix products, arithmetic and copies ran while one was open for 5% -> 5% of each run, Pallas kernels for 35% -> 38%
where the time goes in v1:
time: 82.8 us; the launch traced here: 81.4 us
  starting transfers between devices  38.3 us (46%)
  Pallas kernels  32.2 us (39%)
  other arithmetic  4.71 us (6%)
  waiting for transfers between devices  2.62 us (3%)
  local copies, waits for them, and re-layouts  2.53 us (3%)
  between operations  1 us (1%)
    pallas_call x4, Pallas kernels, halo(): pl.pallas_call(functools.partial(halo_kernel, piece, at, rows), in_specs=...  16.3 us
    ppermute x4, starting transfers between devices, on_device(): swap = lambda array: lax.ppermute(array, 'ctx', core_swap)  10.9 us
    ppermute x3, starting transfers between devices, on_device(): kv2.append((lax.ppermute(block, 'ctx', ahead), 0))  9.43 us
    pallas_call x2, Pallas kernels, local(): pl.pallas_call(functools.partial(local_kernel, rows), grid_spec=pltpu.Pre...  6.76 us
    ppermute x3, starting transfers between devices, send_back(): moved = lax.ppermute(joined[-1], 'ctx', back)  5.98 us
    pallas_call x2, Pallas kernels, own_keys(): pl.pallas_call(functools.partial(own_kernel, tuple(range(len(pieces))), p...  5.53 us
    ppermute x4, starting transfers between devices, on_device(): swapped.append(lax.ppermute(h1, 'ctx', x_swap))  4.58 us
    ppermute x1, starting transfers between devices, far_hop(): moved = lax.ppermute(block, 'ctx', ahead)  2.84 us
  transfers between devices with their start and end apart: 21, of which 4 were waited for; matrix products, arithmetic and copies ran while one was open for 5% of the time, Pallas kernels for 38%

profile of v1, /device:TPU:5, one launch (start us, length us, event | category | flops | bytes accessed | tf_op | source)
XLA Modules:
  0.0 81.4 jit_solution(13287531145230402714)
XLA Ops:
  7.4 3.1 %collective-permute-start.1 = (bf16[1,2,528,128]{3,2,1,0:T(8,128)(2,1)S(1)}, bf16[1,2,528,128]{3,2,1,0:T(8,128)(2,1)S(1)}, u32[]{:S(2)}, u32[]{:S(2)}) collective-permute-start(bf16[1,2,528,128]{3,2,1,0:T(8,128)(2,1)S(1)} %get-tuple-element.75), channel_id=1, source_target_pairs={{0,4},{1,5},{2,6},{3,7},{4,8},{5,9},{6,10},{7,11},{8,12},{9,13},{1... | collective-permute-start | bytes 811016 | tf_op jit(solution)/shard_map/ppermute | solution.py:467
  10.6 1.3 %pad_maximum_fusion.qg_m = bf16[2,256,1024]{2,1,0:T(8,128)(2,1)S(1)} fusion(bf16[1,256,1024]{2,1,0:T(8,128)(2,1)} %get-tuple-element.150, bf16[1,256,1024]{2,1,0:T(8,128)(2,1)} %get-tuple-element.159), kind=kLoop, calls=%fused_computation | loop fusion | flops 524288 | bytes 2097152 | tf_op jit(solution)/shard_map/stack | solution.py:453
  11.9 1.3 %collective-permute-start.2 = (bf16[1,2,528,128]{3,2,1,0:T(8,128)(2,1)S(1)}, bf16[1,2,528,128]{3,2,1,0:T(8,128)(2,1)S(1)}, u32[]{:S(2)}, u32[]{:S(2)}) collective-permute-start(bf16[1,2,528,128]{3,2,1,0:T(8,128)(2,1)S(1)} %get-tuple-element.76), channel_id=1, source_target_pairs={{0,2},{1,3},{2,0},{3,1},{4,6},{5,7},{6,4},{7,5},{8,10},{9,11},{10,... | collective-permute-start | bytes 811016 | tf_op jit(solution)/shard_map/ppermute | solution.py:468
  13.2 3.1 %collective-permute-start.4 = (bf16[1,2,528,128]{3,2,1,0:T(8,128)(2,1)S(1)}, bf16[1,2,528,128]{3,2,1,0:T(8,128)(2,1)S(1)}, u32[]{:S(2)}, u32[]{:S(2)}) collective-permute-start(bf16[1,2,528,128]{3,2,1,0:T(8,128)(2,1)S(1)} %get-tuple-element.80), channel_id=1, source_target_pairs={{0,4},{1,5},{2,6},{3,7},{4,8},{5,9},{6,10},{7,11},{8,12},{9,13},{1... | collective-permute-start | bytes 811016 | tf_op jit(solution)/shard_map/ppermute | solution.py:467
  16.4 3.1 %collective-permute-start.6 = (bf16[1,2,528,128]{3,2,1,0:T(8,128)(2,1)S(1)}, bf16[1,2,528,128]{3,2,1,0:T(8,128)(2,1)S(1)}, u32[]{:S(2)}, u32[]{:S(2)}) collective-permute-start(bf16[1,2,528,128]{3,2,1,0:T(8,128)(2,1)S(1)} %get-tuple-element.89), channel_id=1, source_target_pairs={{0,4},{1,5},{2,6},{3,7},{4,8},{5,9},{6,10},{7,11},{8,12},{9,13},{1... | collective-permute-start | bytes 811016 | tf_op jit(solution)/shard_map/ppermute | solution.py:467
  20.0 3.4 %local_0.1 = (bf16[2,4,128,256]{3,2,1,0:T(8,128)(2,1)S(1)}, bf16[2,4,128,256]{3,2,1,0:T(8,128)(2,1)S(1)}, bf16[2,4,128,256]{3,2,1,0:T(8,128)(2,1)S(1)}, bf16[2,5...) custom-call(s32[2]{0:T(128)S(1)} %pad_add_fusion.meta, ...), custom_call_target="tpu_custom_call" | custom-call | flops 1048576 | bytes 65536 | tf_op jit(solution)/shard_map/local_0/pallas_call | solution.py:112
  23.4 1.3 %collective-permute-start.7 = (bf16[2,528,128]{2,1,0:T(8,128)(2,1)S(1)}, bf16[2,528,128]{2,1,0:T(8,128)(2,1)S(1)}, u32[]{:S(2)}, u32[]{:S(2)}) collective-permute-start(bf16[2,528,128]{2,1,0:T(8,128)(2,1)S(1)} %select_bitcast_fusion.1), channel_id=1, source_target_pairs={{0,2},{1,3},{2,0},{3,1},{4,6},{5,7},{6,4},{7,5},{8,10},{9,11},{10,... | collective-permute-start | bytes 811016 | tf_op jit(solution)/shard_map/ppermute | solution.py:478
  24.7 1.8 %collective-permute-done.5.kv1 = bf16[2,528,128]{2,1,0:T(8,128)(2,1)S(1)} collective-permute-done((bf16[2,528,128]{2,1,0:T(8,128)(2,1)S(1)}, bf16[2,528,128]{2,1,0:T(8,128)(2,1)S(1)}, u32[]{:S(2)}, u32[]{:S(2)}) %collective-permute-start.5) | collective-permute-done | bytes 270368 | tf_op jit(solution)/shard_map/ppermute | solution.py:478
  26.5 4.1 %halo_0.2 = (bf16[2,512,128]{2,1,0:T(8,128)(2,1)S(1)}, bf16[2,512,128]{2,1,0:T(8,128)(2,1)S(1)}, bf16[4,128,256]{2,1,0:T(8,128)(2,1)S(1)}, f32[4,1,256]{2,1,0:T(1,128)S(1)}, f32[4,128,256]{2,1,0:T(8,128)S(1)}) custom-call(s32[2]{0:T(128)S(1)} %pad_add_fusion.meta, bf16[2,4,128,256]{3,2,1,0:T(8,128)(2,1)S(1)} %get-tuple-element.82.qn, ...), custom_call_target="tpu_custom_call" | custom-call | flops 1048576 | bytes 65536 | tf_op jit(solution)/shard_map/halo_0/pallas_call | solution.py:195
  32.3 4.1 %halo_1.2 = (bf16[2,512,128]{2,1,0:T(8,128)(2,1)S(1)}, bf16[2,512,128]{2,1,0:T(8,128)(2,1)S(1)}, bf16[4,128,256]{2,1,0:T(8,128)(2,1)S(1)}, f32[4,1,256]{2,1,0:T(1,128)S(1)}, f32[4,128,256]{2,1,0:T(8,128)S(1)}) custom-call(s32[2]{0:T(128)S(1)} %pad_add_fusion.meta, bf16[2,4,128,256]{3,2,1,0:T(8,128)(2,1)S(1)} %get-tuple-element.82.qn, ...), custom_call_target="tpu_custom_call" | custom-call | flops 1048576 | bytes 65536 | tf_op jit(solution)/shard_map/halo_1/pallas_call | solution.py:195
  37.4 2.8 %collective-permute-start.11 = (bf16[2,2,528,128]{3,2,1,0:T(8,128)(2,1)S(1)}, bf16[2,2,528,128]{3,2,1,0:T(8,128)(2,1)S(1)}, u32[]{:S(2)}, u32[]{:S(2)}) collective-permute-start(bf16[2,2,528,128]{3,2,1,0:T(8,128)(2,1)S(1)} %constant_dynamic-update-slice_fusion), channel_id=1, source_target_pairs={{0,4},{1,5},{2,6},{3,7},{4,8},{5,9},{6,10},{7,11},{8,12},{9,13},{1... | collective-permute-start | bytes 1622024 | tf_op jit(solution)/shard_map/ppermute | solution.py:484
  40.3 3.4 %local_2.1 = (bf16[2,4,128,256]{3,2,1,0:T(8,128)(2,1)S(1)}, bf16[2,4,128,256]{3,2,1,0:T(8,128)(2,1)S(1)}, bf16[2,4,128,256]{3,2,1,0:T(8,128)(2,1)S(1)}, bf16[2,5...) custom-call(s32[2]{0:T(128)S(1)} %pad_add_fusion.meta, ...), custom_call_target="tpu_custom_call" | custom-call | flops 1048576 | bytes 65536 | tf_op jit(solution)/shard_map/local_2/pallas_call | solution.py:112
  43.7 4.1 %halo_0.3 = (bf16[2,512,128]{2,1,0:T(8,128)(2,1)S(1)}, bf16[2,512,128]{2,1,0:T(8,128)(2,1)S(1)}, bf16[4,128,256]{2,1,0:T(8,128)(2,1)S(1)}, f32[4,1,256]{2,1,0:T(1,128)S(1)}, f32[4,128,256]{2,1,0:T(8,128)S(1)}) custom-call(s32[2]{0:T(128)S(1)} %pad_add_fusion.meta, bf16[2,4,128,256]{3,2,1,0:T(8,128)(2,1)S(1)} %get-tuple-element.94.qn, ...), custom_call_target="tpu_custom_call" | custom-call | flops 1048576 | bytes 65536 | tf_op jit(solution)/shard_map/halo_0/pallas_call | solution.py:195
  47.7 1.3 %collective-permute-start.12 = (bf16[2,512,128]{2,1,0:T(8,128)(2,1)S(1)}, bf16[2,512,128]{2,1,0:T(8,128)(2,1)S(1)}, u32[]{:S(2)}, u32[]{:S(2)}) collective-permute-start(bf16[2,512,128]{2,1,0:T(8,128)(2,1)S(1)} %get-tuple-element.111), channel_id=1, source_target_pairs={{0,2},{1,3},{2,0},{3,1},{4,6},{5,7},{6,4},{7,5},{8,10},{9,11},{10,... | collective-permute-start | bytes 786440 | tf_op jit(solution)/shard_map/ppermute | solution.py:516
  49.3 1.9 %collective-permute-start.14 = (bf16[2,2,512,128]{3,2,1,0:T(8,128)(2,1)S(1)}, bf16[2,2,512,128]{3,2,1,0:T(8,128)(2,1)S(1)}, u32[]{:S(2)}, u32[]{:S(2)}) collective-permute-start(bf16[2,2,512,128]{3,2,1,0:T(8,128)(2,1)S(1)} %pad_maximum_fusion.2), channel_id=1, source_target_pairs={{4,0},{5,1},{6,2},{7,3},{8,4},{9,5},{10,6},{11,7},{12,8},{13,9},{1... | collective-permute-start | bytes 1572872 | tf_op jit(solution)/shard_map/ppermute | solution.py:495
  51.3 4.1 %halo_1.3 = (bf16[2,512,128]{2,1,0:T(8,128)(2,1)S(1)}, bf16[2,512,128]{2,1,0:T(8,128)(2,1)S(1)}, bf16[4,128,256]{2,1,0:T(8,128)(2,1)S(1)}, f32[4,1,256]{2,1,0:T(1,128)S(1)}, f32[4,128,256]{2,1,0:T(8,128)S(1)}) custom-call(s32[2]{0:T(128)S(1)} %pad_add_fusion.meta, bf16[2,4,128,256]{3,2,1,0:T(8,128)(2,1)S(1)} %get-tuple-element.94.qn, ...), custom_call_target="tpu_custom_call" | custom-call | flops 1048576 | bytes 65536 | tf_op jit(solution)/shard_map/halo_1/pallas_call | solution.py:195
  56.5 1.9 %collective-permute-start.15 = (bf16[1,2,512,128]{3,2,1,0:T(8,128)(2,1)S(1)}, bf16[1,2,512,128]{3,2,1,0:T(8,128)(2,1)S(1)}, u32[]{:S(2)}, u32[]{:S(2)}) collective-permute-start(bf16[1,2,512,128]{3,2,1,0:T(8,128)(2,1)S(1)} %fusion.3), channel_id=1, source_target_pairs={{4,0},{5,1},{6,2},{7,3},{8,4},{9,5},{10,6},{11,7},{12,8},{13,9},{1... | collective-permute-start | bytes 786440 | tf_op jit(solution)/shard_map/ppermute | solution.py:495
  58.4 2.7 %own_2.1 = (bf16[256,512]{1,0:T(8,128)(2,1)S(1)}, bf16[256,512]{1,0:T(8,128)(2,1)S(1)}, f32[2,512,128]{2,1,0:T(8,128)S(1)}, f32[2,512,128]{2,1,0:T(8,128)S(1)}) custom-call(s32[2]{0:T(128)S(1)} %pad_add_fusion.meta, f32[1,128]{1,0:T(1,128)S(1)} %bitcast.37, bf16[2,4,128,256]{3,2,1,0:T(8,128)(2,1)S(1)} %get-tuple-element.114.qt, ...), custom_call_target="tpu_custom_call" | custom-call | flops 4294967296 | bytes 4194304 | tf_op jit(solution)/shard_map/own_2/pallas_call | solution.py:294
  61.1 4.5 %collective-permute-start.17 = (bf16[256,512]{1,0:T(8,128)(2,1)S(1)}, bf16[256,512]{1,0:T(8,128)(2,1)S(1)}, u32[]{:S(2)}, u32[]{:S(2)}) collective-permute-start(bf16[256,512]{1,0:T(8,128)(2,1)S(1)} %get-tuple-element.138), channel_id=1, source_target_pairs={{0,1},{1,0},{2,3},{3,2},{4,5},{5,4},{6,7},{7,6},{8,9},{9,8},{10,11... | collective-permute-start | bytes 786440 | tf_op jit(solution)/shard_map/ppermute | solution.py:539
  65.7 2.1 %collective-permute-start.18 = (bf16[1,2,512,128]{3,2,1,0:T(8,128)(2,1)S(1)}, bf16[1,2,512,128]{3,2,1,0:T(8,128)(2,1)S(1)}, u32[]{:S(2)}, u32[]{:S(2)}) collective-permute-start(bf16[1,2,512,128]{3,2,1,0:T(8,128)(2,1)S(1)} %fusion.4), channel_id=1, source_target_pairs={{4,0},{5,1},{6,2},{7,3},{8,4},{9,5},{10,6},{11,7},{12,8},{13,9},{1... | collective-permute-start | bytes 786440 | tf_op jit(solution)/shard_map/ppermute | solution.py:495
  67.9 2.8 %own_0.1 = (bf16[256,512]{1,0:T(8,128)(2,1)S(1)}, bf16[256,512]{1,0:T(8,128)(2,1)S(1)}, bf16[512,256]{1,0:T(8,128)(2,1)S(1)}, bf16[512,256]{1,0:T(8,128)(2,1)S(1)}) custom-call(s32[2]{0:T(128)S(1)} %pad_add_fusion.meta, f32[1,128]{1,0:T(1,128)S(1)} %bitcast.38, bf16[2,4,128,256]{3,2,1,0:T(8,128)(2,1)S(1)} %get-tuple-element.127.qt, ...), custom_call_target="tpu_custom_call" | custom-call | flops 4294967296 | bytes 4194304 | tf_op jit(solution)/shard_map/own_0/pallas_call | solution.py:294
  70.7 4.3 %collective-permute-start.16 = (bf16[256,512]{1,0:T(8,128)(2,1)S(1)}, bf16[256,512]{1,0:T(8,128)(2,1)S(1)}, u32[]{:S(2)}, u32[]{:S(2)}) collective-permute-start(bf16[256,512]{1,0:T(8,128)(2,1)S(1)} %get-tuple-element.137), channel_id=1, source_target_pairs={{0,1},{1,0},{2,3},{3,2},{4,5},{5,4},{6,7},{7,6},{8,9},{9,8},{10,11... | collective-permute-start | bytes 786440 | tf_op jit(solution)/shard_map/ppermute | solution.py:539
  76.5 2.0 %collective-permute-start.20 = (bf16[512,256]{1,0:T(8,128)(2,1)S(1)}, bf16[512,256]{1,0:T(8,128)(2,1)S(1)}, u32[]{:S(2)}, u32[]{:S(2)}) collective-permute-start(bf16[512,256]{1,0:T(8,128)(2,1)S(1)} %get-tuple-element.144), channel_id=1, source_target_pairs={{0,1},{1,0},{2,3},{3,2},{4,5},{5,4},{6,7},{7,6},{8,9},{9,8},{10,11... | collective-permute-start | bytes 786440 | tf_op jit(solution)/shard_map/ppermute | solution.py:539
  79.7 1.7 %join_key.1 = (bf16[256,1024]{1,0:T(8,128)(2,1)}, bf16[256,1024]{1,0:T(8,128)(2,1)}) custom-call(f32[1,128]{1,0:T(1,128)S(1)} %bitcast.34, bf16[256,1024]{1,0:T(8,128)(2,1)S(1)} %copy-done, bf16[512,256]{1,0:T(8,128)(2,1)S(1)} %get-tuple-element.139.refs_0_, bf16[512,256]{1,0:T(8,128)(2,1)S(1)} %get-tuple-element.142.refs_1_, ...), custom_call_target="tpu_custom_call" | custom-call | flops 1048576 | bytes 65536 | tf_op jit(solution)/shard_map/join_key/pallas_call | solution.py:393
  (59 shorter events, 14.1 us)
Async XLA Ops:
  3.7 3.6 %collective-permute-start = (bf16[528,512]{1,0:T(8,128)(2,1)}, bf16[528,512]{1,0:T(8,128)(2,1)S(1)}, u32[]{:S(2)}, u32[]{:S(2)}) collective-permute-start(bf16[528,512]{1,0:T(8,128)(2,1)} %get-tuple-element.155), channel_id=1, source_target_pairs={{0,1},{1,0},{2,3},{3,2},{4,5},{5,4},{6,7},{7,6},{8,9},{9,8},{10,11... | collective-permute-start | bytes 1622024 | tf_op jit(solution)/shard_map/ppermute | solution.py:461
  6.6 13.4 %collective-permute-start.3 = (bf16[2,256,1024]{2,1,0:T(8,128)(2,1)}, bf16[2,256,1024]{2,1,0:T(8,128)(2,1)S(1)}, u32[]{:S(2)}, u32[]{:S(2)}) collective-permute-start(bf16[2,256,1024]{2,1,0:T(8,128)(2,1)} %pad_maximum_fusion.1), channel_id=1, source_target_pairs={{0,1},{1,0},{2,3},{3,2},{4,5},{5,4},{6,7},{7,6},{8,9},{9,8},{10,11... | collective-permute-start | bytes 3145736 | tf_op jit(solution)/shard_map/ppermute | solution.py:470
  7.4 12.1 %collective-permute-start.1 = (bf16[1,2,528,128]{3,2,1,0:T(8,128)(2,1)S(1)}, bf16[1,2,528,128]{3,2,1,0:T(8,128)(2,1)S(1)}, u32[]{:S(2)}, u32[]{:S(2)}) collective-permute-start(bf16[1,2,528,128]{3,2,1,0:T(8,128)(2,1)S(1)} %get-tuple-element.75), channel_id=1, source_target_pairs={{0,4},{1,5},{2,6},{3,7},{4,8},{5,9},{6,10},{7,11},{8,12},{9,13},{1... | collective-permute-start | bytes 811016 | tf_op jit(solution)/shard_map/ppermute | solution.py:467
  10.6 9.4 %copy-start.1 = (f32[128]{0:T(128)S(1)}, f32[128]{0:T(128)}, u32[]{:S(2)}) copy-start(f32[128]{0:T(128)} %param.12) | copy-start | bytes 1540
  10.6 9.4 %copy-start.2 = (f32[128]{0:T(128)S(1)}, f32[128]{0:T(128)}, u32[]{:S(2)}) copy-start(f32[128]{0:T(128)} %param.11) | copy-start | bytes 1540
  11.9 8.0 %collective-permute-start.2 = (bf16[1,2,528,128]{3,2,1,0:T(8,128)(2,1)S(1)}, bf16[1,2,528,128]{3,2,1,0:T(8,128)(2,1)S(1)}, u32[]{:S(2)}, u32[]{:S(2)}) collective-permute-start(bf16[1,2,528,128]{3,2,1,0:T(8,128)(2,1)S(1)} %get-tuple-element.76), channel_id=1, source_target_pairs={{0,2},{1,3},{2,0},{3,1},{4,6},{5,7},{6,4},{7,5},{8,10},{9,11},{10,... | collective-permute-start | bytes 811016 | tf_op jit(solution)/shard_map/ppermute | solution.py:468
  13.2 10.2 %collective-permute-start.4 = (bf16[1,2,528,128]{3,2,1,0:T(8,128)(2,1)S(1)}, bf16[1,2,528,128]{3,2,1,0:T(8,128)(2,1)S(1)}, u32[]{:S(2)}, u32[]{:S(2)}) collective-permute-start(bf16[1,2,528,128]{3,2,1,0:T(8,128)(2,1)S(1)} %get-tuple-element.80), channel_id=1, source_target_pairs={{0,4},{1,5},{2,6},{3,7},{4,8},{5,9},{6,10},{7,11},{8,12},{9,13},{1... | collective-permute-start | bytes 811016 | tf_op jit(solution)/shard_map/ppermute | solution.py:467
  16.4 14.2 %collective-permute-start.6 = (bf16[1,2,528,128]{3,2,1,0:T(8,128)(2,1)S(1)}, bf16[1,2,528,128]{3,2,1,0:T(8,128)(2,1)S(1)}, u32[]{:S(2)}, u32[]{:S(2)}) collective-permute-start(bf16[1,2,528,128]{3,2,1,0:T(8,128)(2,1)S(1)} %get-tuple-element.89), channel_id=1, source_target_pairs={{0,4},{1,5},{2,6},{3,7},{4,8},{5,9},{6,10},{7,11},{8,12},{9,13},{1... | collective-permute-start | bytes 811016 | tf_op jit(solution)/shard_map/ppermute | solution.py:467
  19.6 6.9 %collective-permute-start.5 = (bf16[2,528,128]{2,1,0:T(8,128)(2,1)S(1)}, bf16[2,528,128]{2,1,0:T(8,128)(2,1)S(1)}, u32[]{:S(2)}, u32[]{:S(2)}) collective-permute-start(bf16[2,528,128]{2,1,0:T(8,128)(2,1)S(1)} %select_bitcast_fusion.2), channel_id=1, source_target_pairs={{0,2},{1,3},{2,0},{3,1},{4,6},{5,7},{6,4},{7,5},{8,10},{9,11},{10,... | collective-permute-start | bytes 811016 | tf_op jit(solution)/shard_map/ppermute | solution.py:478
  23.4 8.8 %collective-permute-start.7 = (bf16[2,528,128]{2,1,0:T(8,128)(2,1)S(1)}, bf16[2,528,128]{2,1,0:T(8,128)(2,1)S(1)}, u32[]{:S(2)}, u32[]{:S(2)}) collective-permute-start(bf16[2,528,128]{2,1,0:T(8,128)(2,1)S(1)} %select_bitcast_fusion.1), channel_id=1, source_target_pairs={{0,2},{1,3},{2,0},{3,1},{4,6},{5,7},{6,4},{7,5},{8,10},{9,11},{10,... | collective-permute-start | bytes 811016 | tf_op jit(solution)/shard_map/ppermute | solution.py:478
  30.6 13.0 %collective-permute-start.8 = (bf16[2,528,128]{2,1,0:T(8,128)(2,1)S(1)}, bf16[2,528,128]{2,1,0:T(8,128)(2,1)S(1)}, u32[]{:S(2)}, u32[]{:S(2)}) collective-permute-start(bf16[2,528,128]{2,1,0:T(8,128)(2,1)S(1)} %select_bitcast_fusion), channel_id=1, source_target_pairs={{0,2},{1,3},{2,0},{3,1},{4,6},{5,7},{6,4},{7,5},{8,10},{9,11},{10,... | collective-permute-start | bytes 811016 | tf_op jit(solution)/shard_map/ppermute | solution.py:478
  31.0 18.1 %collective-permute-start.9 = (bf16[2,512,128]{2,1,0:T(8,128)(2,1)S(1)}, bf16[2,512,128]{2,1,0:T(8,128)(2,1)S(1)}, u32[]{:S(2)}, u32[]{:S(2)}) collective-permute-start(bf16[2,512,128]{2,1,0:T(8,128)(2,1)S(1)} %get-tuple-element.103), channel_id=1, source_target_pairs={{0,2},{1,3},{2,0},{3,1},{4,6},{5,7},{6,4},{7,5},{8,10},{9,11},{10,... | collective-permute-start | bytes 786440 | tf_op jit(solution)/shard_map/ppermute | solution.py:516
  36.4 12.8 %collective-permute-start.10 = (bf16[2,512,128]{2,1,0:T(8,128)(2,1)S(1)}, bf16[2,512,128]{2,1,0:T(8,128)(2,1)S(1)}, u32[]{:S(2)}, u32[]{:S(2)}) collective-permute-start(bf16[2,512,128]{2,1,0:T(8,128)(2,1)S(1)} %get-tuple-element.105), channel_id=1, source_target_pairs={{0,2},{1,3},{2,0},{3,1},{4,6},{5,7},{6,4},{7,5},{8,10},{9,11},{10,... | collective-permute-start | bytes 786440 | tf_op jit(solution)/shard_map/ppermute | solution.py:516
  37.4 13.8 %collective-permute-start.11 = (bf16[2,2,528,128]{3,2,1,0:T(8,128)(2,1)S(1)}, bf16[2,2,528,128]{3,2,1,0:T(8,128)(2,1)S(1)}, u32[]{:S(2)}, u32[]{:S(2)}) collective-permute-start(bf16[2,2,528,128]{3,2,1,0:T(8,128)(2,1)S(1)} %constant_dynamic-update-slice_fusion), channel_id=1, source_target_pairs={{0,4},{1,5},{2,6},{3,7},{4,8},{5,9},{6,10},{7,11},{8,12},{9,13},{1... | collective-permute-start | bytes 1622024 | tf_op jit(solution)/shard_map/ppermute | solution.py:484
  47.7 8.6 %collective-permute-start.12 = (bf16[2,512,128]{2,1,0:T(8,128)(2,1)S(1)}, bf16[2,512,128]{2,1,0:T(8,128)(2,1)S(1)}, u32[]{:S(2)}, u32[]{:S(2)}) collective-permute-start(bf16[2,512,128]{2,1,0:T(8,128)(2,1)S(1)} %get-tuple-element.111), channel_id=1, source_target_pairs={{0,2},{1,3},{2,0},{3,1},{4,6},{5,7},{6,4},{7,5},{8,10},{9,11},{10,... | collective-permute-start | bytes 786440 | tf_op jit(solution)/shard_map/ppermute | solution.py:516
  49.3 18.6 %collective-permute-start.14 = (bf16[2,2,512,128]{3,2,1,0:T(8,128)(2,1)S(1)}, bf16[2,2,512,128]{3,2,1,0:T(8,128)(2,1)S(1)}, u32[]{:S(2)}, u32[]{:S(2)}) collective-permute-start(bf16[2,2,512,128]{3,2,1,0:T(8,128)(2,1)S(1)} %pad_maximum_fusion.2), channel_id=1, source_target_pairs={{4,0},{5,1},{6,2},{7,3},{8,4},{9,5},{10,6},{11,7},{12,8},{13,9},{1... | collective-permute-start | bytes 1572872 | tf_op jit(solution)/shard_map/ppermute | solution.py:495
  55.4 10.3 %collective-permute-start.13 = (bf16[2,512,128]{2,1,0:T(8,128)(2,1)S(1)}, bf16[2,512,128]{2,1,0:T(8,128)(2,1)S(1)}, u32[]{:S(2)}, u32[]{:S(2)}) collective-permute-start(bf16[2,512,128]{2,1,0:T(8,128)(2,1)S(1)} %get-tuple-element.125), channel_id=1, source_target_pairs={{0,2},{1,3},{2,0},{3,1},{4,6},{5,7},{6,4},{7,5},{8,10},{9,11},{10,... | collective-permute-start | bytes 786440 | tf_op jit(solution)/shard_map/ppermute | solution.py:516
  56.5 11.4 %collective-permute-start.15 = (bf16[1,2,512,128]{3,2,1,0:T(8,128)(2,1)S(1)}, bf16[1,2,512,128]{3,2,1,0:T(8,128)(2,1)S(1)}, u32[]{:S(2)}, u32[]{:S(2)}) collective-permute-start(bf16[1,2,512,128]{3,2,1,0:T(8,128)(2,1)S(1)} %fusion.3), channel_id=1, source_target_pairs={{4,0},{5,1},{6,2},{7,3},{8,4},{9,5},{10,6},{11,7},{12,8},{13,9},{1... | collective-permute-start | bytes 786440 | tf_op jit(solution)/shard_map/ppermute | solution.py:495
  61.1 17.4 %collective-permute-start.17 = (bf16[256,512]{1,0:T(8,128)(2,1)S(1)}, bf16[256,512]{1,0:T(8,128)(2,1)S(1)}, u32[]{:S(2)}, u32[]{:S(2)}) collective-permute-start(bf16[256,512]{1,0:T(8,128)(2,1)S(1)} %get-tuple-element.138), channel_id=1, source_target_pairs={{0,1},{1,0},{2,3},{3,2},{4,5},{5,4},{6,7},{7,6},{8,9},{9,8},{10,11... | collective-permute-start | bytes 786440 | tf_op jit(solution)/shard_map/ppermute | solution.py:539
  65.7 10.0 %collective-permute-start.18 = (bf16[1,2,512,128]{3,2,1,0:T(8,128)(2,1)S(1)}, bf16[1,2,512,128]{3,2,1,0:T(8,128)(2,1)S(1)}, u32[]{:S(2)}, u32[]{:S(2)}) collective-permute-start(bf16[1,2,512,128]{3,2,1,0:T(8,128)(2,1)S(1)} %fusion.4), channel_id=1, source_target_pairs={{4,0},{5,1},{6,2},{7,3},{8,4},{9,5},{10,6},{11,7},{12,8},{13,9},{1... | collective-permute-start | bytes 786440 | tf_op jit(solution)/shard_map/ppermute | solution.py:495
  70.7 7.8 %collective-permute-start.16 = (bf16[256,512]{1,0:T(8,128)(2,1)S(1)}, bf16[256,512]{1,0:T(8,128)(2,1)S(1)}, u32[]{:S(2)}, u32[]{:S(2)}) collective-permute-start(bf16[256,512]{1,0:T(8,128)(2,1)S(1)} %get-tuple-element.137), channel_id=1, source_target_pairs={{0,1},{1,0},{2,3},{3,2},{4,5},{5,4},{6,7},{7,6},{8,9},{9,8},{10,11... | collective-permute-start | bytes 786440 | tf_op jit(solution)/shard_map/ppermute | solution.py:539
  75.0 4.5 %collective-permute-start.19 = (bf16[512,256]{1,0:T(8,128)(2,1)S(1)}, bf16[512,256]{1,0:T(8,128)(2,1)S(1)}, u32[]{:S(2)}, u32[]{:S(2)}) collective-permute-start(bf16[512,256]{1,0:T(8,128)(2,1)S(1)} %get-tuple-element.143), channel_id=1, source_target_pairs={{0,1},{1,0},{2,3},{3,2},{4,5},{5,4},{6,7},{7,6},{8,9},{9,8},{10,11... | collective-permute-start | bytes 786440 | tf_op jit(solution)/shard_map/ppermute | solution.py:539
  76.5 3.2 %copy-start = (bf16[256,1024]{1,0:T(8,128)(2,1)S(1)}, bf16[256,1024]{1,0:T(8,128)(2,1)}, u32[]{:S(2)}) copy-start(bf16[256,1024]{1,0:T(8,128)(2,1)} %keys.1) | copy-start | bytes 1572868
  76.5 3.2 %collective-permute-start.20 = (bf16[512,256]{1,0:T(8,128)(2,1)S(1)}, bf16[512,256]{1,0:T(8,128)(2,1)S(1)}, u32[]{:S(2)}, u32[]{:S(2)}) collective-permute-start(bf16[512,256]{1,0:T(8,128)(2,1)S(1)} %get-tuple-element.144), channel_id=1, source_target_pairs={{0,1},{1,0},{2,3},{3,2},{4,5},{5,4},{6,7},{7,6},{8,9},{9,8},{10,11... | collective-permute-start | bytes 786440 | tf_op jit(solution)/shard_map/ppermute | solution.py:539
  (2 other events, 3.5 us)

commit v2 on v1

--- a/solution.py
+++ b/solution.py
@@ -39,7 +39,7 @@
 
 
 def local_kernel(
-    rows, meta, qg_m, qg_t, kv_m, kv_t, q_gain, k_gain,
+    rows, meta, q_m, g_m, k_m, v_m, ids_m, q_t, g_t, k_t, v_t, ids_t, q_gain, k_gain,
     qt, qn, gt, k_own, kt_own, v_own, e_own, total_own, out_own, doc_own,
 ):
     f32, b16 = jnp.float32, jnp.bfloat16
@@ -49,23 +49,24 @@
     runs = rows // HD
     gain = jnp.broadcast_to(q_gain[...], (HD, HD)).T * qk_scale
     gain = jnp.concatenate([gain] * (wide // HD), axis=1)
-    for part, (qg, kv) in enumerate(((qg_m, kv_m), (qg_t, kv_t))):
+    sides = ((q_m, g_m, k_m, v_m), (q_t, g_t, k_t, v_t))
+    for part, (q_ref, g_ref, k_ref, v_ref) in enumerate(sides):
         slot = core if part == 0 else 1 - core
         for head in range(wide // HD):
             columns = slice(head * HD, (head + 1) * HD)
-            q, g = qg[0, :, columns].T, qg[1, :, columns].T
+            q, g = q_ref[:, columns].T, g_ref[:, columns].T
             for run in range(runs):
                 tokens = slice(run * HD, (run + 1) * HD)
                 qt[slot * runs + run, :, columns] = q[:, tokens]
                 gt[slot * runs + run, :, columns] = g[:, tokens]
         off = pl.multiple_of(slot * rows, rows)
-        k = kv[:rows].astype(f32)
+        k = k_ref[...].astype(f32)
         kn = (k * inverse_rms(k, -1) * k_gain[...]).astype(b16)
         k_own[pl.ds(off, rows), :] = kn
         kt_own[:, pl.ds(off, rows)] = kn.T
-        v_own[pl.ds(off, rows), :] = kv[rows : 2 * rows]
+        v_own[pl.ds(off, rows), :] = v_ref[...]
     token = lax.rem(lax.broadcasted_iota(jnp.int32, (1, wide), 1), HD)
-    ids = [[kv[2 * rows :, :1].astype(f32)[b : b + 1] for b in range(blocks)] for kv in (kv_m, kv_t)]
+    ids = [[one[:, :1].astype(f32)[b : b + 1] for b in range(blocks)] for one in (ids_m, ids_t)]
     base = 0
     for run in range(2 * runs):
         slot, inside = divmod(run * HD, rows)
@@ -90,14 +91,15 @@
         base += count
 
 
-def local(begin, heads, meta, qg_m, qg_t, kv_m, kv_t, q_gain, k_gain):
-    f32, b16 = jnp.float32, jnp.bfloat16
-    rows = qg_m.shape[1]
-    group_cols = qg_m.shape[2] // (kv_m.shape[1] // HD)
+def local(begin, heads, meta, mine, theirs, q_gain, k_gain):
+    f32, b16 = jnp.float32, jnp.bfloat16
+    rows, q_columns = mine[0].shape
+    group_cols = q_columns // (mine[2].shape[1] // HD)
     runs = 2 * rows // HD
     pairs = HD * runs * (runs + 1) // 2
-    qg = pl.BlockSpec((2, rows, group_cols), lambda h, meta: (0, 0, begin + h))
-    kv = pl.BlockSpec((kv_m.shape[0], HD), lambda h, meta: (0, begin + h))
+    qg = pl.BlockSpec((rows, group_cols), lambda h, meta: (0, begin + h))
+    kv = pl.BlockSpec((rows, HD), lambda h, meta: (0, begin + h))
+    ids = pl.BlockSpec((ID_ROWS, HD), lambda h, meta: (0, 0))
     row = pl.BlockSpec((1, HD), lambda h, meta: (0, 0))
     out = lambda dtype, *shape: (
         pl.BlockSpec((None,) + shape, lambda h, meta: (h,) + (0,) * len(shape)),
@@ -114,14 +116,14 @@
         grid_spec=pltpu.PrefetchScalarGridSpec(
             num_scalar_prefetch=1,
             grid=(heads,),
-            in_specs=[qg, qg, kv, kv, row, row],
+            in_specs=[qg, qg, kv, kv, ids] * 2 + [row, row],
             out_specs=[one[0] for one in outs],
         ),
         out_shape=[one[1] for one in outs],
         compiler_params=pltpu.CompilerParams(vmem_limit_bytes=VMEM_LIMIT),
         cost_estimate=SMALL,
         name=f"local_{begin}",
-    )(meta, qg_m, qg_t, kv_m, kv_t, q_gain, k_gain)
+    )(meta, *mine, *theirs, q_gain, k_gain)
 
 
 def halo_kernel(
@@ -188,7 +190,7 @@
 
 def halo(piece, meta, qn, gt, total_own, out_own, doc_own, kv1, kv2, k_gain):
     array, at = kv2
-    rows = (array.shape[2] - ID_ROWS) // 2
+    rows = (array.shape[-2] - ID_ROWS) // 2
     runs, wide = qn.shape[1], qn.shape[-1]
     f32, b16 = jnp.float32, jnp.bfloat16
     vmem = pl.BlockSpec(memory_space=pltpu.VMEM)
@@ -401,25 +403,31 @@
     )(k_gain, keys, *mine, *theirs)
 
 
-def lay_kernel(kv_m, kv_t, *outs):
-    place = [(out, at) for out in outs for at in range(out.shape[0])]
-    for part, kv in enumerate((kv_m, kv_t)):
+def lay_kernel(k_m, v_m, ids_m, k_t, v_t, ids_t, *outs):
+    rows = k_m.shape[0]
+    for part, (k, v, ids) in enumerate(((k_m, v_m, ids_m), (k_t, v_t, ids_t))):
+        place = [(out, at) for out in outs for at in range(out.shape[0])]
         for head, (out, at) in enumerate(place):
-            out[at, part] = kv[:, head * HD : (head + 1) * HD]
-
-
-def lay(kv_m, kv_t):
-    shape = lambda count: jax.ShapeDtypeStruct((count, 2, kv_m.shape[0], HD), kv_m.dtype)
+            columns = slice(head * HD, (head + 1) * HD)
+            out[at, part, :rows] = k[:, columns]
+            out[at, part, rows : 2 * rows] = v[:, columns]
+            out[at, part, 2 * rows :] = ids[...]
+
+
+def lay(mine, theirs):
+    rows, columns = mine[0].shape
+    shape = lambda count: jax.ShapeDtypeStruct((count, 2, 2 * rows + ID_ROWS, HD), mine[0].dtype)
+    counts = [2] + [1] * (columns // HD - 2)
     vmem = pl.BlockSpec(memory_space=pltpu.VMEM)
     return pl.pallas_call(
         lay_kernel,
-        in_specs=[vmem, vmem],
-        out_specs=[vmem] * (kv_m.shape[1] // HD),
-        out_shape=[shape(1)] * (kv_m.shape[1] // HD),
+        in_specs=[vmem] * 6,
+        out_specs=[vmem] * len(counts),
+        out_shape=[shape(count) for count in counts],
         compiler_params=pltpu.CompilerParams(vmem_limit_bytes=VMEM_LIMIT),
         cost_estimate=SMALL,
         name="lay",
-    )(kv_m, kv_t)
+    )(*mine, *theirs)
 
 
 def after(value, *others):
@@ -449,41 +457,41 @@
         width = array.shape[1] // 2
         return lax.dynamic_slice(array, (0, who * width), (rows, width))
 
-    def both(one, two, who):
-        return jnp.stack([half_of(one, who), half_of(two, who)])
-
     id_rows = jnp.pad((doc_ids + 1).astype(b16), (0, ID_ROWS - doc_ids.shape[0]))
-    id_rows = jnp.broadcast_to(id_rows[:, None], (ID_ROWS, half))
-
-    def pack(who):
-        return jnp.concatenate([half_of(keys, who), half_of(values, who), id_rows])
-
-    kv_t = lax.ppermute(pack(1 - core), "ctx", core_swap)
-    kv_m = pack(core)
-
-    kv0 = lay(kv_m, kv_t)
-    kv1, kv2 = [], []
-    for block in kv0[:-1]:
-        kv2.append((lax.ppermute(block, "ctx", ahead), 0))
-    neighbour = lax.ppermute(kv0[-1], "ctx", x_swap)
-    qg_m = both(queries, out_grad, core)
-    qg_t = lax.ppermute(both(queries, out_grad, 1 - core), "ctx", core_swap)
+    id_rows = jnp.broadcast_to(id_rows[:, None], (ID_ROWS, HD))
+    swap = lambda array: lax.ppermute(array, "ctx", core_swap)
+    arrays = (queries, out_grad, keys, values)
+    q_m, g_m, k_m, v_m = (half_of(array, core) for array in arrays)
+    q_t, g_t, k_t, v_t = (swap(half_of(array, 1 - core)) for array in arrays)
+    ids_t = swap(id_rows)
+
+    far = pieces - 2
+    pair, *single = lay((k_m, v_m, id_rows), (k_t, v_t, ids_t))
+    kv0 = [(pair, 0), (pair, 1)] + [(block, 0) for block in single]
+    kv1, kv2 = {}, {}
+    moved = lax.ppermute(pair, "ctx", ahead)
+    kv2[0], kv2[1] = (moved, 0), (moved, 1)
+    neighbour = lax.ppermute(kv0[far][0], "ctx", x_swap)
+    for piece in range(2, pieces):
+        if piece != far:
+            kv2[piece] = (lax.ppermute(kv0[piece][0], "ctx", ahead), 0)
 
     q_gain_row = q_gain.reshape(1, HD)
     k_gain_row = k_gain.reshape(1, HD)
+
     swapped, joined, returned, results, sums_h2 = [], [], [], [], []
 
     def x_hop(piece, turn):
-        operand = jnp.where(turn, kv2[piece][0][0], kv0[piece][0])
-        kv1.append(lax.ppermute(operand, "ctx", x_swap))
+        operand = jnp.where(turn, kv2[piece][0][kv2[piece][1]], kv0[piece][0][kv0[piece][1]])
+        kv1[piece] = lax.ppermute(operand, "ctx", x_swap)
         return operand
 
     def far_hop(turn):
         theirs = after(neighbour, turn)
-        block = jnp.concatenate([kv0[-1], theirs])
+        block = jnp.concatenate([kv0[far][0], theirs])
         moved = lax.ppermute(block, "ctx", ahead)
-        kv2.append((moved, 0))
-        kv1.append(jnp.where(odd, theirs[0], moved[1]))
+        kv2[far] = (moved, 0)
+        kv1[far] = jnp.where(odd, theirs[0], moved[1])
         return block
 
     def send_back(group, turn):
@@ -495,24 +503,26 @@
         moved = lax.ppermute(joined[-1], "ctx", back)
         returned.extend((moved, at) for at in range(len(group)))
 
-    hop_0 = x_hop(0, odd)
     middle = pieces // 2
     local_part = lambda begin, order: local(
-        begin, middle, order, qg_m, qg_t, kv_m, kv_t, q_gain_row, k_gain_row
+        begin, middle, order, (q_m, g_m, k_m, v_m, id_rows), (q_t, g_t, k_t, v_t, ids_t),
+        q_gain_row, k_gain_row,
     )
-    prepared = [local_part(0, after(meta, hop_0, neighbour))]
-    order = after(meta, x_hop(1, after(odd, prepared[0][7])))
+    prepared = [local_part(0, meta)]
+    far_block = far_hop(prepared[0][7])
+    hop_0 = x_hop(0, after(odd, far_block))
+    hop_1 = x_hop(1, after(odd, hop_0))
+    prepared.append(local_part(middle, after(meta, hop_1)))
+    order = after(meta, prepared[1][7])
     for piece in range(pieces):
-        if piece == middle:
-            prepared.append(local_part(middle, order))
         _, qn, gt, *_, total_own, out_own, doc_own = prepared[piece // middle]
         h1, h2, *result = halo(
             piece % middle, order, qn, gt, total_own, out_own, doc_own, kv1[piece], kv2[piece], k_gain_row
         )
         results.append(result)
         order = after(order, result[1])
-        if piece + 3 < pieces:
-            order = after(order, x_hop(piece + 2, after(odd, result[1])), far_hop(result[1]))
+        if piece == 1:
+            order = after(order, x_hop(pieces - 1, after(odd, result[1])))
         swapped.append(lax.ppermute(h1, "ctx", x_swap))
         sums_h2.append(h2)
         if piece == 2:
@@ -536,7 +546,6 @@
     send_back((pieces - 1,), after(odd, dq_m_late))
     order = after(order, joined[-1], returned[0][0], returned[2][0])
     dq_m_soon, dq_t_soon, kv_m_soon, kv_t_soon = own_part(soon, order, ends(soon))
-    swap = lambda array: lax.ppermute(array, "ctx", core_swap)
     query_grad = join_query([dq_m_soon, dq_m_late], [swap(dq_t_soon), swap(dq_t_late)])
     kv_m_late, kv_t_late = finish(order, own_late, ends(late))
     key_grad, value_grad = join_key(

time: 82.8 us -> 91 us (1.099)
  waiting for transfers between devices: 2.62 us -> 12.4 us
  starting transfers between devices: 38.3 us -> 33.9 us
  local copies, waits for them, and re-layouts: 2.53 us -> 5.99 us
  Pallas kernels: 32.2 us -> 34.5 us
  other arithmetic: 4.71 us -> 2.54 us
    ppermute x9 -> x6, waiting for transfers between devices: 1.85 us -> 6.29 us  [the longest x3 3.3 us: x_hop(): kv1[piece] = lax.ppermute(operand, 'ctx', x_swap)]
    dynamic_slice x1 -> x4, local copies, waits for them, and re-layouts: 1.27 us -> 4.16 us  [half_of(): return lax.dynamic_slice(array, (0, who * width), (rows, width))]
    ppermute x3, waiting for transfers between devices: 0.61 us -> 3.11 us  [send_back(): moved = lax.ppermute(joined[-1], 'ctx', back)]
    another operation x2 -> x0, other arithmetic: 2.37 us -> none  [both(): return jnp.stack([half_of(one, who), half_of(two, who)])]
    ppermute x4, starting transfers between devices: 4.58 us -> 2.42 us  [on_device(): swapped.append(lax.ppermute(h1, 'ctx', x_swap))]
    select_n x4, other arithmetic: 0.15 us -> 2.05 us  [the longest x3 2.02 us: x_hop(): jnp.where(turn, kv2[piece][0][kv2[piece][1]], kv0[piece][0][kv0[piece][1]])]
    ppermute x4, waiting for transfers between devices: 0.01 us -> 1.53 us  [on_device(): swapped.append(lax.ppermute(h1, 'ctx', x_swap))]
    ppermute x9 -> x6, starting transfers between devices: 14 us -> 12.4 us  [the longest x1 4.22 us: on_device(): kv2[piece] = (lax.ppermute(kv0[piece][0], 'ctx', ahead), 0)]
  transfers between devices with their start and end apart: 21 -> 23, of which waited for: 4 -> 7; matrix products, arithmetic and copies ran while one was open for 5% -> 7% of each run, Pallas kernels for 38% -> 36%
where the time goes in v2:
time: 91 us; the launch traced here: 90.3 us
  Pallas kernels  34.5 us (38%)
  starting transfers between devices  33.9 us (37%)
  waiting for transfers between devices  12.4 us (14%)
  local copies, waits for them, and re-layouts  5.99 us (7%)
  other arithmetic  2.54 us (3%)
  between operations  0.95 us (1%)
    pallas_call x4, Pallas kernels, halo(): pl.pallas_call(functools.partial(halo_kernel, piece, at, rows), in_specs=...  16.3 us
    ppermute x9, starting transfers between devices, on_device(): swap = lambda array: lax.ppermute(array, 'ctx', core_swap)  9.95 us
    pallas_call x2, Pallas kernels, local(): pl.pallas_call(functools.partial(local_kernel, rows), grid_spec=pltpu.Pre...  8.25 us
    ppermute x3, starting transfers between devices, send_back(): moved = lax.ppermute(joined[-1], 'ctx', back)  5.98 us
    pallas_call x2, Pallas kernels, own_keys(): pl.pallas_call(functools.partial(own_kernel, tuple(range(len(pieces))), p...  5.53 us
    ppermute x1, starting transfers between devices, on_device(): kv2[piece] = (lax.ppermute(kv0[piece][0], 'ctx', ahead), 0)  4.22 us
    dynamic_slice x4, local copies, waits for them, and re-layouts, half_of(): return lax.dynamic_slice(array, (0, who * width), (rows, width))  4.16 us
    ppermute x3, starting transfers between devices, x_hop(): kv1[piece] = lax.ppermute(operand, 'ctx', x_swap)  3.82 us
  transfers between devices with their start and end apart: 23, of which 7 were waited for; matrix products, arithmetic and copies ran while one was open for 7% of the time, Pallas kernels for 36%

profile of v2, /device:TPU:5, one launch (start us, length us, event | category | flops | bytes accessed | tf_op | source)
XLA Modules:
  0.0 90.3 jit_solution(5325500138047653612)
XLA Ops:
  4.1 2.1 %constant_dynamic-slice_fusion = (bf16[256,1024]{1,0:T(8,128)(2,1)}, bf16[256,1024]{1,0:T(8,128)(2,1)S(1)}) fusion(bf16[256,2048]{1,0:T(8,128)(2,1)} %param.10, s32[]{:T(128)S(6)} %select_n.80, s32[]{:T(128)S(6)} %select_n.79), kind=kLoop, calls=%fused_computation.18 | loop fusion | bytes 2097160 | tf_op jit(solution)/shard_map/dynamic_slice | solution.py:458
  9.8 3.1 %collective-permute-start.6 = (bf16[2,2,528,128]{3,2,1,0:T(8,128)(2,1)}, bf16[2,2,528,128]{3,2,1,0:T(8,128)(2,1)S(1)}, u32[]{:S(2)}, u32[]{:S(2)}) collective-permute-start(bf16[2,2,528,128]{3,2,1,0:T(8,128)(2,1)} %get-tuple-element.79), channel_id=1, source_target_pairs={{0,4},{1,5},{2,6},{3,7},{4,8},{5,9},{6,10},{7,11},{8,12},{9,13},{1... | collective-permute-start | bytes 1622024 | tf_op jit(solution)/shard_map/ppermute | solution.py:472
  14.3 4.1 %local_0.1 = (bf16[2,4,128,256]{3,2,1,0:T(8,128)(2,1)S(1)}, bf16[2,4,128,256]{3,2,1,0:T(8,128)(2,1)S(1)}, bf16[2,4,128,256]{3,2,1,0:T(8,128)(2,1)S(1)}, bf16[2,5...) custom-call(s32[2]{0:T(128)S(1)} %pad_add_fusion.meta, ...), custom_call_target="tpu_custom_call" | custom-call | flops 1048576 | bytes 65536 | tf_op jit(solution)/shard_map/local_0/pallas_call | solution.py:114
  18.5 2.2 %collective-permute-done.3 = bf16[1,2,528,128]{3,2,1,0:T(8,128)(2,1)} collective-permute-done((bf16[1,2,528,128]{3,2,1,0:T(8,128)(2,1)S(1)}, bf16[1,2,528,128]{3,2,1,0:T(8,128)(2,1)}, u32[]{:S(2)}, u32[]{:S(2)}) %collective-permute-start.3) | collective-permute-done | bytes 270368 | tf_op jit(solution)/shard_map/ppermute | solution.py:474
  21.7 3.1 %collective-permute-start.10 = (bf16[2,2,528,128]{3,2,1,0:T(8,128)(2,1)S(1)}, bf16[2,2,528,128]{3,2,1,0:T(8,128)(2,1)S(1)}, u32[]{:S(2)}, u32[]{:S(2)}) collective-permute-start(bf16[2,2,528,128]{3,2,1,0:T(8,128)(2,1)S(1)} %constant_dynamic-update-slice_fusion), channel_id=1, source_target_pairs={{0,4},{1,5},{2,6},{3,7},{4,8},{5,9},{6,10},{7,11},{8,12},{9,13},{1... | collective-permute-start | bytes 1622024 | tf_op jit(solution)/shard_map/ppermute | solution.py:492
  29.2 4.2 %collective-permute-start.9 = (bf16[1,2,528,128]{3,2,1,0:T(8,128)(2,1)S(1)}, bf16[1,2,528,128]{3,2,1,0:T(8,128)(2,1)S(1)}, u32[]{:S(2)}, u32[]{:S(2)}) collective-permute-start(bf16[1,2,528,128]{3,2,1,0:T(8,128)(2,1)S(1)} %copy-done.3), channel_id=1, source_target_pairs={{0,4},{1,5},{2,6},{3,7},{4,8},{5,9},{6,10},{7,11},{8,12},{9,13},{1... | collective-permute-start | bytes 811016 | tf_op jit(solution)/shard_map/ppermute | solution.py:477
  33.4 4.1 %local_2.1 = (bf16[2,4,128,256]{3,2,1,0:T(8,128)(2,1)S(1)}, bf16[2,4,128,256]{3,2,1,0:T(8,128)(2,1)S(1)}, bf16[2,4,128,256]{3,2,1,0:T(8,128)(2,1)S(1)}, bf16[2,5...) custom-call(s32[2]{0:T(128)S(1)} %pad_add_fusion.meta, ...), custom_call_target="tpu_custom_call" | custom-call | flops 1048576 | bytes 65536 | tf_op jit(solution)/shard_map/local_2/pallas_call | solution.py:114
  37.6 4.1 %halo_0.2 = (bf16[2,512,128]{2,1,0:T(8,128)(2,1)S(1)}, bf16[2,512,128]{2,1,0:T(8,128)(2,1)S(1)}, bf16[4,128,256]{2,1,0:T(8,128)(2,1)S(1)}, f32[4,1,256]{2,1,0:T(1,128)S(1)}, f32[4,128,256]{2,1,0:T(8,128)S(1)}) custom-call(s32[2]{0:T(128)S(1)} %pad_add_fusion.meta, bf16[2,4,128,256]{3,2,1,0:T(8,128)(2,1)S(1)} %get-tuple-element.84.qn, ...), custom_call_target="tpu_custom_call" | custom-call | flops 1048576 | bytes 65536 | tf_op jit(solution)/shard_map/halo_0/pallas_call | solution.py:197
  42.9 4.1 %halo_1.2 = (bf16[2,512,128]{2,1,0:T(8,128)(2,1)S(1)}, bf16[2,512,128]{2,1,0:T(8,128)(2,1)S(1)}, bf16[4,128,256]{2,1,0:T(8,128)(2,1)S(1)}, f32[4,1,256]{2,1,0:T(1,128)S(1)}, f32[4,128,256]{2,1,0:T(8,128)S(1)}) custom-call(s32[2]{0:T(128)S(1)} %pad_add_fusion.meta, bf16[2,4,128,256]{3,2,1,0:T(8,128)(2,1)S(1)} %get-tuple-element.84.qn, ...), custom_call_target="tpu_custom_call" | custom-call | flops 1048576 | bytes 65536 | tf_op jit(solution)/shard_map/halo_1/pallas_call | solution.py:197
  47.4 4.1 %halo_0.3 = (bf16[2,512,128]{2,1,0:T(8,128)(2,1)S(1)}, bf16[2,512,128]{2,1,0:T(8,128)(2,1)S(1)}, bf16[4,128,256]{2,1,0:T(8,128)(2,1)S(1)}, f32[4,1,256]{2,1,0:T(1,128)S(1)}, f32[4,128,256]{2,1,0:T(8,128)S(1)}) custom-call(s32[2]{0:T(128)S(1)} %pad_add_fusion.meta, bf16[2,4,128,256]{3,2,1,0:T(8,128)(2,1)S(1)} %get-tuple-element.95.qn, ...), custom_call_target="tpu_custom_call" | custom-call | flops 1048576 | bytes 65536 | tf_op jit(solution)/shard_map/halo_0/pallas_call | solution.py:197
  51.5 2.2 %collective-permute-start.13 = (bf16[2,528,128]{2,1,0:T(8,128)(2,1)S(1)}, bf16[2,528,128]{2,1,0:T(8,128)(2,1)S(1)}, u32[]{:S(2)}, u32[]{:S(2)}) collective-permute-start(bf16[2,528,128]{2,1,0:T(8,128)(2,1)S(1)} %select_bitcast_fusion), channel_id=1, source_target_pairs={{0,2},{1,3},{2,0},{3,1},{4,6},{5,7},{6,4},{7,5},{8,10},{9,11},{10,... | collective-permute-start | bytes 811016 | tf_op jit(solution)/shard_map/ppermute | solution.py:486
  54.1 2.1 %collective-permute-start.16 = (bf16[2,2,512,128]{3,2,1,0:T(8,128)(2,1)S(1)}, bf16[2,2,512,128]{3,2,1,0:T(8,128)(2,1)S(1)}, u32[]{:S(2)}, u32[]{:S(2)}) collective-permute-start(bf16[2,2,512,128]{3,2,1,0:T(8,128)(2,1)S(1)} %pad_maximum_fusion), channel_id=1, source_target_pairs={{4,0},{5,1},{6,2},{7,3},{8,4},{9,5},{10,6},{11,7},{12,8},{13,9},{1... | collective-permute-start | bytes 1572872 | tf_op jit(solution)/shard_map/ppermute | solution.py:503
  56.2 3.3 %collective-permute-done.13.kv1 = bf16[2,528,128]{2,1,0:T(8,128)(2,1)S(1)} collective-permute-done((bf16[2,528,128]{2,1,0:T(8,128)(2,1)S(1)}, bf16[2,528,128]{2,1,0:T(8,128)(2,1)S(1)}, u32[]{:S(2)}, u32[]{:S(2)}) %collective-permute-start.13) | collective-permute-done | bytes 270368 | tf_op jit(solution)/shard_map/ppermute | solution.py:486
  59.5 4.1 %halo_1.3 = (bf16[2,512,128]{2,1,0:T(8,128)(2,1)S(1)}, bf16[2,512,128]{2,1,0:T(8,128)(2,1)S(1)}, bf16[4,128,256]{2,1,0:T(8,128)(2,1)S(1)}, f32[4,1,256]{2,1,0:T(1,128)S(1)}, f32[4,128,256]{2,1,0:T(8,128)S(1)}) custom-call(s32[2]{0:T(128)S(1)} %pad_add_fusion.meta, bf16[2,4,128,256]{3,2,1,0:T(8,128)(2,1)S(1)} %get-tuple-element.95.qn, ...), custom_call_target="tpu_custom_call" | custom-call | flops 1048576 | bytes 65536 | tf_op jit(solution)/shard_map/halo_1/pallas_call | solution.py:197
  63.6 1.5 %collective-permute-done.14.refs_1_ = bf16[2,512,128]{2,1,0:T(8,128)(2,1)S(1)} collective-permute-done((bf16[2,512,128]{2,1,0:T(8,128)(2,1)S(1)}, bf16[2,512,128]{2,1,0:T(8,128)(2,1)S(1)}, u32[]{:S(2)}, u32[]{:S(2)}) %collective-permute-start.14) | collective-permute-done | bytes 262176 | tf_op jit(solution)/shard_map/ppermute | solution.py:526
  65.2 1.9 %collective-permute-start.17 = (bf16[1,2,512,128]{3,2,1,0:T(8,128)(2,1)S(1)}, bf16[1,2,512,128]{3,2,1,0:T(8,128)(2,1)S(1)}, u32[]{:S(2)}, u32[]{:S(2)}) collective-permute-start(bf16[1,2,512,128]{3,2,1,0:T(8,128)(2,1)S(1)} %fusion.5), channel_id=1, source_target_pairs={{4,0},{5,1},{6,2},{7,3},{8,4},{9,5},{10,6},{11,7},{12,8},{13,9},{1... | collective-permute-start | bytes 786440 | tf_op jit(solution)/shard_map/ppermute | solution.py:503
  67.9 2.7 %own_2.1 = (bf16[256,512]{1,0:T(8,128)(2,1)S(1)}, bf16[256,512]{1,0:T(8,128)(2,1)S(1)}, f32[2,512,128]{2,1,0:T(8,128)S(1)}, f32[2,512,128]{2,1,0:T(8,128)S(1)}) custom-call(s32[2]{0:T(128)S(1)} %pad_add_fusion.meta, f32[1,128]{1,0:T(1,128)S(1)} %bitcast.29, bf16[2,4,128,256]{3,2,1,0:T(8,128)(2,1)S(1)} %get-tuple-element.114.qt, ...), custom_call_target="tpu_custom_call" | custom-call | flops 4294967296 | bytes 4194304 | tf_op jit(solution)/shard_map/own_2/pallas_call | solution.py:296
  70.6 4.2 %collective-permute-start.19 = (bf16[256,512]{1,0:T(8,128)(2,1)S(1)}, bf16[256,512]{1,0:T(8,128)(2,1)S(1)}, u32[]{:S(2)}, u32[]{:S(2)}) collective-permute-start(bf16[256,512]{1,0:T(8,128)(2,1)S(1)} %get-tuple-element.138), channel_id=1, source_target_pairs={{0,1},{1,0},{2,3},{3,2},{4,5},{5,4},{6,7},{7,6},{8,9},{9,8},{10,11... | collective-permute-start | bytes 786440 | tf_op jit(solution)/shard_map/ppermute | solution.py:462
  74.9 1.9 %collective-permute-start.20 = (bf16[1,2,512,128]{3,2,1,0:T(8,128)(2,1)S(1)}, bf16[1,2,512,128]{3,2,1,0:T(8,128)(2,1)S(1)}, u32[]{:S(2)}, u32[]{:S(2)}) collective-permute-start(bf16[1,2,512,128]{3,2,1,0:T(8,128)(2,1)S(1)} %fusion.6), channel_id=1, source_target_pairs={{4,0},{5,1},{6,2},{7,3},{8,4},{9,5},{10,6},{11,7},{12,8},{13,9},{1... | collective-permute-start | bytes 786440 | tf_op jit(solution)/shard_map/ppermute | solution.py:503
  76.8 2.8 %own_0.1 = (bf16[256,512]{1,0:T(8,128)(2,1)S(1)}, bf16[256,512]{1,0:T(8,128)(2,1)S(1)}, bf16[512,256]{1,0:T(8,128)(2,1)S(1)}, bf16[512,256]{1,0:T(8,128)(2,1)S(1)}) custom-call(s32[2]{0:T(128)S(1)} %pad_add_fusion.meta, f32[1,128]{1,0:T(1,128)S(1)} %bitcast.30, bf16[2,4,128,256]{3,2,1,0:T(8,128)(2,1)S(1)} %get-tuple-element.127.qt, ...), custom_call_target="tpu_custom_call" | custom-call | flops 4294967296 | bytes 4194304 | tf_op jit(solution)/shard_map/own_0/pallas_call | solution.py:296
  79.6 1.6 %collective-permute-start.21 = (bf16[512,256]{1,0:T(8,128)(2,1)S(1)}, bf16[512,256]{1,0:T(8,128)(2,1)S(1)}, u32[]{:S(2)}, u32[]{:S(2)}) collective-permute-start(bf16[512,256]{1,0:T(8,128)(2,1)S(1)} %get-tuple-element.143), channel_id=1, source_target_pairs={{0,1},{1,0},{2,3},{3,2},{4,5},{5,4},{6,7},{7,6},{8,9},{9,8},{10,11... | collective-permute-start | bytes 786440 | tf_op jit(solution)/shard_map/ppermute | solution.py:462
  81.3 3.1 %collective-permute-done.20.refs_5_ = bf16[1,2,512,128]{3,2,1,0:T(8,128)(2,1)S(1)} collective-permute-done((bf16[1,2,512,128]{3,2,1,0:T(8,128)(2,1)S(1)}, bf16[1,2,512,128]{3,2,1,0:T(8,128)(2,1)S(1)}, u32[]{:S(2)}, u32[]{:S(2)}) %collective-permute-start.20) | collective-permute-done | bytes 262176 | tf_op jit(solution)/shard_map/ppermute | solution.py:503
  85.2 2.3 %collective-permute-start.22 = (bf16[512,256]{1,0:T(8,128)(2,1)S(1)}, bf16[512,256]{1,0:T(8,128)(2,1)S(1)}, u32[]{:S(2)}, u32[]{:S(2)}) collective-permute-start(bf16[512,256]{1,0:T(8,128)(2,1)S(1)} %get-tuple-element.144), channel_id=1, source_target_pairs={{0,1},{1,0},{2,3},{3,2},{4,5},{5,4},{6,7},{7,6},{8,9},{9,8},{10,11... | collective-permute-start | bytes 786440 | tf_op jit(solution)/shard_map/ppermute | solution.py:462
  88.7 1.7 %join_key.1 = (bf16[256,1024]{1,0:T(8,128)(2,1)}, bf16[256,1024]{1,0:T(8,128)(2,1)}) custom-call(f32[1,128]{1,0:T(1,128)S(1)} %bitcast.26, bf16[256,1024]{1,0:T(8,128)(2,1)S(1)} %copy-done.1, bf16[512,256]{1,0:T(8,128)(2,1)S(1)} %get-tuple-element.139.refs_0_, bf16[512,256]{1,0:T(8,128)(2,1)S(1)} %get-tuple-element.142.refs_1_, ...), custom_call_target="tpu_custom_call" | custom-call | flops 1048576 | bytes 65536 | tf_op jit(solution)/shard_map/join_key/pallas_call | solution.py:395
  (69 shorter events, 18.6 us)
Async XLA Ops:
  1.9 6.2 %collective-permute-start.1 = (bf16[256,512]{1,0:T(8,128)(2,1)S(1)}, bf16[256,512]{1,0:T(8,128)(2,1)S(1)}, u32[]{:S(2)}, u32[]{:S(2)}) collective-permute-start(bf16[256,512]{1,0:T(8,128)(2,1)S(1)} %get-tuple-element.151), channel_id=1, source_target_pairs={{0,1},{1,0},{2,3},{3,2},{4,5},{5,4},{6,7},{7,6},{8,9},{9,8},{10,11... | collective-permute-start | bytes 786440 | tf_op jit(solution)/shard_map/ppermute | solution.py:462
  2.6 5.4 %collective-permute-start = (bf16[256,512]{1,0:T(8,128)(2,1)S(1)}, bf16[256,512]{1,0:T(8,128)(2,1)S(1)}, u32[]{:S(2)}, u32[]{:S(2)}) collective-permute-start(bf16[256,512]{1,0:T(8,128)(2,1)S(1)} %get-tuple-element.153), channel_id=1, source_target_pairs={{0,1},{1,0},{2,3},{3,2},{4,5},{5,4},{6,7},{7,6},{8,9},{9,8},{10,11... | collective-permute-start | bytes 786440 | tf_op jit(solution)/shard_map/ppermute | solution.py:462
  3.6 10.7 %collective-permute-start.4 = (bf16[256,1024]{1,0:T(8,128)(2,1)}, bf16[256,1024]{1,0:T(8,128)(2,1)S(1)}, u32[]{:S(2)}, u32[]{:S(2)}) collective-permute-start(bf16[256,1024]{1,0:T(8,128)(2,1)} %get-tuple-element.149), channel_id=1, source_target_pairs={{0,1},{1,0},{2,3},{3,2},{4,5},{5,4},{6,7},{7,6},{8,9},{9,8},{10,11... | collective-permute-start | bytes 1572872 | tf_op jit(solution)/shard_map/ppermute | solution.py:462
  6.2 8.1 %collective-permute-start.5 = (bf16[256,1024]{1,0:T(8,128)(2,1)}, bf16[256,1024]{1,0:T(8,128)(2,1)}, u32[]{:S(2)}, u32[]{:S(2)}) collective-permute-start(bf16[256,1024]{1,0:T(8,128)(2,1)} %get-tuple-element.147), channel_id=1, source_target_pairs={{0,1},{1,0},{2,3},{3,2},{4,5},{5,4},{6,7},{7,6},{8,9},{9,8},{10,11... | collective-permute-start | bytes 1572872 | tf_op jit(solution)/shard_map/ppermute | solution.py:462
  6.3 1.8 %collective-permute-start.2 = (bf16[16,128]{1,0:T(8,128)(2,1)S(1)}, bf16[16,128]{1,0:T(8,128)(2,1)S(1)}, u32[]{:S(2)}, u32[]{:S(2)}) collective-permute-start(bf16[16,128]{1,0:T(8,128)(2,1)S(1)} %broadcast_in_dim.13.ids_m), channel_id=1, source_target_pairs={{0,1},{1,0},{2,3},{3,2},{4,5},{5,4},{6,7},{7,6},{8,9},{9,8},{10,11... | collective-permute-start | bytes 12296 | tf_op jit(solution)/shard_map/ppermute | solution.py:462
  9.8 15.8 %collective-permute-start.6 = (bf16[2,2,528,128]{3,2,1,0:T(8,128)(2,1)}, bf16[2,2,528,128]{3,2,1,0:T(8,128)(2,1)S(1)}, u32[]{:S(2)}, u32[]{:S(2)}) collective-permute-start(bf16[2,2,528,128]{3,2,1,0:T(8,128)(2,1)} %get-tuple-element.79), channel_id=1, source_target_pairs={{0,4},{1,5},{2,6},{3,7},{4,8},{5,9},{6,10},{7,11},{8,12},{9,13},{1... | collective-permute-start | bytes 1622024 | tf_op jit(solution)/shard_map/ppermute | solution.py:472
  12.9 7.8 %collective-permute-start.3 = (bf16[1,2,528,128]{3,2,1,0:T(8,128)(2,1)S(1)}, bf16[1,2,528,128]{3,2,1,0:T(8,128)(2,1)}, u32[]{:S(2)}, u32[]{:S(2)}) collective-permute-start(bf16[1,2,528,128]{3,2,1,0:T(8,128)(2,1)S(1)} %get-tuple-element.75), channel_id=1, source_target_pairs={{0,2},{1,3},{2,0},{3,1},{4,6},{5,7},{6,4},{7,5},{8,10},{9,11},{10,... | collective-permute-start | bytes 811016 | tf_op jit(solution)/shard_map/ppermute | solution.py:474
  18.5 10.7 %copy-start.3 = (bf16[1,2,528,128]{3,2,1,0:T(8,128)(2,1)S(1)}, bf16[1,2,528,128]{3,2,1,0:T(8,128)(2,1)}, u32[]{:S(2)}) copy-start(bf16[1,2,528,128]{3,2,1,0:T(8,128)(2,1)} %copy-done.2) | copy-start | bytes 811012
  21.7 25.6 %collective-permute-start.10 = (bf16[2,2,528,128]{3,2,1,0:T(8,128)(2,1)S(1)}, bf16[2,2,528,128]{3,2,1,0:T(8,128)(2,1)S(1)}, u32[]{:S(2)}, u32[]{:S(2)}) collective-permute-start(bf16[2,2,528,128]{3,2,1,0:T(8,128)(2,1)S(1)} %constant_dynamic-update-slice_fusion), channel_id=1, source_target_pairs={{0,4},{1,5},{2,6},{3,7},{4,8},{5,9},{6,10},{7,11},{8,12},{9,13},{1... | collective-permute-start | bytes 1622024 | tf_op jit(solution)/shard_map/ppermute | solution.py:492
  26.6 10.9 %collective-permute-start.7 = (bf16[2,528,128]{2,1,0:T(8,128)(2,1)S(1)}, bf16[2,528,128]{2,1,0:T(8,128)(2,1)S(1)}, u32[]{:S(2)}, u32[]{:S(2)}) collective-permute-start(bf16[2,528,128]{2,1,0:T(8,128)(2,1)S(1)} %fusion.2), channel_id=1, source_target_pairs={{0,2},{1,3},{2,0},{3,1},{4,6},{5,7},{6,4},{7,5},{8,10},{9,11},{10,... | collective-permute-start | bytes 811016 | tf_op jit(solution)/shard_map/ppermute | solution.py:486
  28.9 14.1 %collective-permute-start.8 = (bf16[2,528,128]{2,1,0:T(8,128)(2,1)S(1)}, bf16[2,528,128]{2,1,0:T(8,128)(2,1)S(1)}, u32[]{:S(2)}, u32[]{:S(2)}) collective-permute-start(bf16[2,528,128]{2,1,0:T(8,128)(2,1)S(1)} %fusion.1), channel_id=1, source_target_pairs={{0,2},{1,3},{2,0},{3,1},{4,6},{5,7},{6,4},{7,5},{8,10},{9,11},{10,... | collective-permute-start | bytes 811016 | tf_op jit(solution)/shard_map/ppermute | solution.py:486
  29.2 18.2 %collective-permute-start.9 = (bf16[1,2,528,128]{3,2,1,0:T(8,128)(2,1)S(1)}, bf16[1,2,528,128]{3,2,1,0:T(8,128)(2,1)S(1)}, u32[]{:S(2)}, u32[]{:S(2)}) collective-permute-start(bf16[1,2,528,128]{3,2,1,0:T(8,128)(2,1)S(1)} %copy-done.3), channel_id=1, source_target_pairs={{0,4},{1,5},{2,6},{3,7},{4,8},{5,9},{6,10},{7,11},{8,12},{9,13},{1... | collective-permute-start | bytes 811016 | tf_op jit(solution)/shard_map/ppermute | solution.py:477
  41.6 12.2 %collective-permute-start.11 = (bf16[2,512,128]{2,1,0:T(8,128)(2,1)S(1)}, bf16[2,512,128]{2,1,0:T(8,128)(2,1)S(1)}, u32[]{:S(2)}, u32[]{:S(2)}) collective-permute-start(bf16[2,512,128]{2,1,0:T(8,128)(2,1)S(1)} %get-tuple-element.103), channel_id=1, source_target_pairs={{0,2},{1,3},{2,0},{3,1},{4,6},{5,7},{6,4},{7,5},{8,10},{9,11},{10,... | collective-permute-start | bytes 786440 | tf_op jit(solution)/shard_map/ppermute | solution.py:526
  47.0 6.9 %collective-permute-start.12 = (bf16[2,512,128]{2,1,0:T(8,128)(2,1)S(1)}, bf16[2,512,128]{2,1,0:T(8,128)(2,1)S(1)}, u32[]{:S(2)}, u32[]{:S(2)}) collective-permute-start(bf16[2,512,128]{2,1,0:T(8,128)(2,1)S(1)} %get-tuple-element.105), channel_id=1, source_target_pairs={{0,2},{1,3},{2,0},{3,1},{4,6},{5,7},{6,4},{7,5},{8,10},{9,11},{10,... | collective-permute-start | bytes 786440 | tf_op jit(solution)/shard_map/ppermute | solution.py:526
  51.5 8.0 %collective-permute-start.13 = (bf16[2,528,128]{2,1,0:T(8,128)(2,1)S(1)}, bf16[2,528,128]{2,1,0:T(8,128)(2,1)S(1)}, u32[]{:S(2)}, u32[]{:S(2)}) collective-permute-start(bf16[2,528,128]{2,1,0:T(8,128)(2,1)S(1)} %select_bitcast_fusion), channel_id=1, source_target_pairs={{0,2},{1,3},{2,0},{3,1},{4,6},{5,7},{6,4},{7,5},{8,10},{9,11},{10,... | collective-permute-start | bytes 811016 | tf_op jit(solution)/shard_map/ppermute | solution.py:486
  53.7 11.4 %collective-permute-start.14 = (bf16[2,512,128]{2,1,0:T(8,128)(2,1)S(1)}, bf16[2,512,128]{2,1,0:T(8,128)(2,1)S(1)}, u32[]{:S(2)}, u32[]{:S(2)}) collective-permute-start(bf16[2,512,128]{2,1,0:T(8,128)(2,1)S(1)} %get-tuple-element.111), channel_id=1, source_target_pairs={{0,2},{1,3},{2,0},{3,1},{4,6},{5,7},{6,4},{7,5},{8,10},{9,11},{10,... | collective-permute-start | bytes 786440 | tf_op jit(solution)/shard_map/ppermute | solution.py:526
  54.1 22.7 %collective-permute-start.16 = (bf16[2,2,512,128]{3,2,1,0:T(8,128)(2,1)S(1)}, bf16[2,2,512,128]{3,2,1,0:T(8,128)(2,1)S(1)}, u32[]{:S(2)}, u32[]{:S(2)}) collective-permute-start(bf16[2,2,512,128]{3,2,1,0:T(8,128)(2,1)S(1)} %pad_maximum_fusion), channel_id=1, source_target_pairs={{4,0},{5,1},{6,2},{7,3},{8,4},{9,5},{10,6},{11,7},{12,8},{13,9},{1... | collective-permute-start | bytes 1572872 | tf_op jit(solution)/shard_map/ppermute | solution.py:503
  65.2 11.6 %collective-permute-start.17 = (bf16[1,2,512,128]{3,2,1,0:T(8,128)(2,1)S(1)}, bf16[1,2,512,128]{3,2,1,0:T(8,128)(2,1)S(1)}, u32[]{:S(2)}, u32[]{:S(2)}) collective-permute-start(bf16[1,2,512,128]{3,2,1,0:T(8,128)(2,1)S(1)} %fusion.5), channel_id=1, source_target_pairs={{4,0},{5,1},{6,2},{7,3},{8,4},{9,5},{10,6},{11,7},{12,8},{13,9},{1... | collective-permute-start | bytes 786440 | tf_op jit(solution)/shard_map/ppermute | solution.py:503
  67.1 7.6 %collective-permute-start.15 = (bf16[2,512,128]{2,1,0:T(8,128)(2,1)S(1)}, bf16[2,512,128]{2,1,0:T(8,128)(2,1)S(1)}, u32[]{:S(2)}, u32[]{:S(2)}) collective-permute-start(bf16[2,512,128]{2,1,0:T(8,128)(2,1)S(1)} %get-tuple-element.125), channel_id=1, source_target_pairs={{0,2},{1,3},{2,0},{3,1},{4,6},{5,7},{6,4},{7,5},{8,10},{9,11},{10,... | collective-permute-start | bytes 786440 | tf_op jit(solution)/shard_map/ppermute | solution.py:526
  70.6 16.9 %collective-permute-start.19 = (bf16[256,512]{1,0:T(8,128)(2,1)S(1)}, bf16[256,512]{1,0:T(8,128)(2,1)S(1)}, u32[]{:S(2)}, u32[]{:S(2)}) collective-permute-start(bf16[256,512]{1,0:T(8,128)(2,1)S(1)} %get-tuple-element.138), channel_id=1, source_target_pairs={{0,1},{1,0},{2,3},{3,2},{4,5},{5,4},{6,7},{7,6},{8,9},{9,8},{10,11... | collective-permute-start | bytes 786440 | tf_op jit(solution)/shard_map/ppermute | solution.py:462
  74.9 9.6 %collective-permute-start.20 = (bf16[1,2,512,128]{3,2,1,0:T(8,128)(2,1)S(1)}, bf16[1,2,512,128]{3,2,1,0:T(8,128)(2,1)S(1)}, u32[]{:S(2)}, u32[]{:S(2)}) collective-permute-start(bf16[1,2,512,128]{3,2,1,0:T(8,128)(2,1)S(1)} %fusion.6), channel_id=1, source_target_pairs={{4,0},{5,1},{6,2},{7,3},{8,4},{9,5},{10,6},{11,7},{12,8},{13,9},{1... | collective-permute-start | bytes 786440 | tf_op jit(solution)/shard_map/ppermute | solution.py:503
  79.6 8.9 %collective-permute-start.21 = (bf16[512,256]{1,0:T(8,128)(2,1)S(1)}, bf16[512,256]{1,0:T(8,128)(2,1)S(1)}, u32[]{:S(2)}, u32[]{:S(2)}) collective-permute-start(bf16[512,256]{1,0:T(8,128)(2,1)S(1)} %get-tuple-element.143), channel_id=1, source_target_pairs={{0,1},{1,0},{2,3},{3,2},{4,5},{5,4},{6,7},{7,6},{8,9},{9,8},{10,11... | collective-permute-start | bytes 786440 | tf_op jit(solution)/shard_map/ppermute | solution.py:462
  81.3 6.2 %collective-permute-start.18 = (bf16[256,512]{1,0:T(8,128)(2,1)S(1)}, bf16[256,512]{1,0:T(8,128)(2,1)S(1)}, u32[]{:S(2)}, u32[]{:S(2)}) collective-permute-start(bf16[256,512]{1,0:T(8,128)(2,1)S(1)} %get-tuple-element.137), channel_id=1, source_target_pairs={{0,1},{1,0},{2,3},{3,2},{4,5},{5,4},{6,7},{7,6},{8,9},{9,8},{10,11... | collective-permute-start | bytes 786440 | tf_op jit(solution)/shard_map/ppermute | solution.py:462
  85.2 3.4 %collective-permute-start.22 = (bf16[512,256]{1,0:T(8,128)(2,1)S(1)}, bf16[512,256]{1,0:T(8,128)(2,1)S(1)}, u32[]{:S(2)}, u32[]{:S(2)}) collective-permute-start(bf16[512,256]{1,0:T(8,128)(2,1)S(1)} %get-tuple-element.144), channel_id=1, source_target_pairs={{0,1},{1,0},{2,3},{3,2},{4,5},{5,4},{6,7},{7,6},{8,9},{9,8},{10,11... | collective-permute-start | bytes 786440 | tf_op jit(solution)/shard_map/ppermute | solution.py:462
  (7 other events, 27.1 us)

commit v3 on v1

--- a/solution.py
+++ b/solution.py
@@ -154,18 +154,25 @@
         for part in range(2)
         for b in range(blocks)
     ]
-    for run in range(2 * rows // HD):
+    runs = 2 * rows // HD
+
+    def forward(run):
         low = run * HD
         doc = doc_own[piece, run]
         earlier = jnp.zeros((1, wide), f32)
         for one in ids:
             earlier = earlier + (one < doc).astype(f32)
         first = earlier.astype(jnp.int32) * BLK - low
+        s = jnp.dot(k_s[low:, :], qn[piece, run], preferred_element_type=f32)
+        e_run = e_s.at[run % 2]
+        total = total_own[piece, run] + weights(s, first, "window", token, e_run, low)
+        out = jnp.dot(vt_s[:, low:], e_run[low:, :], preferred_element_type=f32)
+        return total, out_own[piece, run] + out
+
+    def backward(run, total, out):
+        low = run * HD
         qn_run = qn[piece, run]
-        s = jnp.dot(k_s[low:, :], qn_run, preferred_element_type=f32)
-        total = total_own[piece, run] + weights(s, first, "window", token, e_s, low)
-        e = e_s[low:, :]
-        out = out_own[piece, run] + jnp.dot(vt_s[:, low:], e, preferred_element_type=f32)
+        e = e_s[run % 2, low:, :]
         inverse = 1.0 / total
         g_l = (gt[piece, run].astype(f32) * inverse).astype(b16)
         delta = jnp.sum(g_l.astype(f32) * (out * inverse), axis=0, keepdims=True)
@@ -179,6 +186,12 @@
         dk_s[low:, :] = dk if run == 0 else dk_s[low:, :] + dk
         dq_out[run] = jnp.dot(kt_s[:, low:], ds, preferred_element_type=f32)
 
+    state = forward(0)
+    for run in range(runs):
+        following = forward(run + 1) if run + 1 < runs else None
+        backward(run, *state)
+        state = following
+
     for target, base in ((h2, 0), (h1, 2 * rows)):
         for part in range(2):
             off = pl.multiple_of(base + (core if part == 0 else 1 - core) * rows, rows)
@@ -203,7 +216,7 @@
             pltpu.VMEM((HD, WINDOW), b16),
             pltpu.VMEM((WINDOW, HD), f32),
             pltpu.VMEM((WINDOW, HD), f32),
-            pltpu.VMEM((WINDOW, wide), b16),
+            pltpu.VMEM((2, WINDOW, wide), b16),
         ],
         out_shape=[
             jax.ShapeDtypeStruct((2, 2 * rows, HD), b16),

time: 82.8 us -> 82.6 us (level)
  transfers between devices with their start and end apart: 21 -> 21, of which waited for: 4 -> 4; matrix products, arithmetic and copies ran while one was open for 5% -> 5% of each run, Pallas kernels for 38% -> 37%
where the time goes in v3:
time: 82.6 us; the launch traced here: 81.3 us
  starting transfers between devices  38.3 us (46%)
  Pallas kernels  32 us (39%)
  other arithmetic  4.71 us (6%)
  waiting for transfers between devices  2.66 us (3%)
  local copies, waits for them, and re-layouts  2.53 us (3%)
  between operations  1 us (1%)
    pallas_call x4, Pallas kernels, halo(): pl.pallas_call(functools.partial(halo_kernel, piece, at, rows), in_specs=...  16.1 us
    ppermute x4, starting transfers between devices, on_device(): swap = lambda array: lax.ppermute(array, 'ctx', core_swap)  11 us
    ppermute x3, starting transfers between devices, on_device(): kv2.append((lax.ppermute(block, 'ctx', ahead), 0))  9.43 us
    pallas_call x2, Pallas kernels, local(): pl.pallas_call(functools.partial(local_kernel, rows), grid_spec=pltpu.Pre...  6.76 us
    ppermute x3, starting transfers between devices, send_back(): moved = lax.ppermute(joined[-1], 'ctx', back)  5.98 us
    pallas_call x2, Pallas kernels, own_keys(): pl.pallas_call(functools.partial(own_kernel, tuple(range(len(pieces))), p...  5.53 us
    ppermute x4, starting transfers between devices, on_device(): swapped.append(lax.ppermute(h1, 'ctx', x_swap))  4.58 us
    ppermute x1, starting transfers between devices, far_hop(): moved = lax.ppermute(block, 'ctx', ahead)  2.84 us
  transfers between devices with their start and end apart: 21, of which 4 were waited for; matrix products, arithmetic and copies ran while one was open for 5% of the time, Pallas kernels for 37%

profile of v3, /device:TPU:5, one launch (start us, length us, event | category | flops | bytes accessed | tf_op | source)
XLA Modules:
  0.0 81.3 jit_solution(3956374705365468206)
XLA Ops:
  7.4 3.1 %collective-permute-start.1 = (bf16[1,2,528,128]{3,2,1,0:T(8,128)(2,1)S(1)}, bf16[1,2,528,128]{3,2,1,0:T(8,128)(2,1)S(1)}, u32[]{:S(2)}, u32[]{:S(2)}) collective-permute-start(bf16[1,2,528,128]{3,2,1,0:T(8,128)(2,1)S(1)} %get-tuple-element.75), channel_id=1, source_target_pairs={{0,4},{1,5},{2,6},{3,7},{4,8},{5,9},{6,10},{7,11},{8,12},{9,13},{1... | collective-permute-start | bytes 811016 | tf_op jit(solution)/shard_map/ppermute | solution.py:480
  10.6 1.3 %pad_maximum_fusion.qg_m = bf16[2,256,1024]{2,1,0:T(8,128)(2,1)S(1)} fusion(bf16[1,256,1024]{2,1,0:T(8,128)(2,1)} %get-tuple-element.150, bf16[1,256,1024]{2,1,0:T(8,128)(2,1)} %get-tuple-element.159), kind=kLoop, calls=%fused_computation | loop fusion | flops 524288 | bytes 2097152 | tf_op jit(solution)/shard_map/stack | solution.py:466
  11.9 1.3 %collective-permute-start.2 = (bf16[1,2,528,128]{3,2,1,0:T(8,128)(2,1)S(1)}, bf16[1,2,528,128]{3,2,1,0:T(8,128)(2,1)S(1)}, u32[]{:S(2)}, u32[]{:S(2)}) collective-permute-start(bf16[1,2,528,128]{3,2,1,0:T(8,128)(2,1)S(1)} %get-tuple-element.76), channel_id=1, source_target_pairs={{0,2},{1,3},{2,0},{3,1},{4,6},{5,7},{6,4},{7,5},{8,10},{9,11},{10,... | collective-permute-start | bytes 811016 | tf_op jit(solution)/shard_map/ppermute | solution.py:481
  13.2 3.1 %collective-permute-start.4 = (bf16[1,2,528,128]{3,2,1,0:T(8,128)(2,1)S(1)}, bf16[1,2,528,128]{3,2,1,0:T(8,128)(2,1)S(1)}, u32[]{:S(2)}, u32[]{:S(2)}) collective-permute-start(bf16[1,2,528,128]{3,2,1,0:T(8,128)(2,1)S(1)} %get-tuple-element.80), channel_id=1, source_target_pairs={{0,4},{1,5},{2,6},{3,7},{4,8},{5,9},{6,10},{7,11},{8,12},{9,13},{1... | collective-permute-start | bytes 811016 | tf_op jit(solution)/shard_map/ppermute | solution.py:480
  16.4 3.1 %collective-permute-start.6 = (bf16[1,2,528,128]{3,2,1,0:T(8,128)(2,1)S(1)}, bf16[1,2,528,128]{3,2,1,0:T(8,128)(2,1)S(1)}, u32[]{:S(2)}, u32[]{:S(2)}) collective-permute-start(bf16[1,2,528,128]{3,2,1,0:T(8,128)(2,1)S(1)} %get-tuple-element.89), channel_id=1, source_target_pairs={{0,4},{1,5},{2,6},{3,7},{4,8},{5,9},{6,10},{7,11},{8,12},{9,13},{1... | collective-permute-start | bytes 811016 | tf_op jit(solution)/shard_map/ppermute | solution.py:480
  20.0 3.4 %local_0.1 = (bf16[2,4,128,256]{3,2,1,0:T(8,128)(2,1)S(1)}, bf16[2,4,128,256]{3,2,1,0:T(8,128)(2,1)S(1)}, bf16[2,4,128,256]{3,2,1,0:T(8,128)(2,1)S(1)}, bf16[2,5...) custom-call(s32[2]{0:T(128)S(1)} %pad_add_fusion.meta, ...), custom_call_target="tpu_custom_call" | custom-call | flops 1048576 | bytes 65536 | tf_op jit(solution)/shard_map/local_0/pallas_call | solution.py:112
  23.4 1.3 %collective-permute-start.7 = (bf16[2,528,128]{2,1,0:T(8,128)(2,1)S(1)}, bf16[2,528,128]{2,1,0:T(8,128)(2,1)S(1)}, u32[]{:S(2)}, u32[]{:S(2)}) collective-permute-start(bf16[2,528,128]{2,1,0:T(8,128)(2,1)S(1)} %select_bitcast_fusion.1), channel_id=1, source_target_pairs={{0,2},{1,3},{2,0},{3,1},{4,6},{5,7},{6,4},{7,5},{8,10},{9,11},{10,... | collective-permute-start | bytes 811016 | tf_op jit(solution)/shard_map/ppermute | solution.py:491
  24.7 1.8 %collective-permute-done.5.kv1 = bf16[2,528,128]{2,1,0:T(8,128)(2,1)S(1)} collective-permute-done((bf16[2,528,128]{2,1,0:T(8,128)(2,1)S(1)}, bf16[2,528,128]{2,1,0:T(8,128)(2,1)S(1)}, u32[]{:S(2)}, u32[]{:S(2)}) %collective-permute-start.5) | collective-permute-done | bytes 270368 | tf_op jit(solution)/shard_map/ppermute | solution.py:491
  26.5 4.0 %halo_0.2 = (bf16[2,512,128]{2,1,0:T(8,128)(2,1)S(1)}, bf16[2,512,128]{2,1,0:T(8,128)(2,1)S(1)}, bf16[4,128,256]{2,1,0:T(8,128)(2,1)S(1)}, f32[4,1,256]{2,1,0:T(1,128)S(1)}, f32[4,128,256]{2,1,0:T(8,128)S(1)}) custom-call(s32[2]{0:T(128)S(1)} %pad_add_fusion.meta, bf16[2,4,128,256]{3,2,1,0:T(8,128)(2,1)S(1)} %get-tuple-element.82.qn, ...), custom_call_target="tpu_custom_call" | custom-call | flops 1048576 | bytes 65536 | tf_op jit(solution)/shard_map/halo_0/pallas_call | solution.py:208
  32.3 4.0 %halo_1.2 = (bf16[2,512,128]{2,1,0:T(8,128)(2,1)S(1)}, bf16[2,512,128]{2,1,0:T(8,128)(2,1)S(1)}, bf16[4,128,256]{2,1,0:T(8,128)(2,1)S(1)}, f32[4,1,256]{2,1,0:T(1,128)S(1)}, f32[4,128,256]{2,1,0:T(8,128)S(1)}) custom-call(s32[2]{0:T(128)S(1)} %pad_add_fusion.meta, bf16[2,4,128,256]{3,2,1,0:T(8,128)(2,1)S(1)} %get-tuple-element.82.qn, ...), custom_call_target="tpu_custom_call" | custom-call | flops 1048576 | bytes 65536 | tf_op jit(solution)/shard_map/halo_1/pallas_call | solution.py:208
  37.4 2.8 %collective-permute-start.11 = (bf16[2,2,528,128]{3,2,1,0:T(8,128)(2,1)S(1)}, bf16[2,2,528,128]{3,2,1,0:T(8,128)(2,1)S(1)}, u32[]{:S(2)}, u32[]{:S(2)}) collective-permute-start(bf16[2,2,528,128]{3,2,1,0:T(8,128)(2,1)S(1)} %constant_dynamic-update-slice_fusion), channel_id=1, source_target_pairs={{0,4},{1,5},{2,6},{3,7},{4,8},{5,9},{6,10},{7,11},{8,12},{9,13},{1... | collective-permute-start | bytes 1622024 | tf_op jit(solution)/shard_map/ppermute | solution.py:497
  40.2 3.4 %local_2.1 = (bf16[2,4,128,256]{3,2,1,0:T(8,128)(2,1)S(1)}, bf16[2,4,128,256]{3,2,1,0:T(8,128)(2,1)S(1)}, bf16[2,4,128,256]{3,2,1,0:T(8,128)(2,1)S(1)}, bf16[2,5...) custom-call(s32[2]{0:T(128)S(1)} %pad_add_fusion.meta, ...), custom_call_target="tpu_custom_call" | custom-call | flops 1048576 | bytes 65536 | tf_op jit(solution)/shard_map/local_2/pallas_call | solution.py:112
  43.6 4.0 %halo_0.3 = (bf16[2,512,128]{2,1,0:T(8,128)(2,1)S(1)}, bf16[2,512,128]{2,1,0:T(8,128)(2,1)S(1)}, bf16[4,128,256]{2,1,0:T(8,128)(2,1)S(1)}, f32[4,1,256]{2,1,0:T(1,128)S(1)}, f32[4,128,256]{2,1,0:T(8,128)S(1)}) custom-call(s32[2]{0:T(128)S(1)} %pad_add_fusion.meta, bf16[2,4,128,256]{3,2,1,0:T(8,128)(2,1)S(1)} %get-tuple-element.94.qn, ...), custom_call_target="tpu_custom_call" | custom-call | flops 1048576 | bytes 65536 | tf_op jit(solution)/shard_map/halo_0/pallas_call | solution.py:208
  47.7 1.3 %collective-permute-start.12 = (bf16[2,512,128]{2,1,0:T(8,128)(2,1)S(1)}, bf16[2,512,128]{2,1,0:T(8,128)(2,1)S(1)}, u32[]{:S(2)}, u32[]{:S(2)}) collective-permute-start(bf16[2,512,128]{2,1,0:T(8,128)(2,1)S(1)} %get-tuple-element.111), channel_id=1, source_target_pairs={{0,2},{1,3},{2,0},{3,1},{4,6},{5,7},{6,4},{7,5},{8,10},{9,11},{10,... | collective-permute-start | bytes 786440 | tf_op jit(solution)/shard_map/ppermute | solution.py:529
  49.2 1.9 %collective-permute-start.14 = (bf16[2,2,512,128]{3,2,1,0:T(8,128)(2,1)S(1)}, bf16[2,2,512,128]{3,2,1,0:T(8,128)(2,1)S(1)}, u32[]{:S(2)}, u32[]{:S(2)}) collective-permute-start(bf16[2,2,512,128]{3,2,1,0:T(8,128)(2,1)S(1)} %pad_maximum_fusion.2), channel_id=1, source_target_pairs={{4,0},{5,1},{6,2},{7,3},{8,4},{9,5},{10,6},{11,7},{12,8},{13,9},{1... | collective-permute-start | bytes 1572872 | tf_op jit(solution)/shard_map/ppermute | solution.py:508
  51.2 4.0 %halo_1.3 = (bf16[2,512,128]{2,1,0:T(8,128)(2,1)S(1)}, bf16[2,512,128]{2,1,0:T(8,128)(2,1)S(1)}, bf16[4,128,256]{2,1,0:T(8,128)(2,1)S(1)}, f32[4,1,256]{2,1,0:T(1,128)S(1)}, f32[4,128,256]{2,1,0:T(8,128)S(1)}) custom-call(s32[2]{0:T(128)S(1)} %pad_add_fusion.meta, bf16[2,4,128,256]{3,2,1,0:T(8,128)(2,1)S(1)} %get-tuple-element.94.qn, ...), custom_call_target="tpu_custom_call" | custom-call | flops 1048576 | bytes 65536 | tf_op jit(solution)/shard_map/halo_1/pallas_call | solution.py:208
  56.3 1.9 %collective-permute-start.15 = (bf16[1,2,512,128]{3,2,1,0:T(8,128)(2,1)S(1)}, bf16[1,2,512,128]{3,2,1,0:T(8,128)(2,1)S(1)}, u32[]{:S(2)}, u32[]{:S(2)}) collective-permute-start(bf16[1,2,512,128]{3,2,1,0:T(8,128)(2,1)S(1)} %fusion.3), channel_id=1, source_target_pairs={{4,0},{5,1},{6,2},{7,3},{8,4},{9,5},{10,6},{11,7},{12,8},{13,9},{1... | collective-permute-start | bytes 786440 | tf_op jit(solution)/shard_map/ppermute | solution.py:508
  58.3 2.7 %own_2.1 = (bf16[256,512]{1,0:T(8,128)(2,1)S(1)}, bf16[256,512]{1,0:T(8,128)(2,1)S(1)}, f32[2,512,128]{2,1,0:T(8,128)S(1)}, f32[2,512,128]{2,1,0:T(8,128)S(1)}) custom-call(s32[2]{0:T(128)S(1)} %pad_add_fusion.meta, f32[1,128]{1,0:T(1,128)S(1)} %bitcast.37, bf16[2,4,128,256]{3,2,1,0:T(8,128)(2,1)S(1)} %get-tuple-element.114.qt, ...), custom_call_target="tpu_custom_call" | custom-call | flops 4294967296 | bytes 4194304 | tf_op jit(solution)/shard_map/own_2/pallas_call | solution.py:307
  61.0 4.4 %collective-permute-start.17 = (bf16[256,512]{1,0:T(8,128)(2,1)S(1)}, bf16[256,512]{1,0:T(8,128)(2,1)S(1)}, u32[]{:S(2)}, u32[]{:S(2)}) collective-permute-start(bf16[256,512]{1,0:T(8,128)(2,1)S(1)} %get-tuple-element.138), channel_id=1, source_target_pairs={{0,1},{1,0},{2,3},{3,2},{4,5},{5,4},{6,7},{7,6},{8,9},{9,8},{10,11... | collective-permute-start | bytes 786440 | tf_op jit(solution)/shard_map/ppermute | solution.py:552
  65.5 2.1 %collective-permute-start.18 = (bf16[1,2,512,128]{3,2,1,0:T(8,128)(2,1)S(1)}, bf16[1,2,512,128]{3,2,1,0:T(8,128)(2,1)S(1)}, u32[]{:S(2)}, u32[]{:S(2)}) collective-permute-start(bf16[1,2,512,128]{3,2,1,0:T(8,128)(2,1)S(1)} %fusion.4), channel_id=1, source_target_pairs={{4,0},{5,1},{6,2},{7,3},{8,4},{9,5},{10,6},{11,7},{12,8},{13,9},{1... | collective-permute-start | bytes 786440 | tf_op jit(solution)/shard_map/ppermute | solution.py:508
  67.7 2.8 %own_0.1 = (bf16[256,512]{1,0:T(8,128)(2,1)S(1)}, bf16[256,512]{1,0:T(8,128)(2,1)S(1)}, bf16[512,256]{1,0:T(8,128)(2,1)S(1)}, bf16[512,256]{1,0:T(8,128)(2,1)S(1)}) custom-call(s32[2]{0:T(128)S(1)} %pad_add_fusion.meta, f32[1,128]{1,0:T(1,128)S(1)} %bitcast.38, bf16[2,4,128,256]{3,2,1,0:T(8,128)(2,1)S(1)} %get-tuple-element.127.qt, ...), custom_call_target="tpu_custom_call" | custom-call | flops 4294967296 | bytes 4194304 | tf_op jit(solution)/shard_map/own_0/pallas_call | solution.py:307
  70.5 4.5 %collective-permute-start.16 = (bf16[256,512]{1,0:T(8,128)(2,1)S(1)}, bf16[256,512]{1,0:T(8,128)(2,1)S(1)}, u32[]{:S(2)}, u32[]{:S(2)}) collective-permute-start(bf16[256,512]{1,0:T(8,128)(2,1)S(1)} %get-tuple-element.137), channel_id=1, source_target_pairs={{0,1},{1,0},{2,3},{3,2},{4,5},{5,4},{6,7},{7,6},{8,9},{9,8},{10,11... | collective-permute-start | bytes 786440 | tf_op jit(solution)/shard_map/ppermute | solution.py:552
  76.5 1.9 %collective-permute-start.20 = (bf16[512,256]{1,0:T(8,128)(2,1)S(1)}, bf16[512,256]{1,0:T(8,128)(2,1)S(1)}, u32[]{:S(2)}, u32[]{:S(2)}) collective-permute-start(bf16[512,256]{1,0:T(8,128)(2,1)S(1)} %get-tuple-element.144), channel_id=1, source_target_pairs={{0,1},{1,0},{2,3},{3,2},{4,5},{5,4},{6,7},{7,6},{8,9},{9,8},{10,11... | collective-permute-start | bytes 786440 | tf_op jit(solution)/shard_map/ppermute | solution.py:552
  79.6 1.7 %join_key.1 = (bf16[256,1024]{1,0:T(8,128)(2,1)}, bf16[256,1024]{1,0:T(8,128)(2,1)}) custom-call(f32[1,128]{1,0:T(1,128)S(1)} %bitcast.34, bf16[256,1024]{1,0:T(8,128)(2,1)S(1)} %copy-done, bf16[512,256]{1,0:T(8,128)(2,1)S(1)} %get-tuple-element.139.refs_0_, bf16[512,256]{1,0:T(8,128)(2,1)S(1)} %get-tuple-element.142.refs_1_, ...), custom_call_target="tpu_custom_call" | custom-call | flops 1048576 | bytes 65536 | tf_op jit(solution)/shard_map/join_key/pallas_call | solution.py:406
  (59 shorter events, 14.1 us)
Async XLA Ops:
  3.7 3.6 %collective-permute-start = (bf16[528,512]{1,0:T(8,128)(2,1)}, bf16[528,512]{1,0:T(8,128)(2,1)S(1)}, u32[]{:S(2)}, u32[]{:S(2)}) collective-permute-start(bf16[528,512]{1,0:T(8,128)(2,1)} %get-tuple-element.155), channel_id=1, source_target_pairs={{0,1},{1,0},{2,3},{3,2},{4,5},{5,4},{6,7},{7,6},{8,9},{9,8},{10,11... | collective-permute-start | bytes 1622024 | tf_op jit(solution)/shard_map/ppermute | solution.py:474
  6.6 13.4 %collective-permute-start.3 = (bf16[2,256,1024]{2,1,0:T(8,128)(2,1)}, bf16[2,256,1024]{2,1,0:T(8,128)(2,1)S(1)}, u32[]{:S(2)}, u32[]{:S(2)}) collective-permute-start(bf16[2,256,1024]{2,1,0:T(8,128)(2,1)} %pad_maximum_fusion.1), channel_id=1, source_target_pairs={{0,1},{1,0},{2,3},{3,2},{4,5},{5,4},{6,7},{7,6},{8,9},{9,8},{10,11... | collective-permute-start | bytes 3145736 | tf_op jit(solution)/shard_map/ppermute | solution.py:483
  7.4 12.1 %collective-permute-start.1 = (bf16[1,2,528,128]{3,2,1,0:T(8,128)(2,1)S(1)}, bf16[1,2,528,128]{3,2,1,0:T(8,128)(2,1)S(1)}, u32[]{:S(2)}, u32[]{:S(2)}) collective-permute-start(bf16[1,2,528,128]{3,2,1,0:T(8,128)(2,1)S(1)} %get-tuple-element.75), channel_id=1, source_target_pairs={{0,4},{1,5},{2,6},{3,7},{4,8},{5,9},{6,10},{7,11},{8,12},{9,13},{1... | collective-permute-start | bytes 811016 | tf_op jit(solution)/shard_map/ppermute | solution.py:480
  10.6 9.4 %copy-start.1 = (f32[128]{0:T(128)S(1)}, f32[128]{0:T(128)}, u32[]{:S(2)}) copy-start(f32[128]{0:T(128)} %param.12) | copy-start | bytes 1540
  10.6 9.4 %copy-start.2 = (f32[128]{0:T(128)S(1)}, f32[128]{0:T(128)}, u32[]{:S(2)}) copy-start(f32[128]{0:T(128)} %param.11) | copy-start | bytes 1540
  11.9 8.0 %collective-permute-start.2 = (bf16[1,2,528,128]{3,2,1,0:T(8,128)(2,1)S(1)}, bf16[1,2,528,128]{3,2,1,0:T(8,128)(2,1)S(1)}, u32[]{:S(2)}, u32[]{:S(2)}) collective-permute-start(bf16[1,2,528,128]{3,2,1,0:T(8,128)(2,1)S(1)} %get-tuple-element.76), channel_id=1, source_target_pairs={{0,2},{1,3},{2,0},{3,1},{4,6},{5,7},{6,4},{7,5},{8,10},{9,11},{10,... | collective-permute-start | bytes 811016 | tf_op jit(solution)/shard_map/ppermute | solution.py:481
  13.2 10.2 %collective-permute-start.4 = (bf16[1,2,528,128]{3,2,1,0:T(8,128)(2,1)S(1)}, bf16[1,2,528,128]{3,2,1,0:T(8,128)(2,1)S(1)}, u32[]{:S(2)}, u32[]{:S(2)}) collective-permute-start(bf16[1,2,528,128]{3,2,1,0:T(8,128)(2,1)S(1)} %get-tuple-element.80), channel_id=1, source_target_pairs={{0,4},{1,5},{2,6},{3,7},{4,8},{5,9},{6,10},{7,11},{8,12},{9,13},{1... | collective-permute-start | bytes 811016 | tf_op jit(solution)/shard_map/ppermute | solution.py:480
  16.4 14.2 %collective-permute-start.6 = (bf16[1,2,528,128]{3,2,1,0:T(8,128)(2,1)S(1)}, bf16[1,2,528,128]{3,2,1,0:T(8,128)(2,1)S(1)}, u32[]{:S(2)}, u32[]{:S(2)}) collective-permute-start(bf16[1,2,528,128]{3,2,1,0:T(8,128)(2,1)S(1)} %get-tuple-element.89), channel_id=1, source_target_pairs={{0,4},{1,5},{2,6},{3,7},{4,8},{5,9},{6,10},{7,11},{8,12},{9,13},{1... | collective-permute-start | bytes 811016 | tf_op jit(solution)/shard_map/ppermute | solution.py:480
  19.6 6.9 %collective-permute-start.5 = (bf16[2,528,128]{2,1,0:T(8,128)(2,1)S(1)}, bf16[2,528,128]{2,1,0:T(8,128)(2,1)S(1)}, u32[]{:S(2)}, u32[]{:S(2)}) collective-permute-start(bf16[2,528,128]{2,1,0:T(8,128)(2,1)S(1)} %select_bitcast_fusion.2), channel_id=1, source_target_pairs={{0,2},{1,3},{2,0},{3,1},{4,6},{5,7},{6,4},{7,5},{8,10},{9,11},{10,... | collective-permute-start | bytes 811016 | tf_op jit(solution)/shard_map/ppermute | solution.py:491
  23.4 8.8 %collective-permute-start.7 = (bf16[2,528,128]{2,1,0:T(8,128)(2,1)S(1)}, bf16[2,528,128]{2,1,0:T(8,128)(2,1)S(1)}, u32[]{:S(2)}, u32[]{:S(2)}) collective-permute-start(bf16[2,528,128]{2,1,0:T(8,128)(2,1)S(1)} %select_bitcast_fusion.1), channel_id=1, source_target_pairs={{0,2},{1,3},{2,0},{3,1},{4,6},{5,7},{6,4},{7,5},{8,10},{9,11},{10,... | collective-permute-start | bytes 811016 | tf_op jit(solution)/shard_map/ppermute | solution.py:491
  30.6 13.0 %collective-permute-start.8 = (bf16[2,528,128]{2,1,0:T(8,128)(2,1)S(1)}, bf16[2,528,128]{2,1,0:T(8,128)(2,1)S(1)}, u32[]{:S(2)}, u32[]{:S(2)}) collective-permute-start(bf16[2,528,128]{2,1,0:T(8,128)(2,1)S(1)} %select_bitcast_fusion), channel_id=1, source_target_pairs={{0,2},{1,3},{2,0},{3,1},{4,6},{5,7},{6,4},{7,5},{8,10},{9,11},{10,... | collective-permute-start | bytes 811016 | tf_op jit(solution)/shard_map/ppermute | solution.py:491
  30.9 18.1 %collective-permute-start.9 = (bf16[2,512,128]{2,1,0:T(8,128)(2,1)S(1)}, bf16[2,512,128]{2,1,0:T(8,128)(2,1)S(1)}, u32[]{:S(2)}, u32[]{:S(2)}) collective-permute-start(bf16[2,512,128]{2,1,0:T(8,128)(2,1)S(1)} %get-tuple-element.103), channel_id=1, source_target_pairs={{0,2},{1,3},{2,0},{3,1},{4,6},{5,7},{6,4},{7,5},{8,10},{9,11},{10,... | collective-permute-start | bytes 786440 | tf_op jit(solution)/shard_map/ppermute | solution.py:529
  36.3 12.7 %collective-permute-start.10 = (bf16[2,512,128]{2,1,0:T(8,128)(2,1)S(1)}, bf16[2,512,128]{2,1,0:T(8,128)(2,1)S(1)}, u32[]{:S(2)}, u32[]{:S(2)}) collective-permute-start(bf16[2,512,128]{2,1,0:T(8,128)(2,1)S(1)} %get-tuple-element.105), channel_id=1, source_target_pairs={{0,2},{1,3},{2,0},{3,1},{4,6},{5,7},{6,4},{7,5},{8,10},{9,11},{10,... | collective-permute-start | bytes 786440 | tf_op jit(solution)/shard_map/ppermute | solution.py:529
  37.4 13.8 %collective-permute-start.11 = (bf16[2,2,528,128]{3,2,1,0:T(8,128)(2,1)S(1)}, bf16[2,2,528,128]{3,2,1,0:T(8,128)(2,1)S(1)}, u32[]{:S(2)}, u32[]{:S(2)}) collective-permute-start(bf16[2,2,528,128]{3,2,1,0:T(8,128)(2,1)S(1)} %constant_dynamic-update-slice_fusion), channel_id=1, source_target_pairs={{0,4},{1,5},{2,6},{3,7},{4,8},{5,9},{6,10},{7,11},{8,12},{9,13},{1... | collective-permute-start | bytes 1622024 | tf_op jit(solution)/shard_map/ppermute | solution.py:497
  47.7 8.6 %collective-permute-start.12 = (bf16[2,512,128]{2,1,0:T(8,128)(2,1)S(1)}, bf16[2,512,128]{2,1,0:T(8,128)(2,1)S(1)}, u32[]{:S(2)}, u32[]{:S(2)}) collective-permute-start(bf16[2,512,128]{2,1,0:T(8,128)(2,1)S(1)} %get-tuple-element.111), channel_id=1, source_target_pairs={{0,2},{1,3},{2,0},{3,1},{4,6},{5,7},{6,4},{7,5},{8,10},{9,11},{10,... | collective-permute-start | bytes 786440 | tf_op jit(solution)/shard_map/ppermute | solution.py:529
  49.2 18.5 %collective-permute-start.14 = (bf16[2,2,512,128]{3,2,1,0:T(8,128)(2,1)S(1)}, bf16[2,2,512,128]{3,2,1,0:T(8,128)(2,1)S(1)}, u32[]{:S(2)}, u32[]{:S(2)}) collective-permute-start(bf16[2,2,512,128]{3,2,1,0:T(8,128)(2,1)S(1)} %pad_maximum_fusion.2), channel_id=1, source_target_pairs={{4,0},{5,1},{6,2},{7,3},{8,4},{9,5},{10,6},{11,7},{12,8},{13,9},{1... | collective-permute-start | bytes 1572872 | tf_op jit(solution)/shard_map/ppermute | solution.py:508
  55.2 10.2 %collective-permute-start.13 = (bf16[2,512,128]{2,1,0:T(8,128)(2,1)S(1)}, bf16[2,512,128]{2,1,0:T(8,128)(2,1)S(1)}, u32[]{:S(2)}, u32[]{:S(2)}) collective-permute-start(bf16[2,512,128]{2,1,0:T(8,128)(2,1)S(1)} %get-tuple-element.125), channel_id=1, source_target_pairs={{0,2},{1,3},{2,0},{3,1},{4,6},{5,7},{6,4},{7,5},{8,10},{9,11},{10,... | collective-permute-start | bytes 786440 | tf_op jit(solution)/shard_map/ppermute | solution.py:529
  56.3 11.3 %collective-permute-start.15 = (bf16[1,2,512,128]{3,2,1,0:T(8,128)(2,1)S(1)}, bf16[1,2,512,128]{3,2,1,0:T(8,128)(2,1)S(1)}, u32[]{:S(2)}, u32[]{:S(2)}) collective-permute-start(bf16[1,2,512,128]{3,2,1,0:T(8,128)(2,1)S(1)} %fusion.3), channel_id=1, source_target_pairs={{4,0},{5,1},{6,2},{7,3},{8,4},{9,5},{10,6},{11,7},{12,8},{13,9},{1... | collective-permute-start | bytes 786440 | tf_op jit(solution)/shard_map/ppermute | solution.py:508
  61.0 17.4 %collective-permute-start.17 = (bf16[256,512]{1,0:T(8,128)(2,1)S(1)}, bf16[256,512]{1,0:T(8,128)(2,1)S(1)}, u32[]{:S(2)}, u32[]{:S(2)}) collective-permute-start(bf16[256,512]{1,0:T(8,128)(2,1)S(1)} %get-tuple-element.138), channel_id=1, source_target_pairs={{0,1},{1,0},{2,3},{3,2},{4,5},{5,4},{6,7},{7,6},{8,9},{9,8},{10,11... | collective-permute-start | bytes 786440 | tf_op jit(solution)/shard_map/ppermute | solution.py:552
  65.5 10.2 %collective-permute-start.18 = (bf16[1,2,512,128]{3,2,1,0:T(8,128)(2,1)S(1)}, bf16[1,2,512,128]{3,2,1,0:T(8,128)(2,1)S(1)}, u32[]{:S(2)}, u32[]{:S(2)}) collective-permute-start(bf16[1,2,512,128]{3,2,1,0:T(8,128)(2,1)S(1)} %fusion.4), channel_id=1, source_target_pairs={{4,0},{5,1},{6,2},{7,3},{8,4},{9,5},{10,6},{11,7},{12,8},{13,9},{1... | collective-permute-start | bytes 786440 | tf_op jit(solution)/shard_map/ppermute | solution.py:508
  70.5 7.9 %collective-permute-start.16 = (bf16[256,512]{1,0:T(8,128)(2,1)S(1)}, bf16[256,512]{1,0:T(8,128)(2,1)S(1)}, u32[]{:S(2)}, u32[]{:S(2)}) collective-permute-start(bf16[256,512]{1,0:T(8,128)(2,1)S(1)} %get-tuple-element.137), channel_id=1, source_target_pairs={{0,1},{1,0},{2,3},{3,2},{4,5},{5,4},{6,7},{7,6},{8,9},{9,8},{10,11... | collective-permute-start | bytes 786440 | tf_op jit(solution)/shard_map/ppermute | solution.py:552
  75.0 4.4 %collective-permute-start.19 = (bf16[512,256]{1,0:T(8,128)(2,1)S(1)}, bf16[512,256]{1,0:T(8,128)(2,1)S(1)}, u32[]{:S(2)}, u32[]{:S(2)}) collective-permute-start(bf16[512,256]{1,0:T(8,128)(2,1)S(1)} %get-tuple-element.143), channel_id=1, source_target_pairs={{0,1},{1,0},{2,3},{3,2},{4,5},{5,4},{6,7},{7,6},{8,9},{9,8},{10,11... | collective-permute-start | bytes 786440 | tf_op jit(solution)/shard_map/ppermute | solution.py:552
  76.5 3.1 %copy-start = (bf16[256,1024]{1,0:T(8,128)(2,1)S(1)}, bf16[256,1024]{1,0:T(8,128)(2,1)}, u32[]{:S(2)}) copy-start(bf16[256,1024]{1,0:T(8,128)(2,1)} %keys.1) | copy-start | bytes 1572868
  76.5 3.1 %collective-permute-start.20 = (bf16[512,256]{1,0:T(8,128)(2,1)S(1)}, bf16[512,256]{1,0:T(8,128)(2,1)S(1)}, u32[]{:S(2)}, u32[]{:S(2)}) collective-permute-start(bf16[512,256]{1,0:T(8,128)(2,1)S(1)} %get-tuple-element.144), channel_id=1, source_target_pairs={{0,1},{1,0},{2,3},{3,2},{4,5},{5,4},{6,7},{7,6},{8,9},{9,8},{10,11... | collective-permute-start | bytes 786440 | tf_op jit(solution)/shard_map/ppermute | solution.py:552
  (2 other events, 3.5 us)

commit v4 on v3

--- a/solution.py
+++ b/solution.py
@@ -476,7 +476,7 @@
 
     kv0 = lay(kv_m, kv_t)
     kv1, kv2 = [], []
-    for block in kv0[:-1]:
+    for block in kv0[:2]:
         kv2.append((lax.ppermute(block, "ctx", ahead), 0))
     neighbour = lax.ppermute(kv0[-1], "ctx", x_swap)
     qg_m = both(queries, out_grad, core)
@@ -509,6 +509,8 @@
         returned.extend((moved, at) for at in range(len(group)))
 
     hop_0 = x_hop(0, odd)
+    for block in kv0[2:-1]:
+        kv2.append((lax.ppermute(after(block, hop_0), "ctx", ahead), 0))
     middle = pieces // 2
     local_part = lambda begin, order: local(
         begin, middle, order, qg_m, qg_t, kv_m, kv_t, q_gain_row, k_gain_row

time: 82.6 us -> 83.2 us (level); the launches traced: 81.3 us -> 82.8 us
  waiting for transfers between devices: 2.66 us -> 5.77 us
  starting transfers between devices: 38.3 us -> 36.8 us
    ppermute x0 -> x1, starting transfers between devices: none -> 4.03 us  [on_device(): kv2.append((lax.ppermute(after(block, hop_0), 'ctx', ahead), 0))]
    ppermute x3 -> x2, starting transfers between devices: 9.43 us -> 6.28 us  [on_device(): kv2.append((lax.ppermute(block, 'ctx', ahead), 0))]
    ppermute x4, starting transfers between devices: 4.58 us -> 1.92 us  [on_device(): swapped.append(lax.ppermute(h1, 'ctx', x_swap))]
    ppermute x4, waiting for transfers between devices: 0.01 us -> 2.39 us  [on_device(): swapped.append(lax.ppermute(h1, 'ctx', x_swap))]
    ppermute x3, waiting for transfers between devices: 1.88 us -> 0.3 us  [x_hop(): kv1.append(lax.ppermute(operand, 'ctx', x_swap))]
    ppermute x3, waiting for transfers between devices: 0.6 us -> 1.83 us  [send_back(): moved = lax.ppermute(joined[-1], 'ctx', back)]
    ppermute x3 -> x2, waiting for transfers between devices: 0.01 us -> 1.08 us  [on_device(): kv2.append((lax.ppermute(block, 'ctx', ahead), 0))]
    ppermute x3, starting transfers between devices: 1.92 us -> 2.87 us  [x_hop(): kv1.append(lax.ppermute(operand, 'ctx', x_swap))]
  transfers between devices with their start and end apart: 21 -> 21, of which waited for: 4 -> 5; matrix products, arithmetic and copies ran while one was open for 5% -> 5% of each run, Pallas kernels for 37% -> 37%
where the time goes in v4:
time: 83.2 us; the launch traced here: 82.8 us
  starting transfers between devices  36.8 us (44%)
  Pallas kernels  32 us (38%)
  waiting for transfers between devices  5.77 us (7%)
  other arithmetic  4.69 us (6%)
  local copies, waits for them, and re-layouts  2.53 us (3%)
  between operations  0.98 us (1%)
    pallas_call x4, Pallas kernels, halo(): pl.pallas_call(functools.partial(halo_kernel, piece, at, rows), in_specs=...  16.1 us
    ppermute x4, starting transfers between devices, on_device(): swap = lambda array: lax.ppermute(array, 'ctx', core_swap)  10.7 us
    pallas_call x2, Pallas kernels, local(): pl.pallas_call(functools.partial(local_kernel, rows), grid_spec=pltpu.Pre...  6.76 us
    ppermute x2, starting transfers between devices, on_device(): kv2.append((lax.ppermute(block, 'ctx', ahead), 0))  6.28 us
    ppermute x3, starting transfers between devices, send_back(): moved = lax.ppermute(joined[-1], 'ctx', back)  5.98 us
    pallas_call x2, Pallas kernels, own_keys(): pl.pallas_call(functools.partial(own_kernel, tuple(range(len(pieces))), p...  5.5 us
    ppermute x1, starting transfers between devices, on_device(): kv2.append((lax.ppermute(after(block, hop_0), 'ctx', ahead), 0))  4.03 us
    ppermute x3, starting transfers between devices, x_hop(): kv1.append(lax.ppermute(operand, 'ctx', x_swap))  2.87 us
  transfers between devices with their start and end apart: 21, of which 5 were waited for; matrix products, arithmetic and copies ran while one was open for 5% of the time, Pallas kernels for 37%

profile of v4, /device:TPU:5, one launch (start us, length us, event | category | flops | bytes accessed | tf_op | source)
XLA Modules:
  0.0 82.8 jit_solution(13118144110535870969)
XLA Ops:
  7.4 3.1 %collective-permute-start.1 = (bf16[1,2,528,128]{3,2,1,0:T(8,128)(2,1)S(1)}, bf16[1,2,528,128]{3,2,1,0:T(8,128)(2,1)S(1)}, u32[]{:S(2)}, u32[]{:S(2)}) collective-permute-start(bf16[1,2,528,128]{3,2,1,0:T(8,128)(2,1)S(1)} %get-tuple-element.76), channel_id=1, source_target_pairs={{0,4},{1,5},{2,6},{3,7},{4,8},{5,9},{6,10},{7,11},{8,12},{9,13},{1... | collective-permute-start | bytes 811016 | tf_op jit(solution)/shard_map/ppermute | solution.py:480
  10.6 1.3 %pad_maximum_fusion.qg_m = bf16[2,256,1024]{2,1,0:T(8,128)(2,1)S(1)} fusion(bf16[1,256,1024]{2,1,0:T(8,128)(2,1)} %get-tuple-element.152, bf16[1,256,1024]{2,1,0:T(8,128)(2,1)} %get-tuple-element.161), kind=kLoop, calls=%fused_computation | loop fusion | flops 524288 | bytes 2097152 | tf_op jit(solution)/shard_map/stack | solution.py:466
  11.9 1.3 %collective-permute-start.2 = (bf16[1,2,528,128]{3,2,1,0:T(8,128)(2,1)S(1)}, bf16[1,2,528,128]{3,2,1,0:T(8,128)(2,1)S(1)}, u32[]{:S(2)}, u32[]{:S(2)}) collective-permute-start(bf16[1,2,528,128]{3,2,1,0:T(8,128)(2,1)S(1)} %get-tuple-element.77), channel_id=1, source_target_pairs={{0,2},{1,3},{2,0},{3,1},{4,6},{5,7},{6,4},{7,5},{8,10},{9,11},{10,... | collective-permute-start | bytes 811016 | tf_op jit(solution)/shard_map/ppermute | solution.py:481
  13.2 3.1 %collective-permute-start.4 = (bf16[1,2,528,128]{3,2,1,0:T(8,128)(2,1)S(1)}, bf16[1,2,528,128]{3,2,1,0:T(8,128)(2,1)S(1)}, u32[]{:S(2)}, u32[]{:S(2)}) collective-permute-start(bf16[1,2,528,128]{3,2,1,0:T(8,128)(2,1)S(1)} %get-tuple-element.81), channel_id=1, source_target_pairs={{0,4},{1,5},{2,6},{3,7},{4,8},{5,9},{6,10},{7,11},{8,12},{9,13},{1... | collective-permute-start | bytes 811016 | tf_op jit(solution)/shard_map/ppermute | solution.py:480
  17.5 1.3 %collective-permute-start.5 = (bf16[2,528,128]{2,1,0:T(8,128)(2,1)S(1)}, bf16[2,528,128]{2,1,0:T(8,128)(2,1)S(1)}, u32[]{:S(2)}, u32[]{:S(2)}) collective-permute-start(bf16[2,528,128]{2,1,0:T(8,128)(2,1)S(1)} %select_bitcast_fusion.2), channel_id=1, source_target_pairs={{0,2},{1,3},{2,0},{3,1},{4,6},{5,7},{6,4},{7,5},{8,10},{9,11},{10,... | collective-permute-start | bytes 811016 | tf_op jit(solution)/shard_map/ppermute | solution.py:491
  18.8 4.0 %collective-permute-start.6 = (bf16[1,2,528,128]{3,2,1,0:T(8,128)(2,1)S(1)}, bf16[1,2,528,128]{3,2,1,0:T(8,128)(2,1)S(1)}, u32[]{:S(2)}, u32[]{:S(2)}) collective-permute-start(bf16[1,2,528,128]{3,2,1,0:T(8,128)(2,1)S(1)} %get-tuple-element.91), channel_id=1, source_target_pairs={{0,4},{1,5},{2,6},{3,7},{4,8},{5,9},{6,10},{7,11},{8,12},{9,13},{1... | collective-permute-start | bytes 811016 | tf_op jit(solution)/shard_map/ppermute | solution.py:513
  22.9 3.4 %local_0.1 = (bf16[2,4,128,256]{3,2,1,0:T(8,128)(2,1)S(1)}, bf16[2,4,128,256]{3,2,1,0:T(8,128)(2,1)S(1)}, bf16[2,4,128,256]{3,2,1,0:T(8,128)(2,1)S(1)}, bf16[2,5...) custom-call(s32[2]{0:T(128)S(1)} %pad_add_fusion.meta, ...), custom_call_target="tpu_custom_call" | custom-call | flops 1048576 | bytes 65536 | tf_op jit(solution)/shard_map/local_0/pallas_call | solution.py:112
  26.7 4.0 %halo_0.2 = (bf16[2,512,128]{2,1,0:T(8,128)(2,1)S(1)}, bf16[2,512,128]{2,1,0:T(8,128)(2,1)S(1)}, bf16[4,128,256]{2,1,0:T(8,128)(2,1)S(1)}, f32[4,1,256]{2,1,0:T(1,128)S(1)}, f32[4,128,256]{2,1,0:T(8,128)S(1)}) custom-call(s32[2]{0:T(128)S(1)} %pad_add_fusion.meta, bf16[2,4,128,256]{3,2,1,0:T(8,128)(2,1)S(1)} %get-tuple-element.83.qn, ...), custom_call_target="tpu_custom_call" | custom-call | flops 1048576 | bytes 65536 | tf_op jit(solution)/shard_map/halo_0/pallas_call | solution.py:208
  30.8 1.3 %collective-permute-start.8 = (bf16[2,528,128]{2,1,0:T(8,128)(2,1)S(1)}, bf16[2,528,128]{2,1,0:T(8,128)(2,1)S(1)}, u32[]{:S(2)}, u32[]{:S(2)}) collective-permute-start(bf16[2,528,128]{2,1,0:T(8,128)(2,1)S(1)} %select_bitcast_fusion), channel_id=1, source_target_pairs={{0,2},{1,3},{2,0},{3,1},{4,6},{5,7},{6,4},{7,5},{8,10},{9,11},{10,... | collective-permute-start | bytes 811016 | tf_op jit(solution)/shard_map/ppermute | solution.py:491
  32.7 4.0 %halo_1.2 = (bf16[2,512,128]{2,1,0:T(8,128)(2,1)S(1)}, bf16[2,512,128]{2,1,0:T(8,128)(2,1)S(1)}, bf16[4,128,256]{2,1,0:T(8,128)(2,1)S(1)}, f32[4,1,256]{2,1,0:T(1,128)S(1)}, f32[4,128,256]{2,1,0:T(8,128)S(1)}) custom-call(s32[2]{0:T(128)S(1)} %pad_add_fusion.meta, bf16[2,4,128,256]{3,2,1,0:T(8,128)(2,1)S(1)} %get-tuple-element.83.qn, ...), custom_call_target="tpu_custom_call" | custom-call | flops 1048576 | bytes 65536 | tf_op jit(solution)/shard_map/halo_1/pallas_call | solution.py:208
  37.7 2.4 %collective-permute-start.11 = (bf16[2,2,528,128]{3,2,1,0:T(8,128)(2,1)S(1)}, bf16[2,2,528,128]{3,2,1,0:T(8,128)(2,1)S(1)}, u32[]{:S(2)}, u32[]{:S(2)}) collective-permute-start(bf16[2,2,528,128]{3,2,1,0:T(8,128)(2,1)S(1)} %constant_dynamic-update-slice_fusion), channel_id=1, source_target_pairs={{0,4},{1,5},{2,6},{3,7},{4,8},{5,9},{6,10},{7,11},{8,12},{9,13},{1... | collective-permute-start | bytes 1622024 | tf_op jit(solution)/shard_map/ppermute | solution.py:497
  40.1 3.4 %local_2.1 = (bf16[2,4,128,256]{3,2,1,0:T(8,128)(2,1)S(1)}, bf16[2,4,128,256]{3,2,1,0:T(8,128)(2,1)S(1)}, bf16[2,4,128,256]{3,2,1,0:T(8,128)(2,1)S(1)}, bf16[2,5...) custom-call(s32[2]{0:T(128)S(1)} %pad_add_fusion.meta, ...), custom_call_target="tpu_custom_call" | custom-call | flops 1048576 | bytes 65536 | tf_op jit(solution)/shard_map/local_2/pallas_call | solution.py:112
  43.5 4.0 %halo_0.3 = (bf16[2,512,128]{2,1,0:T(8,128)(2,1)S(1)}, bf16[2,512,128]{2,1,0:T(8,128)(2,1)S(1)}, bf16[4,128,256]{2,1,0:T(8,128)(2,1)S(1)}, f32[4,1,256]{2,1,0:T(1,128)S(1)}, f32[4,128,256]{2,1,0:T(8,128)S(1)}) custom-call(s32[2]{0:T(128)S(1)} %pad_add_fusion.meta, bf16[2,4,128,256]{3,2,1,0:T(8,128)(2,1)S(1)} %get-tuple-element.96.qn, ...), custom_call_target="tpu_custom_call" | custom-call | flops 1048576 | bytes 65536 | tf_op jit(solution)/shard_map/halo_0/pallas_call | solution.py:208
  48.2 2.4 %collective-permute-done.10.refs_8_ = bf16[2,512,128]{2,1,0:T(8,128)(2,1)S(1)} collective-permute-done((bf16[2,512,128]{2,1,0:T(8,128)(2,1)S(1)}, bf16[2,512,128]{2,1,0:T(8,128)(2,1)S(1)}, u32[]{:S(2)}, u32[]{:S(2)}) %collective-permute-start.10) | collective-permute-done | bytes 262176 | tf_op jit(solution)/shard_map/ppermute | solution.py:531
  50.8 1.9 %collective-permute-start.14 = (bf16[2,2,512,128]{3,2,1,0:T(8,128)(2,1)S(1)}, bf16[2,2,512,128]{3,2,1,0:T(8,128)(2,1)S(1)}, u32[]{:S(2)}, u32[]{:S(2)}) collective-permute-start(bf16[2,2,512,128]{3,2,1,0:T(8,128)(2,1)S(1)} %pad_maximum_fusion.2), channel_id=1, source_target_pairs={{4,0},{5,1},{6,2},{7,3},{8,4},{9,5},{10,6},{11,7},{12,8},{13,9},{1... | collective-permute-start | bytes 1572872 | tf_op jit(solution)/shard_map/ppermute | solution.py:508
  52.8 4.0 %halo_1.3 = (bf16[2,512,128]{2,1,0:T(8,128)(2,1)S(1)}, bf16[2,512,128]{2,1,0:T(8,128)(2,1)S(1)}, bf16[4,128,256]{2,1,0:T(8,128)(2,1)S(1)}, f32[4,1,256]{2,1,0:T(1,128)S(1)}, f32[4,128,256]{2,1,0:T(8,128)S(1)}) custom-call(s32[2]{0:T(128)S(1)} %pad_add_fusion.meta, bf16[2,4,128,256]{3,2,1,0:T(8,128)(2,1)S(1)} %get-tuple-element.96.qn, ...), custom_call_target="tpu_custom_call" | custom-call | flops 1048576 | bytes 65536 | tf_op jit(solution)/shard_map/halo_1/pallas_call | solution.py:208
  57.0 1.9 %collective-permute-start.15 = (bf16[1,2,512,128]{3,2,1,0:T(8,128)(2,1)S(1)}, bf16[1,2,512,128]{3,2,1,0:T(8,128)(2,1)S(1)}, u32[]{:S(2)}, u32[]{:S(2)}) collective-permute-start(bf16[1,2,512,128]{3,2,1,0:T(8,128)(2,1)S(1)} %fusion.3), channel_id=1, source_target_pairs={{4,0},{5,1},{6,2},{7,3},{8,4},{9,5},{10,6},{11,7},{12,8},{13,9},{1... | collective-permute-start | bytes 786440 | tf_op jit(solution)/shard_map/ppermute | solution.py:508
  58.9 2.7 %own_2.1 = (bf16[256,512]{1,0:T(8,128)(2,1)S(1)}, bf16[256,512]{1,0:T(8,128)(2,1)S(1)}, f32[2,512,128]{2,1,0:T(8,128)S(1)}, f32[2,512,128]{2,1,0:T(8,128)S(1)}) custom-call(s32[2]{0:T(128)S(1)} %pad_add_fusion.meta, f32[1,128]{1,0:T(1,128)S(1)} %bitcast.37, bf16[2,4,128,256]{3,2,1,0:T(8,128)(2,1)S(1)} %get-tuple-element.116.qt, ...), custom_call_target="tpu_custom_call" | custom-call | flops 4294967296 | bytes 4194304 | tf_op jit(solution)/shard_map/own_2/pallas_call | solution.py:307
  61.6 3.9 %collective-permute-start.17 = (bf16[256,512]{1,0:T(8,128)(2,1)S(1)}, bf16[256,512]{1,0:T(8,128)(2,1)S(1)}, u32[]{:S(2)}, u32[]{:S(2)}) collective-permute-start(bf16[256,512]{1,0:T(8,128)(2,1)S(1)} %get-tuple-element.140), channel_id=1, source_target_pairs={{0,1},{1,0},{2,3},{3,2},{4,5},{5,4},{6,7},{7,6},{8,9},{9,8},{10,11... | collective-permute-start | bytes 786440 | tf_op jit(solution)/shard_map/ppermute | solution.py:554
  65.6 2.1 %collective-permute-start.18 = (bf16[1,2,512,128]{3,2,1,0:T(8,128)(2,1)S(1)}, bf16[1,2,512,128]{3,2,1,0:T(8,128)(2,1)S(1)}, u32[]{:S(2)}, u32[]{:S(2)}) collective-permute-start(bf16[1,2,512,128]{3,2,1,0:T(8,128)(2,1)S(1)} %fusion.4), channel_id=1, source_target_pairs={{4,0},{5,1},{6,2},{7,3},{8,4},{9,5},{10,6},{11,7},{12,8},{13,9},{1... | collective-permute-start | bytes 786440 | tf_op jit(solution)/shard_map/ppermute | solution.py:508
  67.8 1.8 %collective-permute-done.15.refs_2_ = bf16[1,2,512,128]{3,2,1,0:T(8,128)(2,1)S(1)} collective-permute-done((bf16[1,2,512,128]{3,2,1,0:T(8,128)(2,1)S(1)}, bf16[1,2,512,128]{3,2,1,0:T(8,128)(2,1)S(1)}, u32[]{:S(2)}, u32[]{:S(2)}) %collective-permute-start.15) | collective-permute-done | bytes 262176 | tf_op jit(solution)/shard_map/ppermute | solution.py:508
  69.6 2.8 %own_0.1 = (bf16[256,512]{1,0:T(8,128)(2,1)S(1)}, bf16[256,512]{1,0:T(8,128)(2,1)S(1)}, bf16[512,256]{1,0:T(8,128)(2,1)S(1)}, bf16[512,256]{1,0:T(8,128)(2,1)S(1)}) custom-call(s32[2]{0:T(128)S(1)} %pad_add_fusion.meta, f32[1,128]{1,0:T(1,128)S(1)} %bitcast.38, bf16[2,4,128,256]{3,2,1,0:T(8,128)(2,1)S(1)} %get-tuple-element.129.qt, ...), custom_call_target="tpu_custom_call" | custom-call | flops 4294967296 | bytes 4194304 | tf_op jit(solution)/shard_map/own_0/pallas_call | solution.py:307
  72.4 5.7 %collective-permute-start.16 = (bf16[256,512]{1,0:T(8,128)(2,1)S(1)}, bf16[256,512]{1,0:T(8,128)(2,1)S(1)}, u32[]{:S(2)}, u32[]{:S(2)}) collective-permute-start(bf16[256,512]{1,0:T(8,128)(2,1)S(1)} %get-tuple-element.139), channel_id=1, source_target_pairs={{0,1},{1,0},{2,3},{3,2},{4,5},{5,4},{6,7},{7,6},{8,9},{9,8},{10,11... | collective-permute-start | bytes 786440 | tf_op jit(solution)/shard_map/ppermute | solution.py:554
  81.1 1.7 %join_key.1 = (bf16[256,1024]{1,0:T(8,128)(2,1)}, bf16[256,1024]{1,0:T(8,128)(2,1)}) custom-call(f32[1,128]{1,0:T(1,128)S(1)} %bitcast.34, bf16[256,1024]{1,0:T(8,128)(2,1)S(1)} %copy-done, bf16[512,256]{1,0:T(8,128)(2,1)S(1)} %get-tuple-element.141.refs_0_, bf16[512,256]{1,0:T(8,128)(2,1)S(1)} %get-tuple-element.144.refs_1_, ...), custom_call_target="tpu_custom_call" | custom-call | flops 1048576 | bytes 65536 | tf_op jit(solution)/shard_map/join_key/pallas_call | solution.py:406
  (59 shorter events, 14.1 us)
Async XLA Ops:
  3.7 3.6 %collective-permute-start = (bf16[528,512]{1,0:T(8,128)(2,1)}, bf16[528,512]{1,0:T(8,128)(2,1)S(1)}, u32[]{:S(2)}, u32[]{:S(2)}) collective-permute-start(bf16[528,512]{1,0:T(8,128)(2,1)} %get-tuple-element.157), channel_id=1, source_target_pairs={{0,1},{1,0},{2,3},{3,2},{4,5},{5,4},{6,7},{7,6},{8,9},{9,8},{10,11... | collective-permute-start | bytes 1622024 | tf_op jit(solution)/shard_map/ppermute | solution.py:474
  6.6 16.3 %collective-permute-start.3 = (bf16[2,256,1024]{2,1,0:T(8,128)(2,1)}, bf16[2,256,1024]{2,1,0:T(8,128)(2,1)S(1)}, u32[]{:S(2)}, u32[]{:S(2)}) collective-permute-start(bf16[2,256,1024]{2,1,0:T(8,128)(2,1)} %pad_maximum_fusion.1), channel_id=1, source_target_pairs={{0,1},{1,0},{2,3},{3,2},{4,5},{5,4},{6,7},{7,6},{8,9},{9,8},{10,11... | collective-permute-start | bytes 3145736 | tf_op jit(solution)/shard_map/ppermute | solution.py:483
  7.4 10.0 %collective-permute-start.1 = (bf16[1,2,528,128]{3,2,1,0:T(8,128)(2,1)S(1)}, bf16[1,2,528,128]{3,2,1,0:T(8,128)(2,1)S(1)}, u32[]{:S(2)}, u32[]{:S(2)}) collective-permute-start(bf16[1,2,528,128]{3,2,1,0:T(8,128)(2,1)S(1)} %get-tuple-element.76), channel_id=1, source_target_pairs={{0,4},{1,5},{2,6},{3,7},{4,8},{5,9},{6,10},{7,11},{8,12},{9,13},{1... | collective-permute-start | bytes 811016 | tf_op jit(solution)/shard_map/ppermute | solution.py:480
  10.6 12.3 %copy-start.1 = (f32[128]{0:T(128)S(1)}, f32[128]{0:T(128)}, u32[]{:S(2)}) copy-start(f32[128]{0:T(128)} %param.12) | copy-start | bytes 1540
  10.6 12.3 %copy-start.2 = (f32[128]{0:T(128)S(1)}, f32[128]{0:T(128)}, u32[]{:S(2)}) copy-start(f32[128]{0:T(128)} %param.11) | copy-start | bytes 1540
  11.9 10.9 %collective-permute-start.2 = (bf16[1,2,528,128]{3,2,1,0:T(8,128)(2,1)S(1)}, bf16[1,2,528,128]{3,2,1,0:T(8,128)(2,1)S(1)}, u32[]{:S(2)}, u32[]{:S(2)}) collective-permute-start(bf16[1,2,528,128]{3,2,1,0:T(8,128)(2,1)S(1)} %get-tuple-element.77), channel_id=1, source_target_pairs={{0,2},{1,3},{2,0},{3,1},{4,6},{5,7},{6,4},{7,5},{8,10},{9,11},{10,... | collective-permute-start | bytes 811016 | tf_op jit(solution)/shard_map/ppermute | solution.py:481
  13.2 13.1 %collective-permute-start.4 = (bf16[1,2,528,128]{3,2,1,0:T(8,128)(2,1)S(1)}, bf16[1,2,528,128]{3,2,1,0:T(8,128)(2,1)S(1)}, u32[]{:S(2)}, u32[]{:S(2)}) collective-permute-start(bf16[1,2,528,128]{3,2,1,0:T(8,128)(2,1)S(1)} %get-tuple-element.81), channel_id=1, source_target_pairs={{0,4},{1,5},{2,6},{3,7},{4,8},{5,9},{6,10},{7,11},{8,12},{9,13},{1... | collective-permute-start | bytes 811016 | tf_op jit(solution)/shard_map/ppermute | solution.py:480
  17.5 9.2 %collective-permute-start.5 = (bf16[2,528,128]{2,1,0:T(8,128)(2,1)S(1)}, bf16[2,528,128]{2,1,0:T(8,128)(2,1)S(1)}, u32[]{:S(2)}, u32[]{:S(2)}) collective-permute-start(bf16[2,528,128]{2,1,0:T(8,128)(2,1)S(1)} %select_bitcast_fusion.2), channel_id=1, source_target_pairs={{0,2},{1,3},{2,0},{3,1},{4,6},{5,7},{6,4},{7,5},{8,10},{9,11},{10,... | collective-permute-start | bytes 811016 | tf_op jit(solution)/shard_map/ppermute | solution.py:491
  18.8 12.0 %collective-permute-start.6 = (bf16[1,2,528,128]{3,2,1,0:T(8,128)(2,1)S(1)}, bf16[1,2,528,128]{3,2,1,0:T(8,128)(2,1)S(1)}, u32[]{:S(2)}, u32[]{:S(2)}) collective-permute-start(bf16[1,2,528,128]{3,2,1,0:T(8,128)(2,1)S(1)} %get-tuple-element.91), channel_id=1, source_target_pairs={{0,4},{1,5},{2,6},{3,7},{4,8},{5,9},{6,10},{7,11},{8,12},{9,13},{1... | collective-permute-start | bytes 811016 | tf_op jit(solution)/shard_map/ppermute | solution.py:513
  26.3 6.3 %collective-permute-start.7 = (bf16[2,528,128]{2,1,0:T(8,128)(2,1)S(1)}, bf16[2,528,128]{2,1,0:T(8,128)(2,1)S(1)}, u32[]{:S(2)}, u32[]{:S(2)}) collective-permute-start(bf16[2,528,128]{2,1,0:T(8,128)(2,1)S(1)} %select_bitcast_fusion.1), channel_id=1, source_target_pairs={{0,2},{1,3},{2,0},{3,1},{4,6},{5,7},{6,4},{7,5},{8,10},{9,11},{10,... | collective-permute-start | bytes 811016 | tf_op jit(solution)/shard_map/ppermute | solution.py:491
  30.8 12.8 %collective-permute-start.8 = (bf16[2,528,128]{2,1,0:T(8,128)(2,1)S(1)}, bf16[2,528,128]{2,1,0:T(8,128)(2,1)S(1)}, u32[]{:S(2)}, u32[]{:S(2)}) collective-permute-start(bf16[2,528,128]{2,1,0:T(8,128)(2,1)S(1)} %select_bitcast_fusion), channel_id=1, source_target_pairs={{0,2},{1,3},{2,0},{3,1},{4,6},{5,7},{6,4},{7,5},{8,10},{9,11},{10,... | collective-permute-start | bytes 811016 | tf_op jit(solution)/shard_map/ppermute | solution.py:491
  32.0 16.1 %collective-permute-start.9 = (bf16[2,512,128]{2,1,0:T(8,128)(2,1)S(1)}, bf16[2,512,128]{2,1,0:T(8,128)(2,1)S(1)}, u32[]{:S(2)}, u32[]{:S(2)}) collective-permute-start(bf16[2,512,128]{2,1,0:T(8,128)(2,1)S(1)} %get-tuple-element.105), channel_id=1, source_target_pairs={{0,2},{1,3},{2,0},{3,1},{4,6},{5,7},{6,4},{7,5},{8,10},{9,11},{10,... | collective-permute-start | bytes 786440 | tf_op jit(solution)/shard_map/ppermute | solution.py:531
  36.7 13.9 %collective-permute-start.10 = (bf16[2,512,128]{2,1,0:T(8,128)(2,1)S(1)}, bf16[2,512,128]{2,1,0:T(8,128)(2,1)S(1)}, u32[]{:S(2)}, u32[]{:S(2)}) collective-permute-start(bf16[2,512,128]{2,1,0:T(8,128)(2,1)S(1)} %get-tuple-element.107), channel_id=1, source_target_pairs={{0,2},{1,3},{2,0},{3,1},{4,6},{5,7},{6,4},{7,5},{8,10},{9,11},{10,... | collective-permute-start | bytes 786440 | tf_op jit(solution)/shard_map/ppermute | solution.py:531
  37.7 15.0 %collective-permute-start.11 = (bf16[2,2,528,128]{3,2,1,0:T(8,128)(2,1)S(1)}, bf16[2,2,528,128]{3,2,1,0:T(8,128)(2,1)S(1)}, u32[]{:S(2)}, u32[]{:S(2)}) collective-permute-start(bf16[2,2,528,128]{3,2,1,0:T(8,128)(2,1)S(1)} %constant_dynamic-update-slice_fusion), channel_id=1, source_target_pairs={{0,4},{1,5},{2,6},{3,7},{4,8},{5,9},{6,10},{7,11},{8,12},{9,13},{1... | collective-permute-start | bytes 1622024 | tf_op jit(solution)/shard_map/ppermute | solution.py:497
  47.6 9.3 %collective-permute-start.12 = (bf16[2,512,128]{2,1,0:T(8,128)(2,1)S(1)}, bf16[2,512,128]{2,1,0:T(8,128)(2,1)S(1)}, u32[]{:S(2)}, u32[]{:S(2)}) collective-permute-start(bf16[2,512,128]{2,1,0:T(8,128)(2,1)S(1)} %get-tuple-element.113), channel_id=1, source_target_pairs={{0,2},{1,3},{2,0},{3,1},{4,6},{5,7},{6,4},{7,5},{8,10},{9,11},{10,... | collective-permute-start | bytes 786440 | tf_op jit(solution)/shard_map/ppermute | solution.py:531
  50.8 18.8 %collective-permute-start.14 = (bf16[2,2,512,128]{3,2,1,0:T(8,128)(2,1)S(1)}, bf16[2,2,512,128]{3,2,1,0:T(8,128)(2,1)S(1)}, u32[]{:S(2)}, u32[]{:S(2)}) collective-permute-start(bf16[2,2,512,128]{3,2,1,0:T(8,128)(2,1)S(1)} %pad_maximum_fusion.2), channel_id=1, source_target_pairs={{4,0},{5,1},{6,2},{7,3},{8,4},{9,5},{10,6},{11,7},{12,8},{13,9},{1... | collective-permute-start | bytes 1572872 | tf_op jit(solution)/shard_map/ppermute | solution.py:508
  56.8 8.7 %collective-permute-start.13 = (bf16[2,512,128]{2,1,0:T(8,128)(2,1)S(1)}, bf16[2,512,128]{2,1,0:T(8,128)(2,1)S(1)}, u32[]{:S(2)}, u32[]{:S(2)}) collective-permute-start(bf16[2,512,128]{2,1,0:T(8,128)(2,1)S(1)} %get-tuple-element.127), channel_id=1, source_target_pairs={{0,2},{1,3},{2,0},{3,1},{4,6},{5,7},{6,4},{7,5},{8,10},{9,11},{10,... | collective-permute-start | bytes 786440 | tf_op jit(solution)/shard_map/ppermute | solution.py:531
  57.0 12.6 %collective-permute-start.15 = (bf16[1,2,512,128]{3,2,1,0:T(8,128)(2,1)S(1)}, bf16[1,2,512,128]{3,2,1,0:T(8,128)(2,1)S(1)}, u32[]{:S(2)}, u32[]{:S(2)}) collective-permute-start(bf16[1,2,512,128]{3,2,1,0:T(8,128)(2,1)S(1)} %fusion.3), channel_id=1, source_target_pairs={{4,0},{5,1},{6,2},{7,3},{8,4},{9,5},{10,6},{11,7},{12,8},{13,9},{1... | collective-permute-start | bytes 786440 | tf_op jit(solution)/shard_map/ppermute | solution.py:508
  61.6 18.4 %collective-permute-start.17 = (bf16[256,512]{1,0:T(8,128)(2,1)S(1)}, bf16[256,512]{1,0:T(8,128)(2,1)S(1)}, u32[]{:S(2)}, u32[]{:S(2)}) collective-permute-start(bf16[256,512]{1,0:T(8,128)(2,1)S(1)} %get-tuple-element.140), channel_id=1, source_target_pairs={{0,1},{1,0},{2,3},{3,2},{4,5},{5,4},{6,7},{7,6},{8,9},{9,8},{10,11... | collective-permute-start | bytes 786440 | tf_op jit(solution)/shard_map/ppermute | solution.py:554
  65.6 12.5 %collective-permute-start.18 = (bf16[1,2,512,128]{3,2,1,0:T(8,128)(2,1)S(1)}, bf16[1,2,512,128]{3,2,1,0:T(8,128)(2,1)S(1)}, u32[]{:S(2)}, u32[]{:S(2)}) collective-permute-start(bf16[1,2,512,128]{3,2,1,0:T(8,128)(2,1)S(1)} %fusion.4), channel_id=1, source_target_pairs={{4,0},{5,1},{6,2},{7,3},{8,4},{9,5},{10,6},{11,7},{12,8},{13,9},{1... | collective-permute-start | bytes 786440 | tf_op jit(solution)/shard_map/ppermute | solution.py:508
  72.4 7.6 %collective-permute-start.16 = (bf16[256,512]{1,0:T(8,128)(2,1)S(1)}, bf16[256,512]{1,0:T(8,128)(2,1)S(1)}, u32[]{:S(2)}, u32[]{:S(2)}) collective-permute-start(bf16[256,512]{1,0:T(8,128)(2,1)S(1)} %get-tuple-element.139), channel_id=1, source_target_pairs={{0,1},{1,0},{2,3},{3,2},{4,5},{5,4},{6,7},{7,6},{8,9},{9,8},{10,11... | collective-permute-start | bytes 786440 | tf_op jit(solution)/shard_map/ppermute | solution.py:554
  78.1 2.9 %collective-permute-start.19 = (bf16[512,256]{1,0:T(8,128)(2,1)S(1)}, bf16[512,256]{1,0:T(8,128)(2,1)S(1)}, u32[]{:S(2)}, u32[]{:S(2)}) collective-permute-start(bf16[512,256]{1,0:T(8,128)(2,1)S(1)} %get-tuple-element.145), channel_id=1, source_target_pairs={{0,1},{1,0},{2,3},{3,2},{4,5},{5,4},{6,7},{7,6},{8,9},{9,8},{10,11... | collective-permute-start | bytes 786440 | tf_op jit(solution)/shard_map/ppermute | solution.py:554
  78.9 2.2 %copy-start = (bf16[256,1024]{1,0:T(8,128)(2,1)S(1)}, bf16[256,1024]{1,0:T(8,128)(2,1)}, u32[]{:S(2)}) copy-start(bf16[256,1024]{1,0:T(8,128)(2,1)} %keys.1) | copy-start | bytes 1572868
  78.9 2.2 %collective-permute-start.20 = (bf16[512,256]{1,0:T(8,128)(2,1)S(1)}, bf16[512,256]{1,0:T(8,128)(2,1)S(1)}, u32[]{:S(2)}, u32[]{:S(2)}) collective-permute-start(bf16[512,256]{1,0:T(8,128)(2,1)S(1)} %get-tuple-element.146), channel_id=1, source_target_pairs={{0,1},{1,0},{2,3},{3,2},{4,5},{5,4},{6,7},{7,6},{8,9},{9,8},{10,11... | collective-permute-start | bytes 786440 | tf_op jit(solution)/shard_map/ppermute | solution.py:554
  (2 other events, 3.5 us)

commit v5 on v3

--- a/solution.py
+++ b/solution.py
@@ -382,21 +382,35 @@
 def join_key_kernel(count, rows, k_gain, keys, *refs):
     f32 = jnp.float32
     core = lax.rem(lax.axis_index("ctx"), 2)
-    key_out, value_out = refs[2 * count :]
+    key_out, value_out, grads, sem = refs[2 * count :]
     half = key_out.shape[1] // 2
+    places, copies = [], []
     for parts, who in ((refs[:count], core), (refs[count : 2 * count], 1 - core)):
         at = 0
         for part in parts:
+            columns = pl.ds(pl.multiple_of(who * half + at, HD), part.shape[1])
+            copies.append(
+                pltpu.make_async_copy(
+                    part.at[pl.ds(rows, rows)], value_out.at[:, columns], sem.at[len(copies)]
+                )
+            )
+            copies[-1].start()
             for head in range(part.shape[1] // HD):
-                columns = pl.ds(pl.multiple_of(who * half + at, HD), HD)
-                inside = slice(head * HD, (head + 1) * HD)
-                k = keys[:, columns].astype(f32)
-                r = inverse_rms(k, -1)
-                scaled = part[:rows, inside].astype(f32) * k_gain[...]
-                grad = r * scaled - k * (r * r * r * jnp.mean(k * scaled, axis=-1, keepdims=True))
-                key_out[:, columns] = grad.astype(key_out.dtype)
-                value_out[:, columns] = part[rows:, inside]
+                places.append((part, head, who * half + at))
                 at += HD
+    for index, (part, head, begin) in enumerate(places):
+        columns = pl.ds(pl.multiple_of(begin, HD), HD)
+        k = keys[:, columns].astype(f32)
+        r = inverse_rms(k, -1)
+        scaled = part[:rows, head * HD : (head + 1) * HD].astype(f32) * k_gain[...]
+        grad = r * scaled - k * (r * r * r * jnp.mean(k * scaled, axis=-1, keepdims=True))
+        grads[index] = grad.astype(grads.dtype)
+        copies.append(
+            pltpu.make_async_copy(grads.at[index], key_out.at[:, columns], sem.at[len(copies)])
+        )
+        copies[-1].start()
+    for copy in copies:
+        copy.wait()
 
 
 def join_key(k_gain, keys, mine, theirs):
@@ -406,8 +420,12 @@
     return pl.pallas_call(
         functools.partial(join_key_kernel, len(mine), rows),
         in_specs=[vmem] * (2 + 2 * len(mine)),
-        out_specs=[vmem, vmem],
+        out_specs=[pl.BlockSpec(memory_space=pltpu.HBM)] * 2,
         out_shape=[out, out],
+        scratch_shapes=[
+            pltpu.VMEM((width // HD, rows, HD), keys.dtype),
+            pltpu.SemaphoreType.DMA((width // HD + 2 * len(mine),)),
+        ],
         compiler_params=pltpu.CompilerParams(vmem_limit_bytes=VMEM_LIMIT),
         cost_estimate=SMALL,
         name="join_key",

time: 82.6 us -> 82.5 us (level)
  no operation moved by 1% of the time
where the time goes in v5:
time: 82.5 us; the launch traced here: 81.2 us
  starting transfers between devices  38.3 us (46%)
  Pallas kernels  31.7 us (38%)
  other arithmetic  4.71 us (6%)
  waiting for transfers between devices  2.66 us (3%)
  local copies, waits for them, and re-layouts  2.53 us (3%)
  between operations  1.18 us (1%)
    pallas_call x4, Pallas kernels, halo(): pl.pallas_call(functools.partial(halo_kernel, piece, at, rows), in_specs=...  16.1 us
    ppermute x4, starting transfers between devices, on_device(): swap = lambda array: lax.ppermute(array, 'ctx', core_swap)  11 us
    ppermute x3, starting transfers between devices, on_device(): kv2.append((lax.ppermute(block, 'ctx', ahead), 0))  9.43 us
    pallas_call x2, Pallas kernels, local(): pl.pallas_call(functools.partial(local_kernel, rows), grid_spec=pltpu.Pre...  6.76 us
    ppermute x3, starting transfers between devices, send_back(): moved = lax.ppermute(joined[-1], 'ctx', back)  5.98 us
    pallas_call x2, Pallas kernels, own_keys(): pl.pallas_call(functools.partial(own_kernel, tuple(range(len(pieces))), p...  5.53 us
    ppermute x4, starting transfers between devices, on_device(): swapped.append(lax.ppermute(h1, 'ctx', x_swap))  4.58 us
    ppermute x1, starting transfers between devices, far_hop(): moved = lax.ppermute(block, 'ctx', ahead)  2.84 us
  transfers between devices with their start and end apart: 21, of which 4 were waited for; matrix products, arithmetic and copies ran while one was open for 5% of the time, Pallas kernels for 37%

profile of v5, /device:TPU:5, one launch (start us, length us, event | category | flops | bytes accessed | tf_op | source)
XLA Modules:
  0.0 81.2 jit_solution(15322617329018485882)
XLA Ops:
  7.4 3.1 %collective-permute-start.1 = (bf16[1,2,528,128]{3,2,1,0:T(8,128)(2,1)S(1)}, bf16[1,2,528,128]{3,2,1,0:T(8,128)(2,1)S(1)}, u32[]{:S(2)}, u32[]{:S(2)}) collective-permute-start(bf16[1,2,528,128]{3,2,1,0:T(8,128)(2,1)S(1)} %get-tuple-element.75), channel_id=1, source_target_pairs={{0,4},{1,5},{2,6},{3,7},{4,8},{5,9},{6,10},{7,11},{8,12},{9,13},{1... | collective-permute-start | bytes 811016 | tf_op jit(solution)/shard_map/ppermute | solution.py:498
  10.6 1.3 %pad_maximum_fusion.qg_m = bf16[2,256,1024]{2,1,0:T(8,128)(2,1)S(1)} fusion(bf16[1,256,1024]{2,1,0:T(8,128)(2,1)} %get-tuple-element.150, bf16[1,256,1024]{2,1,0:T(8,128)(2,1)} %get-tuple-element.159), kind=kLoop, calls=%fused_computation | loop fusion | flops 524288 | bytes 2097152 | tf_op jit(solution)/shard_map/stack | solution.py:484
  11.9 1.3 %collective-permute-start.2 = (bf16[1,2,528,128]{3,2,1,0:T(8,128)(2,1)S(1)}, bf16[1,2,528,128]{3,2,1,0:T(8,128)(2,1)S(1)}, u32[]{:S(2)}, u32[]{:S(2)}) collective-permute-start(bf16[1,2,528,128]{3,2,1,0:T(8,128)(2,1)S(1)} %get-tuple-element.76), channel_id=1, source_target_pairs={{0,2},{1,3},{2,0},{3,1},{4,6},{5,7},{6,4},{7,5},{8,10},{9,11},{10,... | collective-permute-start | bytes 811016 | tf_op jit(solution)/shard_map/ppermute | solution.py:499
  13.2 3.1 %collective-permute-start.4 = (bf16[1,2,528,128]{3,2,1,0:T(8,128)(2,1)S(1)}, bf16[1,2,528,128]{3,2,1,0:T(8,128)(2,1)S(1)}, u32[]{:S(2)}, u32[]{:S(2)}) collective-permute-start(bf16[1,2,528,128]{3,2,1,0:T(8,128)(2,1)S(1)} %get-tuple-element.80), channel_id=1, source_target_pairs={{0,4},{1,5},{2,6},{3,7},{4,8},{5,9},{6,10},{7,11},{8,12},{9,13},{1... | collective-permute-start | bytes 811016 | tf_op jit(solution)/shard_map/ppermute | solution.py:498
  16.4 3.1 %collective-permute-start.6 = (bf16[1,2,528,128]{3,2,1,0:T(8,128)(2,1)S(1)}, bf16[1,2,528,128]{3,2,1,0:T(8,128)(2,1)S(1)}, u32[]{:S(2)}, u32[]{:S(2)}) collective-permute-start(bf16[1,2,528,128]{3,2,1,0:T(8,128)(2,1)S(1)} %get-tuple-element.89), channel_id=1, source_target_pairs={{0,4},{1,5},{2,6},{3,7},{4,8},{5,9},{6,10},{7,11},{8,12},{9,13},{1... | collective-permute-start | bytes 811016 | tf_op jit(solution)/shard_map/ppermute | solution.py:498
  20.0 3.4 %local_0.1 = (bf16[2,4,128,256]{3,2,1,0:T(8,128)(2,1)S(1)}, bf16[2,4,128,256]{3,2,1,0:T(8,128)(2,1)S(1)}, bf16[2,4,128,256]{3,2,1,0:T(8,128)(2,1)S(1)}, bf16[2,5...) custom-call(s32[2]{0:T(128)S(1)} %pad_add_fusion.meta, ...), custom_call_target="tpu_custom_call" | custom-call | flops 1048576 | bytes 65536 | tf_op jit(solution)/shard_map/local_0/pallas_call | solution.py:112
  23.4 1.3 %collective-permute-start.7 = (bf16[2,528,128]{2,1,0:T(8,128)(2,1)S(1)}, bf16[2,528,128]{2,1,0:T(8,128)(2,1)S(1)}, u32[]{:S(2)}, u32[]{:S(2)}) collective-permute-start(bf16[2,528,128]{2,1,0:T(8,128)(2,1)S(1)} %select_bitcast_fusion.1), channel_id=1, source_target_pairs={{0,2},{1,3},{2,0},{3,1},{4,6},{5,7},{6,4},{7,5},{8,10},{9,11},{10,... | collective-permute-start | bytes 811016 | tf_op jit(solution)/shard_map/ppermute | solution.py:509
  24.7 1.8 %collective-permute-done.5.kv1 = bf16[2,528,128]{2,1,0:T(8,128)(2,1)S(1)} collective-permute-done((bf16[2,528,128]{2,1,0:T(8,128)(2,1)S(1)}, bf16[2,528,128]{2,1,0:T(8,128)(2,1)S(1)}, u32[]{:S(2)}, u32[]{:S(2)}) %collective-permute-start.5) | collective-permute-done | bytes 270368 | tf_op jit(solution)/shard_map/ppermute | solution.py:509
  26.5 4.0 %halo_0.2 = (bf16[2,512,128]{2,1,0:T(8,128)(2,1)S(1)}, bf16[2,512,128]{2,1,0:T(8,128)(2,1)S(1)}, bf16[4,128,256]{2,1,0:T(8,128)(2,1)S(1)}, f32[4,1,256]{2,1,0:T(1,128)S(1)}, f32[4,128,256]{2,1,0:T(8,128)S(1)}) custom-call(s32[2]{0:T(128)S(1)} %pad_add_fusion.meta, bf16[2,4,128,256]{3,2,1,0:T(8,128)(2,1)S(1)} %get-tuple-element.82.qn, ...), custom_call_target="tpu_custom_call" | custom-call | flops 1048576 | bytes 65536 | tf_op jit(solution)/shard_map/halo_0/pallas_call | solution.py:208
  32.3 4.0 %halo_1.2 = (bf16[2,512,128]{2,1,0:T(8,128)(2,1)S(1)}, bf16[2,512,128]{2,1,0:T(8,128)(2,1)S(1)}, bf16[4,128,256]{2,1,0:T(8,128)(2,1)S(1)}, f32[4,1,256]{2,1,0:T(1,128)S(1)}, f32[4,128,256]{2,1,0:T(8,128)S(1)}) custom-call(s32[2]{0:T(128)S(1)} %pad_add_fusion.meta, bf16[2,4,128,256]{3,2,1,0:T(8,128)(2,1)S(1)} %get-tuple-element.82.qn, ...), custom_call_target="tpu_custom_call" | custom-call | flops 1048576 | bytes 65536 | tf_op jit(solution)/shard_map/halo_1/pallas_call | solution.py:208
  37.4 2.8 %collective-permute-start.11 = (bf16[2,2,528,128]{3,2,1,0:T(8,128)(2,1)S(1)}, bf16[2,2,528,128]{3,2,1,0:T(8,128)(2,1)S(1)}, u32[]{:S(2)}, u32[]{:S(2)}) collective-permute-start(bf16[2,2,528,128]{3,2,1,0:T(8,128)(2,1)S(1)} %constant_dynamic-update-slice_fusion), channel_id=1, source_target_pairs={{0,4},{1,5},{2,6},{3,7},{4,8},{5,9},{6,10},{7,11},{8,12},{9,13},{1... | collective-permute-start | bytes 1622024 | tf_op jit(solution)/shard_map/ppermute | solution.py:515
  40.2 3.4 %local_2.1 = (bf16[2,4,128,256]{3,2,1,0:T(8,128)(2,1)S(1)}, bf16[2,4,128,256]{3,2,1,0:T(8,128)(2,1)S(1)}, bf16[2,4,128,256]{3,2,1,0:T(8,128)(2,1)S(1)}, bf16[2,5...) custom-call(s32[2]{0:T(128)S(1)} %pad_add_fusion.meta, ...), custom_call_target="tpu_custom_call" | custom-call | flops 1048576 | bytes 65536 | tf_op jit(solution)/shard_map/local_2/pallas_call | solution.py:112
  43.6 4.0 %halo_0.3 = (bf16[2,512,128]{2,1,0:T(8,128)(2,1)S(1)}, bf16[2,512,128]{2,1,0:T(8,128)(2,1)S(1)}, bf16[4,128,256]{2,1,0:T(8,128)(2,1)S(1)}, f32[4,1,256]{2,1,0:T(1,128)S(1)}, f32[4,128,256]{2,1,0:T(8,128)S(1)}) custom-call(s32[2]{0:T(128)S(1)} %pad_add_fusion.meta, bf16[2,4,128,256]{3,2,1,0:T(8,128)(2,1)S(1)} %get-tuple-element.94.qn, ...), custom_call_target="tpu_custom_call" | custom-call | flops 1048576 | bytes 65536 | tf_op jit(solution)/shard_map/halo_0/pallas_call | solution.py:208
  47.7 1.3 %collective-permute-start.12 = (bf16[2,512,128]{2,1,0:T(8,128)(2,1)S(1)}, bf16[2,512,128]{2,1,0:T(8,128)(2,1)S(1)}, u32[]{:S(2)}, u32[]{:S(2)}) collective-permute-start(bf16[2,512,128]{2,1,0:T(8,128)(2,1)S(1)} %get-tuple-element.111), channel_id=1, source_target_pairs={{0,2},{1,3},{2,0},{3,1},{4,6},{5,7},{6,4},{7,5},{8,10},{9,11},{10,... | collective-permute-start | bytes 786440 | tf_op jit(solution)/shard_map/ppermute | solution.py:547
  49.2 1.9 %collective-permute-start.14 = (bf16[2,2,512,128]{3,2,1,0:T(8,128)(2,1)S(1)}, bf16[2,2,512,128]{3,2,1,0:T(8,128)(2,1)S(1)}, u32[]{:S(2)}, u32[]{:S(2)}) collective-permute-start(bf16[2,2,512,128]{3,2,1,0:T(8,128)(2,1)S(1)} %pad_maximum_fusion.2), channel_id=1, source_target_pairs={{4,0},{5,1},{6,2},{7,3},{8,4},{9,5},{10,6},{11,7},{12,8},{13,9},{1... | collective-permute-start | bytes 1572872 | tf_op jit(solution)/shard_map/ppermute | solution.py:526
  51.2 4.0 %halo_1.3 = (bf16[2,512,128]{2,1,0:T(8,128)(2,1)S(1)}, bf16[2,512,128]{2,1,0:T(8,128)(2,1)S(1)}, bf16[4,128,256]{2,1,0:T(8,128)(2,1)S(1)}, f32[4,1,256]{2,1,0:T(1,128)S(1)}, f32[4,128,256]{2,1,0:T(8,128)S(1)}) custom-call(s32[2]{0:T(128)S(1)} %pad_add_fusion.meta, bf16[2,4,128,256]{3,2,1,0:T(8,128)(2,1)S(1)} %get-tuple-element.94.qn, ...), custom_call_target="tpu_custom_call" | custom-call | flops 1048576 | bytes 65536 | tf_op jit(solution)/shard_map/halo_1/pallas_call | solution.py:208
  56.3 1.9 %collective-permute-start.15 = (bf16[1,2,512,128]{3,2,1,0:T(8,128)(2,1)S(1)}, bf16[1,2,512,128]{3,2,1,0:T(8,128)(2,1)S(1)}, u32[]{:S(2)}, u32[]{:S(2)}) collective-permute-start(bf16[1,2,512,128]{3,2,1,0:T(8,128)(2,1)S(1)} %fusion.3), channel_id=1, source_target_pairs={{4,0},{5,1},{6,2},{7,3},{8,4},{9,5},{10,6},{11,7},{12,8},{13,9},{1... | collective-permute-start | bytes 786440 | tf_op jit(solution)/shard_map/ppermute | solution.py:526
  58.3 2.7 %own_2.1 = (bf16[256,512]{1,0:T(8,128)(2,1)S(1)}, bf16[256,512]{1,0:T(8,128)(2,1)S(1)}, f32[2,512,128]{2,1,0:T(8,128)S(1)}, f32[2,512,128]{2,1,0:T(8,128)S(1)}) custom-call(s32[2]{0:T(128)S(1)} %pad_add_fusion.meta, f32[1,128]{1,0:T(1,128)S(1)} %bitcast.37, bf16[2,4,128,256]{3,2,1,0:T(8,128)(2,1)S(1)} %get-tuple-element.114.qt, ...), custom_call_target="tpu_custom_call" | custom-call | flops 4294967296 | bytes 4194304 | tf_op jit(solution)/shard_map/own_2/pallas_call | solution.py:307
  61.0 4.4 %collective-permute-start.17 = (bf16[256,512]{1,0:T(8,128)(2,1)S(1)}, bf16[256,512]{1,0:T(8,128)(2,1)S(1)}, u32[]{:S(2)}, u32[]{:S(2)}) collective-permute-start(bf16[256,512]{1,0:T(8,128)(2,1)S(1)} %get-tuple-element.138), channel_id=1, source_target_pairs={{0,1},{1,0},{2,3},{3,2},{4,5},{5,4},{6,7},{7,6},{8,9},{9,8},{10,11... | collective-permute-start | bytes 786440 | tf_op jit(solution)/shard_map/ppermute | solution.py:570
  65.5 2.1 %collective-permute-start.18 = (bf16[1,2,512,128]{3,2,1,0:T(8,128)(2,1)S(1)}, bf16[1,2,512,128]{3,2,1,0:T(8,128)(2,1)S(1)}, u32[]{:S(2)}, u32[]{:S(2)}) collective-permute-start(bf16[1,2,512,128]{3,2,1,0:T(8,128)(2,1)S(1)} %fusion.4), channel_id=1, source_target_pairs={{4,0},{5,1},{6,2},{7,3},{8,4},{9,5},{10,6},{11,7},{12,8},{13,9},{1... | collective-permute-start | bytes 786440 | tf_op jit(solution)/shard_map/ppermute | solution.py:526
  67.7 2.8 %own_0.1 = (bf16[256,512]{1,0:T(8,128)(2,1)S(1)}, bf16[256,512]{1,0:T(8,128)(2,1)S(1)}, bf16[512,256]{1,0:T(8,128)(2,1)S(1)}, bf16[512,256]{1,0:T(8,128)(2,1)S(1)}) custom-call(s32[2]{0:T(128)S(1)} %pad_add_fusion.meta, f32[1,128]{1,0:T(1,128)S(1)} %bitcast.38, bf16[2,4,128,256]{3,2,1,0:T(8,128)(2,1)S(1)} %get-tuple-element.127.qt, ...), custom_call_target="tpu_custom_call" | custom-call | flops 4294967296 | bytes 4194304 | tf_op jit(solution)/shard_map/own_0/pallas_call | solution.py:307
  70.5 4.5 %collective-permute-start.16 = (bf16[256,512]{1,0:T(8,128)(2,1)S(1)}, bf16[256,512]{1,0:T(8,128)(2,1)S(1)}, u32[]{:S(2)}, u32[]{:S(2)}) collective-permute-start(bf16[256,512]{1,0:T(8,128)(2,1)S(1)} %get-tuple-element.137), channel_id=1, source_target_pairs={{0,1},{1,0},{2,3},{3,2},{4,5},{5,4},{6,7},{7,6},{8,9},{9,8},{10,11... | collective-permute-start | bytes 786440 | tf_op jit(solution)/shard_map/ppermute | solution.py:570
  76.5 1.9 %collective-permute-start.20 = (bf16[512,256]{1,0:T(8,128)(2,1)S(1)}, bf16[512,256]{1,0:T(8,128)(2,1)S(1)}, u32[]{:S(2)}, u32[]{:S(2)}) collective-permute-start(bf16[512,256]{1,0:T(8,128)(2,1)S(1)} %get-tuple-element.144), channel_id=1, source_target_pairs={{0,1},{1,0},{2,3},{3,2},{4,5},{5,4},{6,7},{7,6},{8,9},{9,8},{10,11... | collective-permute-start | bytes 786440 | tf_op jit(solution)/shard_map/ppermute | solution.py:570
  79.6 1.4 %join_key.1 = (bf16[256,1024]{1,0:T(8,128)(2,1)}, bf16[256,1024]{1,0:T(8,128)(2,1)}) custom-call(f32[1,128]{1,0:T(1,128)S(1)} %bitcast.34, bf16[256,1024]{1,0:T(8,128)(2,1)S(1)} %copy-done, bf16[512,256]{1,0:T(8,128)(2,1)S(1)} %get-tuple-element.139.refs_0_, bf16[512,256]{1,0:T(8,128)(2,1)S(1)} %get-tuple-element.142.refs_1_, ...), custom_call_target="tpu_custom_call" | custom-call | flops 1048576 | bytes 65536 | tf_op jit(solution)/shard_map/join_key/pallas_call | solution.py:420
  (59 shorter events, 14.1 us)
Async XLA Ops:
  3.7 3.6 %collective-permute-start = (bf16[528,512]{1,0:T(8,128)(2,1)}, bf16[528,512]{1,0:T(8,128)(2,1)S(1)}, u32[]{:S(2)}, u32[]{:S(2)}) collective-permute-start(bf16[528,512]{1,0:T(8,128)(2,1)} %get-tuple-element.155), channel_id=1, source_target_pairs={{0,1},{1,0},{2,3},{3,2},{4,5},{5,4},{6,7},{7,6},{8,9},{9,8},{10,11... | collective-permute-start | bytes 1622024 | tf_op jit(solution)/shard_map/ppermute | solution.py:492
  6.6 13.4 %collective-permute-start.3 = (bf16[2,256,1024]{2,1,0:T(8,128)(2,1)}, bf16[2,256,1024]{2,1,0:T(8,128)(2,1)S(1)}, u32[]{:S(2)}, u32[]{:S(2)}) collective-permute-start(bf16[2,256,1024]{2,1,0:T(8,128)(2,1)} %pad_maximum_fusion.1), channel_id=1, source_target_pairs={{0,1},{1,0},{2,3},{3,2},{4,5},{5,4},{6,7},{7,6},{8,9},{9,8},{10,11... | collective-permute-start | bytes 3145736 | tf_op jit(solution)/shard_map/ppermute | solution.py:501
  7.4 12.1 %collective-permute-start.1 = (bf16[1,2,528,128]{3,2,1,0:T(8,128)(2,1)S(1)}, bf16[1,2,528,128]{3,2,1,0:T(8,128)(2,1)S(1)}, u32[]{:S(2)}, u32[]{:S(2)}) collective-permute-start(bf16[1,2,528,128]{3,2,1,0:T(8,128)(2,1)S(1)} %get-tuple-element.75), channel_id=1, source_target_pairs={{0,4},{1,5},{2,6},{3,7},{4,8},{5,9},{6,10},{7,11},{8,12},{9,13},{1... | collective-permute-start | bytes 811016 | tf_op jit(solution)/shard_map/ppermute | solution.py:498
  10.6 9.4 %copy-start.1 = (f32[128]{0:T(128)S(1)}, f32[128]{0:T(128)}, u32[]{:S(2)}) copy-start(f32[128]{0:T(128)} %param.12) | copy-start | bytes 1540
  10.6 9.4 %copy-start.2 = (f32[128]{0:T(128)S(1)}, f32[128]{0:T(128)}, u32[]{:S(2)}) copy-start(f32[128]{0:T(128)} %param.11) | copy-start | bytes 1540
  11.9 8.0 %collective-permute-start.2 = (bf16[1,2,528,128]{3,2,1,0:T(8,128)(2,1)S(1)}, bf16[1,2,528,128]{3,2,1,0:T(8,128)(2,1)S(1)}, u32[]{:S(2)}, u32[]{:S(2)}) collective-permute-start(bf16[1,2,528,128]{3,2,1,0:T(8,128)(2,1)S(1)} %get-tuple-element.76), channel_id=1, source_target_pairs={{0,2},{1,3},{2,0},{3,1},{4,6},{5,7},{6,4},{7,5},{8,10},{9,11},{10,... | collective-permute-start | bytes 811016 | tf_op jit(solution)/shard_map/ppermute | solution.py:499
  13.2 10.2 %collective-permute-start.4 = (bf16[1,2,528,128]{3,2,1,0:T(8,128)(2,1)S(1)}, bf16[1,2,528,128]{3,2,1,0:T(8,128)(2,1)S(1)}, u32[]{:S(2)}, u32[]{:S(2)}) collective-permute-start(bf16[1,2,528,128]{3,2,1,0:T(8,128)(2,1)S(1)} %get-tuple-element.80), channel_id=1, source_target_pairs={{0,4},{1,5},{2,6},{3,7},{4,8},{5,9},{6,10},{7,11},{8,12},{9,13},{1... | collective-permute-start | bytes 811016 | tf_op jit(solution)/shard_map/ppermute | solution.py:498
  16.4 14.2 %collective-permute-start.6 = (bf16[1,2,528,128]{3,2,1,0:T(8,128)(2,1)S(1)}, bf16[1,2,528,128]{3,2,1,0:T(8,128)(2,1)S(1)}, u32[]{:S(2)}, u32[]{:S(2)}) collective-permute-start(bf16[1,2,528,128]{3,2,1,0:T(8,128)(2,1)S(1)} %get-tuple-element.89), channel_id=1, source_target_pairs={{0,4},{1,5},{2,6},{3,7},{4,8},{5,9},{6,10},{7,11},{8,12},{9,13},{1... | collective-permute-start | bytes 811016 | tf_op jit(solution)/shard_map/ppermute | solution.py:498
  19.6 6.9 %collective-permute-start.5 = (bf16[2,528,128]{2,1,0:T(8,128)(2,1)S(1)}, bf16[2,528,128]{2,1,0:T(8,128)(2,1)S(1)}, u32[]{:S(2)}, u32[]{:S(2)}) collective-permute-start(bf16[2,528,128]{2,1,0:T(8,128)(2,1)S(1)} %select_bitcast_fusion.2), channel_id=1, source_target_pairs={{0,2},{1,3},{2,0},{3,1},{4,6},{5,7},{6,4},{7,5},{8,10},{9,11},{10,... | collective-permute-start | bytes 811016 | tf_op jit(solution)/shard_map/ppermute | solution.py:509
  23.4 8.8 %collective-permute-start.7 = (bf16[2,528,128]{2,1,0:T(8,128)(2,1)S(1)}, bf16[2,528,128]{2,1,0:T(8,128)(2,1)S(1)}, u32[]{:S(2)}, u32[]{:S(2)}) collective-permute-start(bf16[2,528,128]{2,1,0:T(8,128)(2,1)S(1)} %select_bitcast_fusion.1), channel_id=1, source_target_pairs={{0,2},{1,3},{2,0},{3,1},{4,6},{5,7},{6,4},{7,5},{8,10},{9,11},{10,... | collective-permute-start | bytes 811016 | tf_op jit(solution)/shard_map/ppermute | solution.py:509
  30.6 13.0 %collective-permute-start.8 = (bf16[2,528,128]{2,1,0:T(8,128)(2,1)S(1)}, bf16[2,528,128]{2,1,0:T(8,128)(2,1)S(1)}, u32[]{:S(2)}, u32[]{:S(2)}) collective-permute-start(bf16[2,528,128]{2,1,0:T(8,128)(2,1)S(1)} %select_bitcast_fusion), channel_id=1, source_target_pairs={{0,2},{1,3},{2,0},{3,1},{4,6},{5,7},{6,4},{7,5},{8,10},{9,11},{10,... | collective-permute-start | bytes 811016 | tf_op jit(solution)/shard_map/ppermute | solution.py:509
  30.9 18.1 %collective-permute-start.9 = (bf16[2,512,128]{2,1,0:T(8,128)(2,1)S(1)}, bf16[2,512,128]{2,1,0:T(8,128)(2,1)S(1)}, u32[]{:S(2)}, u32[]{:S(2)}) collective-permute-start(bf16[2,512,128]{2,1,0:T(8,128)(2,1)S(1)} %get-tuple-element.103), channel_id=1, source_target_pairs={{0,2},{1,3},{2,0},{3,1},{4,6},{5,7},{6,4},{7,5},{8,10},{9,11},{10,... | collective-permute-start | bytes 786440 | tf_op jit(solution)/shard_map/ppermute | solution.py:547
  36.3 12.7 %collective-permute-start.10 = (bf16[2,512,128]{2,1,0:T(8,128)(2,1)S(1)}, bf16[2,512,128]{2,1,0:T(8,128)(2,1)S(1)}, u32[]{:S(2)}, u32[]{:S(2)}) collective-permute-start(bf16[2,512,128]{2,1,0:T(8,128)(2,1)S(1)} %get-tuple-element.105), channel_id=1, source_target_pairs={{0,2},{1,3},{2,0},{3,1},{4,6},{5,7},{6,4},{7,5},{8,10},{9,11},{10,... | collective-permute-start | bytes 786440 | tf_op jit(solution)/shard_map/ppermute | solution.py:547
  37.4 13.8 %collective-permute-start.11 = (bf16[2,2,528,128]{3,2,1,0:T(8,128)(2,1)S(1)}, bf16[2,2,528,128]{3,2,1,0:T(8,128)(2,1)S(1)}, u32[]{:S(2)}, u32[]{:S(2)}) collective-permute-start(bf16[2,2,528,128]{3,2,1,0:T(8,128)(2,1)S(1)} %constant_dynamic-update-slice_fusion), channel_id=1, source_target_pairs={{0,4},{1,5},{2,6},{3,7},{4,8},{5,9},{6,10},{7,11},{8,12},{9,13},{1... | collective-permute-start | bytes 1622024 | tf_op jit(solution)/shard_map/ppermute | solution.py:515
  47.7 8.6 %collective-permute-start.12 = (bf16[2,512,128]{2,1,0:T(8,128)(2,1)S(1)}, bf16[2,512,128]{2,1,0:T(8,128)(2,1)S(1)}, u32[]{:S(2)}, u32[]{:S(2)}) collective-permute-start(bf16[2,512,128]{2,1,0:T(8,128)(2,1)S(1)} %get-tuple-element.111), channel_id=1, source_target_pairs={{0,2},{1,3},{2,0},{3,1},{4,6},{5,7},{6,4},{7,5},{8,10},{9,11},{10,... | collective-permute-start | bytes 786440 | tf_op jit(solution)/shard_map/ppermute | solution.py:547
  49.2 18.5 %collective-permute-start.14 = (bf16[2,2,512,128]{3,2,1,0:T(8,128)(2,1)S(1)}, bf16[2,2,512,128]{3,2,1,0:T(8,128)(2,1)S(1)}, u32[]{:S(2)}, u32[]{:S(2)}) collective-permute-start(bf16[2,2,512,128]{3,2,1,0:T(8,128)(2,1)S(1)} %pad_maximum_fusion.2), channel_id=1, source_target_pairs={{4,0},{5,1},{6,2},{7,3},{8,4},{9,5},{10,6},{11,7},{12,8},{13,9},{1... | collective-permute-start | bytes 1572872 | tf_op jit(solution)/shard_map/ppermute | solution.py:526
  55.2 10.2 %collective-permute-start.13 = (bf16[2,512,128]{2,1,0:T(8,128)(2,1)S(1)}, bf16[2,512,128]{2,1,0:T(8,128)(2,1)S(1)}, u32[]{:S(2)}, u32[]{:S(2)}) collective-permute-start(bf16[2,512,128]{2,1,0:T(8,128)(2,1)S(1)} %get-tuple-element.125), channel_id=1, source_target_pairs={{0,2},{1,3},{2,0},{3,1},{4,6},{5,7},{6,4},{7,5},{8,10},{9,11},{10,... | collective-permute-start | bytes 786440 | tf_op jit(solution)/shard_map/ppermute | solution.py:547
  56.3 11.3 %collective-permute-start.15 = (bf16[1,2,512,128]{3,2,1,0:T(8,128)(2,1)S(1)}, bf16[1,2,512,128]{3,2,1,0:T(8,128)(2,1)S(1)}, u32[]{:S(2)}, u32[]{:S(2)}) collective-permute-start(bf16[1,2,512,128]{3,2,1,0:T(8,128)(2,1)S(1)} %fusion.3), channel_id=1, source_target_pairs={{4,0},{5,1},{6,2},{7,3},{8,4},{9,5},{10,6},{11,7},{12,8},{13,9},{1... | collective-permute-start | bytes 786440 | tf_op jit(solution)/shard_map/ppermute | solution.py:526
  61.0 17.4 %collective-permute-start.17 = (bf16[256,512]{1,0:T(8,128)(2,1)S(1)}, bf16[256,512]{1,0:T(8,128)(2,1)S(1)}, u32[]{:S(2)}, u32[]{:S(2)}) collective-permute-start(bf16[256,512]{1,0:T(8,128)(2,1)S(1)} %get-tuple-element.138), channel_id=1, source_target_pairs={{0,1},{1,0},{2,3},{3,2},{4,5},{5,4},{6,7},{7,6},{8,9},{9,8},{10,11... | collective-permute-start | bytes 786440 | tf_op jit(solution)/shard_map/ppermute | solution.py:570
  65.5 10.2 %collective-permute-start.18 = (bf16[1,2,512,128]{3,2,1,0:T(8,128)(2,1)S(1)}, bf16[1,2,512,128]{3,2,1,0:T(8,128)(2,1)S(1)}, u32[]{:S(2)}, u32[]{:S(2)}) collective-permute-start(bf16[1,2,512,128]{3,2,1,0:T(8,128)(2,1)S(1)} %fusion.4), channel_id=1, source_target_pairs={{4,0},{5,1},{6,2},{7,3},{8,4},{9,5},{10,6},{11,7},{12,8},{13,9},{1... | collective-permute-start | bytes 786440 | tf_op jit(solution)/shard_map/ppermute | solution.py:526
  70.5 7.9 %collective-permute-start.16 = (bf16[256,512]{1,0:T(8,128)(2,1)S(1)}, bf16[256,512]{1,0:T(8,128)(2,1)S(1)}, u32[]{:S(2)}, u32[]{:S(2)}) collective-permute-start(bf16[256,512]{1,0:T(8,128)(2,1)S(1)} %get-tuple-element.137), channel_id=1, source_target_pairs={{0,1},{1,0},{2,3},{3,2},{4,5},{5,4},{6,7},{7,6},{8,9},{9,8},{10,11... | collective-permute-start | bytes 786440 | tf_op jit(solution)/shard_map/ppermute | solution.py:570
  75.0 4.4 %collective-permute-start.19 = (bf16[512,256]{1,0:T(8,128)(2,1)S(1)}, bf16[512,256]{1,0:T(8,128)(2,1)S(1)}, u32[]{:S(2)}, u32[]{:S(2)}) collective-permute-start(bf16[512,256]{1,0:T(8,128)(2,1)S(1)} %get-tuple-element.143), channel_id=1, source_target_pairs={{0,1},{1,0},{2,3},{3,2},{4,5},{5,4},{6,7},{7,6},{8,9},{9,8},{10,11... | collective-permute-start | bytes 786440 | tf_op jit(solution)/shard_map/ppermute | solution.py:570
  76.5 3.1 %copy-start = (bf16[256,1024]{1,0:T(8,128)(2,1)S(1)}, bf16[256,1024]{1,0:T(8,128)(2,1)}, u32[]{:S(2)}) copy-start(bf16[256,1024]{1,0:T(8,128)(2,1)} %keys.1) | copy-start | bytes 1572868
  76.5 3.1 %collective-permute-start.20 = (bf16[512,256]{1,0:T(8,128)(2,1)S(1)}, bf16[512,256]{1,0:T(8,128)(2,1)S(1)}, u32[]{:S(2)}, u32[]{:S(2)}) collective-permute-start(bf16[512,256]{1,0:T(8,128)(2,1)S(1)} %get-tuple-element.144), channel_id=1, source_target_pairs={{0,1},{1,0},{2,3},{3,2},{4,5},{5,4},{6,7},{7,6},{8,9},{9,8},{10,11... | collective-permute-start | bytes 786440 | tf_op jit(solution)/shard_map/ppermute | solution.py:570
  (2 other events, 3.5 us)
